TPU v7x, 32 devices: a whole 2x2x4 slice. The times are simulated.
32 devices in a mesh: dp: 8 (over z, y), chan: 4 (over x, core).
Axes of the slice: x: 2, y: 2, z: 4, core: 2. Of those that a mesh axis runs over, the one named last changes fastest.
Arguments:
- features: bfloat16 [32, 660, 1024], P('dp', 'chan'), may hold values from -6 to 6
- gain1: float32 [660], P('chan'), may hold values from 0.1 to 1.9
- bias1: float32 [660], P('chan'), may hold values from -3 to 3
- weight1: bfloat16 [660, 132], P('chan'), may hold values from -0.25 to 0.25
- gain2: float32 [132], P('chan'), may hold values from 0.1 to 1.9
- bias2: float32 [132], P('chan'), may hold values from -3 to 3
- weight2: bfloat16 [3, 3, 132, 33], P(None, None, 'chan'), may hold values from -0.3125 to 0.3125
- cotangent: bfloat16 [32, 660, 1024], P('dp', 'chan'), may hold values from -6 to 6
- image_side: int32 [32], P('dp'), may hold values from 24 to 32, as said below
- block_slot: int32 [20], replicated, may hold values from 0 to 19, each once
Outputs:
- output: float32 [32, 660, 1024], P('dp', 'chan')
- grad_features: float32 [32, 660, 1024], P('dp', 'chan')
- grad_weight1: float32 [660, 132], P('chan')
- grad_gain1: float32 [660], P('chan')
- grad_bias1: float32 [660], P('chan')
- grad_weight2: float32 [3, 3, 132, 33], P(None, None, 'chan')
- grad_gain2: float32 [132], P('chan')
- grad_bias2: float32 [132], P('chan')
Inputs may be any that keep to these rules, and one draw needn't show every extreme that they name: `image_side`: each image's side is 24 or 32; both occur in every draw; its valid pixels are the top-left square of that side. A permutation: block k is stored in channel slot block_slot[k]; the last block is the new one.
All inputs are finite; a program needn't handle non-finite values.
Results may differ from a plain program's by a relative error of at most 0.00089.
Values may be sent and summed in bfloat16 or wider, within the bound.
A program may use at most 64 MiB of HBM per device.

v0:
```python
import jax
import jax.numpy as jnp
from jax import lax
from jax.sharding import PartitionSpec as P

SIDE = 32


EPS = 1e-05


def broadcast(block, axis, owner):
    block = jnp.where(lax.axis_index(axis) == owner, block, jnp.zeros_like(block))
    return lax.psum(block, axis)


def smooth(values):
    return values * jax.nn.sigmoid(values)


def smooth_slope(values):
    sigma = jax.nn.sigmoid(values)
    return sigma + values * sigma * (1.0 - sigma)


def totals(values):
    return jnp.sum(values, axis=(0, 2))


def column(values):
    return values[:, None]


def conv_three(inputs, kernel):
    images = inputs.shape[0]
    squares = inputs.reshape(images, inputs.shape[1], SIDE, SIDE)
    result = lax.conv_general_dilated(
        squares,
        kernel,
        (1, 1),
        "SAME",
        dimension_numbers=("NCHW", "HWIO", "NCHW"),
        preferred_element_type=jnp.float32,
    )
    return result.reshape(images, kernel.shape[3], SIDE * SIDE)


def kernel_grad(inputs, grad_out):
    images = inputs.shape[0]
    squares = inputs.reshape(images, inputs.shape[1], SIDE, SIDE)
    grad_squares = grad_out.reshape(images, grad_out.shape[1], SIDE, SIDE)
    padded = jnp.pad(squares, ((0, 0), (0, 0), (1, 1), (1, 1)))
    row_list = []
    for offset_y in range(3):
        col_list = []
        for offset_x in range(3):
            window_in = padded[:, :, offset_y : offset_y + SIDE, offset_x : offset_x + SIDE]
            col_list.append(
                jnp.einsum(
                    "bcij,bdij->cd", window_in, grad_squares, preferred_element_type=jnp.float32
                )
            )
        row_list.append(jnp.stack(col_list))
    return jnp.stack(row_list)


def on_device(
    features, gain1, bias1, weight1, gain2, bias2, weight2, cotangent, image_side, block_slot
):
    lane = lax.axis_index("chan")
    images = features.shape[0]
    local_width = features.shape[1]
    grow = weight2.shape[3]
    per_device = local_width // grow
    steps_along = jnp.arange(SIDE, dtype=jnp.int32)
    inside = steps_along[None, :] < image_side[:, None]
    pixel_mask = (
        (inside[:, :, None] & inside[:, None, :])
        .astype(jnp.float32)
        .reshape(images, 1, SIDE * SIDE)
    )
    new_slot = block_slot[block_slot.shape[0] - 1]
    owner = new_slot // per_device
    local_slot = new_slot % per_device
    channel_ids = lane * local_width + jnp.arange(local_width, dtype=jnp.int32)
    keep = column((channel_ids // grow != new_slot).astype(jnp.float32))
    inputs = features.astype(jnp.float32)
    weighted = inputs * pixel_mask
    sum_one, square_one, count = lax.psum(
        (totals(weighted), totals(weighted * inputs), jnp.sum(pixel_mask)), "dp"
    )
    mean_one = sum_one / count
    rstd_one = column(lax.rsqrt(square_one / count - mean_one * mean_one + EPS))
    norm_one = (inputs - column(mean_one)) * rstd_one
    pre_one = norm_one * column(gain1) + column(bias1)
    act_one = (smooth(pre_one) * pixel_mask * keep).astype(jnp.bfloat16)
    partial_value = jnp.einsum("bcp,cd->bdp", act_one, weight1, preferred_element_type=jnp.float32)
    hidden = lax.psum_scatter(partial_value, "chan", scatter_dimension=1, tiled=True)
    gain_two, bias_two, kernel = (gain2, bias2, weight2)
    weighted_two = hidden * pixel_mask
    sum_two, square_two = lax.psum((totals(weighted_two), totals(weighted_two * hidden)), "dp")
    mean_two = sum_two / count
    rstd_two = column(lax.rsqrt(square_two / count - mean_two * mean_two + EPS))
    norm_two = (hidden - column(mean_two)) * rstd_two
    pre_two = norm_two * column(gain_two) + column(bias_two)
    act_two = (smooth(pre_two) * pixel_mask).astype(jnp.bfloat16)
    grown = lax.psum(conv_three(act_two, kernel), "chan") * pixel_mask
    kept_inputs = inputs * keep
    placed = lax.dynamic_update_slice_in_dim(kept_inputs, grown, local_slot * grow, 1)
    output = jnp.where(lane == owner, placed, kept_inputs)
    own_grad = lax.dynamic_slice_in_dim(cotangent, local_slot * grow, grow, 1)
    growth_grad = broadcast(own_grad, "chan", owner)
    growth_grad = (growth_grad.astype(jnp.float32) * pixel_mask).astype(jnp.bfloat16)
    back_kernel = jnp.swapaxes(jnp.flip(kernel, (0, 1)), 2, 3)
    back_input = conv_three(growth_grad, back_kernel)
    grad_pre_two = back_input * pixel_mask * smooth_slope(pre_two)
    kernel_part = kernel_grad(act_two, growth_grad)
    kernel_sum, bias_sum_two, gain_sum_two = lax.psum(
        (kernel_part, totals(grad_pre_two), totals(grad_pre_two * norm_two)), "dp"
    )
    gain_col = column(gain_two)
    grad_hidden = rstd_two * (
        grad_pre_two * gain_col
        - pixel_mask * gain_col * (column(bias_sum_two) + norm_two * column(gain_sum_two)) / count
    )
    grad_hidden = grad_hidden.astype(jnp.bfloat16)
    full_grad = lax.all_gather(grad_hidden, "chan", axis=1, tiled=True)
    grad_act_one = jnp.einsum("bdp,cd->bcp", full_grad, weight1, preferred_element_type=jnp.float32)
    weight_part = jnp.einsum("bcp,bdp->cd", act_one, full_grad, preferred_element_type=jnp.float32)
    grad_pre_one = grad_act_one * pixel_mask * keep * smooth_slope(pre_one)
    weight_sum, bias_sum_one, gain_sum_one = lax.psum(
        (weight_part, totals(grad_pre_one), totals(grad_pre_one * norm_one)), "dp"
    )
    gain_one = column(gain1)
    grad_inputs = rstd_one * (
        grad_pre_one * gain_one
        - pixel_mask * gain_one * (column(bias_sum_one) + norm_one * column(gain_sum_one)) / count
    )
    grad_features = cotangent.astype(jnp.float32) * keep + grad_inputs
    return (
        output,
        grad_features,
        weight_sum,
        gain_sum_one,
        bias_sum_one,
        kernel_sum,
        gain_sum_two,
        bias_sum_two,
    )


def solution(mesh):
    in_specs = (
        P("dp", "chan", None),
        P("chan"),
        P("chan"),
        P("chan", None),
        P("chan"),
        P("chan"),
        P(None, None, "chan", None),
        P("dp", "chan", None),
        P("dp"),
        P(),
    )
    out_specs = (
        P("dp", "chan", None),
        P("dp", "chan", None),
        P("chan", None),
        P("chan"),
        P("chan"),
        P(None, None, "chan", None),
        P("chan"),
        P("chan"),
    )
    return jax.shard_map(
        on_device, mesh=mesh, in_specs=in_specs, out_specs=out_specs, check_vma=False
    )
```

profile of v0, /device:TPU:0, one launch (start us, length us, event | category | flops | bytes accessed | tf_op | source)
XLA Modules:
  0.0 333.9 jit_solution(12953952966662737701)
XLA Ops:
  8.8 1.2 slice.28
  10.8 2.1 fusion.20
  12.9 23.8 %all-reduce.5 = (f32[165]{0:T(256)S(1)}, f32[]{:T(128)}, f32[165]{0:T(256)S(1)}) all-reduce(f32[165]{0:T(256)S(1)} %get-tuple-element.35, f32[]{:T(128)} %fusion.42, f32[165]{0:T(256)S(1)} %get-tuple-element.34), channel_id=1, replica_groups=mesh['dp'=8,'chan'=4] {'dp'}, use_global_device_ids=true, to_apply=%region_1.2 | all-reduce | flops 331 | bytes 2648 | tf_op jit(solution)/shard_map/psum | solution.py:89
  37.3 2.8 multiply_convert_fusion
  40.1 1.1 copy-done.2
  41.8 2.7 copy.63
  47.0 0.8 dynamic-slice_select_fusion.1
  49.3 45.1 %all-reduce.17.cloned.1.call-done = f32[4,132,1024]{2,0,1:T(4,128)} async-done(((f32[4,132,1024]{2,0,1:T(4,128)}), f32[4,132,1024]{2,0,1:T(4,128)}) %all-reduce.17.cloned.1.call-update) | async-done | bytes 2162704
  94.4 1.1 constant_dynamic-slice_fusion
  95.5 33.8 %all-reduce.13.cloned.1.call-done = bf16[4,33,1024]{2,1,0:T(8,128)(2,1)} async-done(((bf16[4,33,1024]{2,1,0:T(8,128)(2,1)}), bf16[4,33,1024]{2,1,0:T(8,128)(2,1)}) %all-reduce.13.cloned.1.call-update) | async-done | bytes 270352 | tf_op jit(solution)/shard_map/psum | solution.py:14
  129.2 1.4 fusion.38
  131.4 2.2 copy.85
  133.6 2.3 copy.108
  136.9 2.6 fusion.32
  139.5 1.5 copy.78
  141.0 1.5 slice_bitcast_fusion
  142.5 3.5 %copy.104 = f32[4,33,32,32]{3,2,1,0:T(8,128)S(1)} copy(f32[4,33,32,32]{1,2,3,0:T(8,128)} %slice_bitcast_fusion) | data formatting | bytes 1081344 | tf_op jit(solution)/shard_map/reshape | solution.py:45
  146.0 1.9 reshape.147
  147.9 21.3 %all-reduce.4 = (f32[33]{0:T(128)S(1)}, f32[33]{0:T(128)S(1)}) all-reduce(f32[33]{0:T(128)S(1)} %get-tuple-element.39, f32[33]{0:T(128)S(1)} %get-tuple-element.38), channel_id=1, replica_groups=mesh['dp'=8,'chan'=4] {'dp'}, use_global_device_ids=true, to_apply=%region_8.9 | all-reduce | flops 66 | bytes 528 | tf_op jit(solution)/shard_map/psum | solution.py:101
  169.9 1.8 fusion.52
  171.8 17.1 %all-reduce.3 = (f32[33]{0:T(128)S(1)}, f32[33]{0:T(128)S(1)}) all-reduce(f32[33]{0:T(128)S(1)} %get-tuple-element.37, f32[33]{0:T(128)S(1)} %get-tuple-element.36), channel_id=1, replica_groups=mesh['dp'=8,'chan'=4] {'dp'}, use_global_device_ids=true, to_apply=%region_16.17 | all-reduce | flops 66 | bytes 528 | tf_op jit(solution)/shard_map/psum | solution.py:118
  188.9 1.1 multiply_convert_fusion.1
  190.0 1.0 copy.81
  191.8 2.4 copy.84
  194.2 2.3 copy.107
  197.2 2.7 fusion.29
  199.9 1.5 copy.70
  201.4 1.5 slice_bitcast_fusion.1
  202.9 3.5 %copy.103 = f32[4,33,32,32]{3,2,1,0:T(8,128)S(1)} copy(f32[4,33,32,32]{1,2,3,0:T(8,128)} %slice_bitcast_fusion.1) | data formatting | bytes 1081344 | tf_op jit(solution)/shard_map/reshape | solution.py:45
  206.4 1.9 reshape.146
  208.3 2.1 convolution_bitcast_fusion.9
  210.4 2.6 convolution_bitcast_fusion.8
  213.0 1.1 convolution_bitcast_fusion.7
  214.1 1.1 convolution_bitcast_fusion.5
  215.2 1.1 convolution_bitcast_fusion.4
  216.3 1.0 convolution_bitcast_fusion.3
  217.3 1.1 convolution_bitcast_fusion.2
  218.4 1.1 convolution_bitcast_fusion.10
  220.8 0.8 maximum_bitcast_fusion
  221.7 2.9 convolution_bitcast_fusion.1
  224.7 5.1 %fusion.51 = (f32[165]{0:T(256)S(1)}, f32[165]{0:T(256)S(1)}, f32[4,165,1024]{2,1,0:T(8,128)}) fusion(f32[165]{0:T(256)S(1)} %get-tuple-element.53, f32[165]{0:T(256)S(1)} %get-tuple-element.54, bf16[4,165,1024]{2,0,1:T(4,128)(2,1)S(1)} %copy-done.1, f32[165]{0:T(256)S(1)} %copy-done.12, f32[165]{0:T(256)S(1)} %copy-done.10, ...), kind=kOutput, calls=%fused_computation.102 | convolution fusion | flops 190586560 | bytes 5200948 | tf_op jit(solution)/shard_map/bdp,cd->bcp/dot_general | solution.py:128
  229.8 37.7 %all-reduce.2 = (f32[165]{0:T(256)S(1)}, f32[165]{0:T(256)S(1)}, f32[3,3,33,33]{3,2,1,0:T(8,128)}) all-reduce(f32[165]{0:T(256)S(1)} %get-tuple-element.33, f32[165]{0:T(256)S(1)} %get-tuple-element.32, f32[3,3,33,33]{3,2,1,0:T(8,128)S(1)} %pad_maximum_fusion), channel_id=1, replica_groups=mesh['dp'=8,'chan'=4] {'dp'}, use_global_device_ids=true, to_apply=%region_20.21 | all-reduce | flops 10131 | bytes 81048 | tf_op jit(solution)/shard_map/psum | solution.py:131
  267.5 6.5 %fusion.19 = (f32[4,165,1024]{2,1,0:T(8,128)}, f32[4,165,1024]{2,1,0:T(8,128)S(1)}) fusion(f32[4,165,1024]{2,1,0:T(8,128)} %get-tuple-element.59, f32[]{:T(128)} %get-tuple-element.48, f32[165]{0:T(256)S(1)} %get-tuple-element.65, f32[165]{0:T(256)S(1)} %get-tuple-element.66, f32[165]{0:T(256)S(1)} %copy-done.10, f32[165]{0:T(256)S(1)} %get-tuple-element.53, ...), kind=kLoop, calls=%fused_computation.24 | loop fusion | flops 10137600 | bytes 10833788 | tf_op jit(solution)/shard_map/add | solution.py:139
  274.0 1.3 dynamic-slice_select_fusion
  275.3 5.0 %copy.94 = f32[4,165,1024]{2,0,1:T(4,128)} copy(f32[4,165,1024]{2,1,0:T(8,128)} %get-tuple-element.55) | data formatting | bytes 5406720
  281.0 3.3 copy.93
  284.3 41.1 %all-reduce.15.cloned.1.call-done = f32[165,132]{0,1:T(8,128)} async-done(((f32[165,132]{0,1:T(8,128)}), f32[165,132]{0,1:T(8,128)}) %all-reduce.15.cloned.1.call-update) | async-done | bytes 87136 | tf_op jit(solution)/shard_map/psum | solution.py:131
  325.4 1.6 copy.167
  (75 shorter events, 10.8 us)
Async XLA Ops:
  7.2 129.5 %copy-start = (bf16[3,3,33,33]{3,2,1,0:T(8,128)(2,1)S(1)}, bf16[3,3,33,33]{3,2,1,0:T(8,128)(2,1)}, u32[]{:S(2)}) copy-start(bf16[3,3,33,33]{3,2,1,0:T(8,128)(2,1)} %param.16) | copy-start | bytes 58810
  7.2 34.0 %copy-start.8 = (bf16[165,132]{0,1:T(8,128)(2,1)S(1)}, bf16[165,132]{0,1:T(8,128)(2,1)}, u32[]{:S(2)}) copy-start(bf16[165,132]{0,1:T(8,128)(2,1)} %param.13) | copy-start | bytes 130684
  7.2 87.2 %all-reduce.17.cloned.1.call-start = ((), (), s32[]{:S(2)}) async-start(), calls=%async_computation.4 | async-start | bytes 4325376
  40.1 1.1 copy-start.2
  41.7 4.8 %copy-start.4 = (bf16[4,165,1024]{2,0,1:T(4,128)(2,1)S(1)}, bf16[4,165,1024]{2,0,1:T(4,128)(2,1)}, u32[]{:S(2)}) copy-start(bf16[4,165,1024]{2,0,1:T(4,128)(2,1)} %param.17) | copy-start | bytes 4055044
  44.5 3.6 %copy-start.18 = (u32[32]{0:T(128)S(1)}, u32[32]{0:T(128)}, u32[]{:S(2)}) copy-start(u32[32]{0:T(128)} %constant.67) | copy-start | bytes 388
  44.5 84.7 %all-reduce.13.cloned.1.call-start = ((), (), s32[]{:S(2)}) async-start(), calls=%async_computation.1 | async-start | bytes 655360 | tf_op jit(solution)/shard_map/psum | solution.py:14
  47.8 173.9 %all-gather.2.cloned.1.call-start = ((), (), s32[]{:S(2)}) async-start(), calls=%async_computation.2 | async-start | bytes 1351680 | tf_op jit(solution)/shard_map/all_gather | solution.py:127
  136.2 0.7 copy-start.19
  142.5 27.4 %copy-start.11 = (f32[33]{0:T(128)S(1)}, f32[33]{0:T(128)}, u32[]{:S(2)}) copy-start(f32[33]{0:T(128)} %param.14) | copy-start | bytes 400
  142.5 27.4 %copy-start.15 = (f32[33]{0:T(128)S(1)}, f32[33]{0:T(128)}, u32[]{:S(2)}) copy-start(f32[33]{0:T(128)} %param.15) | copy-start | bytes 400
  188.9 5.3 %copy-start.16 = (f32[33]{0:T(128)}, f32[33]{0:T(128)S(1)}, u32[]{:S(2)}) copy-start(f32[33]{0:T(128)S(1)} %get-tuple-element.68) | copy-start | bytes 400
  188.9 5.3 %copy-start.17 = (f32[33]{0:T(128)}, f32[33]{0:T(128)S(1)}, u32[]{:S(2)}) copy-start(f32[33]{0:T(128)S(1)} %get-tuple-element.69) | copy-start | bytes 400
  191.0 83.1 %all-reduce.11.cloned.1.call-start = ((), (), s32[]{:S(2)}) async-start(), calls=%async_computation | async-start | bytes 1310720 | tf_op jit(solution)/shard_map/psum | solution.py:107
  208.3 4.7 %copy-start.5 = (bf16[4,33,32,32]{1,3,2,0:T(8,128)(2,1)S(1)}, bf16[4,33,32,32]{1,3,2,0:T(8,128)(2,1)}, u32[]{:S(2)}) copy-start(bf16[4,33,32,32]{1,3,2,0:T(8,128)(2,1)} %copy.85) | copy-start | bytes 811012
  208.3 4.7 %copy-start.6 = (bf16[4,33,32,32]{1,3,2,0:T(8,128)(2,1)S(1)}, bf16[4,33,32,32]{1,3,2,0:T(8,128)(2,1)}, u32[]{:S(2)}) copy-start(bf16[4,33,32,32]{1,3,2,0:T(8,128)(2,1)} %copy.84) | copy-start | bytes 811012
  216.3 2.1 copy-start.7
  218.4 3.3 copy-start.3
  219.5 5.1 %copy-start.1 = (bf16[4,165,1024]{2,0,1:T(4,128)(2,1)S(1)}, bf16[4,165,1024]{2,0,1:T(4,128)(2,1)}, u32[]{:S(2)}) copy-start(bf16[4,165,1024]{2,0,1:T(4,128)(2,1)} %param.10) | copy-start | bytes 4055044
  219.5 5.1 %copy-start.10 = (f32[165]{0:T(256)S(1)}, f32[165]{0:T(256)}, u32[]{:S(2)}) copy-start(f32[165]{0:T(256)} %param.11) | copy-start | bytes 1984
  219.5 5.2 %copy-start.12 = (f32[165]{0:T(256)S(1)}, f32[165]{0:T(256)}, u32[]{:S(2)}) copy-start(f32[165]{0:T(256)} %param.12) | copy-start | bytes 1984
  219.7 4.9 %copy-start.9 = (bf16[165,132]{0,1:T(8,128)(2,1)S(1)}, bf16[165,132]{0,1:T(8,128)(2,1)}, u32[]{:S(2)}) copy-start(bf16[165,132]{0,1:T(8,128)(2,1)} %param.13) | copy-start | bytes 130684
  219.8 105.6 %all-reduce.15.cloned.1.call-start = ((), (), s32[]{:S(2)}) async-start(), calls=%async_computation.3 | async-start | bytes 278528 | tf_op jit(solution)/shard_map/psum | solution.py:131
  267.5 6.5 %copy-start.13 = (f32[165]{0:T(256)}, f32[165]{0:T(256)S(1)}, u32[]{:S(2)}) copy-start(f32[165]{0:T(256)S(1)} %get-tuple-element.65) | copy-start | bytes 1984
  267.5 6.5 %copy-start.14 = (f32[165]{0:T(256)}, f32[165]{0:T(256)S(1)}, u32[]{:S(2)}) copy-start(f32[165]{0:T(256)S(1)} %get-tuple-element.66) | copy-start | bytes 1984
Sparse Core Ops, SparseCore 0:
  44.6 49.6 all-reduce.16
  96.8 32.3 all-reduce.12
  191.1 14.6 all-gather.1
  219.9 31.6 all-reduce.10
  255.7 69.5 all-reduce.14
where the time goes:
time: 339 us; the launch traced here: 334 us
  waiting for transfers between devices  120 us (35%)
  blocking collectives  99.9 us (29%)
  local copies, waits for them, and re-layouts  47.3 us (14%)
  matrix products  25.3 us (7%)
  other arithmetic  23.6 us (7%)
  between operations  17.2 us (5%)
    unnamed x6, waiting for transfers between devices  45.2 us
    psum x1, waiting for transfers between devices, on_device(): lax.psum((weight_part, totals(grad_pre_one), totals(grad_pre_one * norm_o...  41.1 us
    psum x1, blocking collectives, on_device(): lax.psum((weight_part, totals(grad_pre_one), totals(grad_pre_one * norm_o...  37.7 us
    psum x1, waiting for transfers between devices, broadcast(): return lax.psum(block, axis)  33.8 us
    psum x1, blocking collectives, on_device(): lax.psum((totals(weighted), totals(weighted * inputs), jnp.sum(pixel_mask...  23.8 us
    psum x1, blocking collectives, on_device(): lax.psum((totals(weighted_two), totals(weighted_two * hidden)), 'dp')  21.3 us
    unnamed x48, local copies, waits for them, and re-layouts  18 us
    psum x1, blocking collectives, on_device(): lax.psum((kernel_part, totals(grad_pre_two), totals(grad_pre_two * norm_t...  17.1 us
  transfers between devices with their start and end apart: 5, of which 3 were waited for; matrix products, arithmetic and copies ran while one was open for 17% of the time, Pallas kernels for 0%

commit v1 on v0

v1 whole, which is shorter than its diff:
```python
import functools

import jax
import jax.numpy as jnp
from jax import lax
from jax.experimental import pallas as pl
from jax.experimental.pallas import tpu as pltpu
from jax.sharding import PartitionSpec as P

SIDE = 32
EPS = 1e-05
LANES = 128
TAP = 48
TAPS = 512
OWNERS = 8

MESH = pl.DeviceIdType.MESH
F32 = jnp.float32
BF16 = jnp.bfloat16


def pad_to(size, unit):
    return (size + unit - 1) // unit * unit


def iota(shape, axis):
    return lax.broadcasted_iota(jnp.int32, shape, axis)


def as_row(column):
    n = column.shape[0]
    eye = iota((n, LANES), 0) == iota((n, LANES), 1)
    return jnp.sum(jnp.where(eye, column, 0.0), axis=0, keepdims=True)


def as_column(row, n):
    eye = iota((n, LANES), 0) == iota((n, LANES), 1)
    return jnp.broadcast_to(jnp.sum(jnp.where(eye, row, 0.0), axis=1, keepdims=True), (n, LANES))


def as_rows(values, sizes):
    column = jnp.sum(values, axis=1, keepdims=True)
    rows, start = [], 0
    for size in sizes:
        rows.append(as_row(column[start : start + size]))
        start += size
    return rows


def layer(
    cfg,
    feat_h, cot_h, w1_h, gain1_h, bias1_h, gain2_h, bias2_h, w2_h, side_h, slot_h,
    out_x, out_g, out_w1, out_g1, out_b1, out_w2, out_g2, out_b2,
    feat, cot, w1v, gain1v, bias1v, gain2v, bias2v, w2v, side, slot,
    mask, xb, act, slope, gp1, gact,
    col_a, col_b, col_m, col_k, col_c, sum_a, sum_b, rowbuf,
    w1s, part, rx_a, rx_b, rx_x, hid,
    graw, gsend, grecv, g9, w2blk, w2r, w2b, gsl,
    act2, gp2, back, zbuf, gall, gcur, gha,
    cb, cw, cwr, rsl, fin, w1acc, w2acc,
    ar1, ar2, ar3, ar4,
    load_sem, s1, r1, s2, r2, s3, r3, s4, r4, sx, rxs, sg, rg, sw, rw, sb, rb, sh, rh, so, ro, sc, rc, sr, rr, sa, ra,
):
    n_dp, n_ch, n_img, n_c, n_px, n_d, grow = cfg
    n_dev = n_dp * n_ch
    cp = xb.shape[1]
    dpad = w1s.shape[0]
    d8 = pad_to(n_d, 8)
    tiles = n_px // LANES
    rpc = tiles * n_img
    c_sizes = (LANES, cp - LANES)
    d_sizes = (LANES, d8 - LANES)
    dp = lax.axis_index("dp")
    ch = lax.axis_index("chan")
    me = dp * n_ch + ch
    half = n_ch // 2
    cx, cc = ch // half, lax.rem(ch, half)
    sib = cx * half + (1 - cc)
    xp = (1 - cx) * half + cc
    xs = (1 - cx) * half + (1 - cc)

    def dev_peer(k):
        q = lax.rem(me + k, n_dev)
        return {"dp": q // n_ch, "chan": lax.rem(q, n_ch)}

    def dp_peer(k):
        return {"dp": lax.rem(dp + k, n_dp)}

    def ch_peer(k):
        return {"chan": lax.rem(ch + k, n_ch)}

    loads = [
        pltpu.make_async_copy(h, v, load_sem.at[i])
        for i, (h, v) in enumerate(
            (
                (feat_h, feat), (cot_h, cot), (w1_h, w1v), (gain1_h, gain1v), (bias1_h, bias1v),
                (gain2_h, gain2v), (bias2_h, bias2v), (w2_h, w2v), (side_h, side), (slot_h, slot),
            )
        )
    ]
    for copy in loads:
        copy.start()
    barrier = pltpu.get_barrier_semaphore()

    def greet(k, c):
        pl.semaphore_signal(barrier, inc=1, device_id=dev_peer(k), device_id_type=MESH)
        return c

    lax.fori_loop(1, n_dev, greet, 0)

    def remote(src, dst, send, recv, device):
        return pltpu.make_async_remote_copy(
            src_ref=src, dst_ref=dst, send_sem=send, recv_sem=recv, device_id=device, device_id_type=MESH
        )

    def share_start(slots, mine, count, peer, send, recv):
        def step(k, c):
            remote(slots.at[mine], slots.at[mine], send.at[k], recv.at[k], peer(k)).start()
            return c

        lax.fori_loop(1, count, step, 0)

    def share_wait(slots, mine, count, peer, send, recv):
        def step(k, c):
            remote(slots.at[mine], slots.at[mine], send.at[k], recv.at[k], peer(k)).wait()
            return c

        lax.fori_loop(1, count, step, 0)

    def total(slots):
        if slots.shape[0] <= 32:
            value = slots[0]
            for i in range(1, slots.shape[0]):
                value = value + slots[i]
            return value
        return lax.fori_loop(1, slots.shape[0], lambda i, v: v + slots[i], slots[0])

    for copy in loads[8:]:
        copy.wait()
    lane16 = iota((16, n_px), 1)
    row_of, col_of = lane16 >> 5, lane16 & (SIDE - 1)
    count_here = jnp.int32(0)
    for b in range(n_img):
        s = side[b]
        count_here = count_here + s * s
        mask[b] = jnp.where((row_of < s) & (col_of < s), 1.0, 0.0)
    new_slot = slot[slot.shape[0] - 1]
    per_device = n_c // grow
    slot_of = iota((rpc, LANES), 0) * 0 + new_slot

    n_rows = feat.shape[0]
    out_x[pl.ds(n_rows, out_x.shape[0] - n_rows), :] = jnp.zeros((out_x.shape[0] - n_rows, LANES), F32)
    out_g[pl.ds(n_rows, out_g.shape[0] - n_rows), :] = jnp.zeros((out_g.shape[0] - n_rows, LANES), F32)
    step_rows = 3 * rpc
    loads[0].wait()

    def widen(i, c):
        r = pl.ds(pl.multiple_of(i * step_rows, step_rows), step_rows)
        out_x[r, :] = feat[r, :].astype(F32)
        return c

    lax.fori_loop(0, n_rows // step_rows, widen, 0)

    def relayout(g, c):
        base = g * 16 * rpc
        r = pl.ds(pl.multiple_of(g * 16, 16), 16)
        s_acc = jnp.zeros((16, LANES), F32)
        q_acc = jnp.zeros((16, LANES), F32)
        for b in range(n_img):
            for t in range(tiles):
                k = t * n_img + b
                v = jnp.concatenate(
                    [out_x[pl.ds(base + h * 8 * rpc + k, 8, stride=rpc), :] for h in range(2)], axis=0
                )
                w = v * mask[b, :, t * LANES : (t + 1) * LANES]
                s_acc = s_acc + w
                q_acc = q_acc + w * v
                xb[b, r, t * LANES : (t + 1) * LANES] = v.astype(BF16)
        sum_a[r, :] = s_acc
        sum_b[r, :] = q_acc
        return c

    lax.fori_loop(0, cp // 16, relayout, 0)
    lane1 = iota((1, LANES), 1)
    s0, sq0 = as_rows(sum_a[...], c_sizes), as_rows(sum_b[...], c_sizes)
    ar1[dp, 0:1, :] = s0[0]
    ar1[dp, 1:2, :] = jnp.where(lane1 == LANES - 1, count_here.astype(F32), s0[1])
    ar1[dp, 2:3, :] = sq0[0]
    ar1[dp, 3:4, :] = sq0[1]

    loads[7].wait()
    w2blk[...] = jnp.zeros(w2blk.shape, BF16)
    acc = jnp.zeros((grow, w2blk.shape[1]), F32)
    for t in range(9):
        place = jnp.where(
            iota((grow, w2blk.shape[1]), 1) == iota((grow, w2blk.shape[1]), 0) + t * TAP, 1.0, 0.0
        ).astype(BF16)
        acc = acc + jnp.dot(w2v[t], place, preferred_element_type=F32)
    w2blk[0:grow, :] = acc.astype(BF16)
    loads[5].wait()
    loads[6].wait()
    gsl[ch, 0:1, 0:grow] = gain2v[...]
    gsl[ch, 1:2, 0:grow] = bias2v[...]
    loads[1].wait()

    def widen_cot(i, c):
        r = pl.ds(pl.multiple_of(i * step_rows, step_rows), step_rows)
        out_g[r, :] = cot[r, :].astype(F32)
        return c

    lax.fori_loop(0, n_rows // step_rows, widen_cot, 0)
    graw[...] = jnp.zeros(graw.shape, F32)

    picks = [jnp.where(slot_of == ch * per_device + i, 1.0, 0.0) for i in range(per_device)]

    def pick(i, c):
        v = jnp.zeros((rpc, LANES), F32)
        for k in range(per_device):
            v = v + out_g[pl.ds(pl.multiple_of((k * grow + i) * rpc, rpc), rpc), :] * picks[k]
        graw[pl.ds(pl.multiple_of(i * rpc, rpc), rpc), :] = v
        return c

    lax.fori_loop(0, grow, pick, 0)
    for b in range(n_img):
        for t in range(tiles):
            for h in range(TAP // 16):
                v = jnp.concatenate(
                    [
                        graw[pl.ds((h * 16 + i * 8) * rpc + t * n_img + b, 8, stride=rpc), :]
                        for i in range(2)
                    ],
                    axis=0,
                )
                v = v * mask[b, :, t * LANES : (t + 1) * LANES]
                gsend[b, h * 16 : h * 16 + 16, t * LANES : (t + 1) * LANES] = v.astype(BF16)

    pl.semaphore_wait(barrier, n_dev - 1)
    share_start(ar1, dp, n_dp, dp_peer, s1, r1)
    w2r[ch] = w2blk[...]
    share_start(gsl, ch, n_ch, ch_peer, sb, rb)
    for k in range(1, n_ch):
        to = lax.rem(ch + k, n_ch)
        remote(gsend.at[to], grecv.at[ch], sg.at[k], rg.at[k], {"chan": to}).start()
    share_start(w2r, ch, n_ch, ch_peer, sw, rw)

    loads[2].wait()
    w1s[...] = jnp.zeros(w1s.shape, BF16)
    w1s[0:n_d, 0:n_c] = w1v[...]
    rowbuf[...] = jnp.zeros(rowbuf.shape, F32)
    loads[3].wait()
    loads[4].wait()
    rowbuf[0:1, :] = gain1v[0:1, 0:LANES]
    rowbuf[1:2, 0 : n_c - LANES] = gain1v[0:1, LANES:n_c]
    rowbuf[2:3, :] = bias1v[0:1, 0:LANES]
    rowbuf[3:4, 0 : n_c - LANES] = bias1v[0:1, LANES:n_c]

    share_wait(ar1, dp, n_dp, dp_peer, s1, r1)
    tot1 = total(ar1)
    count = tot1[1:2, LANES - 1 : LANES]
    mean1, rstd1, scale1 = [], [], []
    for i in range(2):
        mean = tot1[i : i + 1] / count
        rstd = lax.rsqrt(tot1[2 + i : 3 + i] / count - mean * mean + EPS)
        here = lane1 + i * LANES
        ids = ch * n_c + here
        first = new_slot * grow
        keep = jnp.where(
            (here < n_c) & ((ids < first) | (ids >= first + grow)), 1.0, 0.0
        )
        scale = rstd * rowbuf[i : i + 1, :]
        shift = rowbuf[2 + i : 3 + i, :] - mean * scale
        size = c_sizes[i]
        r = pl.ds(i * LANES, size)
        col_a[r, :] = as_column(0.5 * scale * keep, size)
        col_b[r, :] = as_column(0.5 * shift * keep, size)
        col_m[r, :] = as_column(mean, size)
        col_k[r, :] = as_column(keep, size)
        mean1.append(mean)
        rstd1.append(rstd)
        scale1.append(scale)

    def partial(j):
        def body(g, c):
            r = pl.ds(pl.multiple_of(g * 16, 16), 16)
            a, b = col_a[r, :], col_b[r, :]
            for t in range(tiles):
                sl = slice(t * LANES, (t + 1) * LANES)
                v = xb[j, r, sl].astype(F32) * a + b
                act[j, r, sl] = ((v * jnp.tanh(v) + v) * mask[j, :, sl]).astype(BF16)
            return c

        lax.fori_loop(0, cp // 16, body, 0)
        part[j] = jnp.dot(w1s[...], act[j], preferred_element_type=F32)

    rows_d = pl.ds(0, d8)
    partial(xs)
    to_sib_a = remote(part.at[xs, rows_d], rx_a.at[rows_d], sx.at[0], rxs.at[0], {"chan": sib})
    to_sib_a.start()
    partial(xp)
    to_sib_a.wait()

    def add_a(g, c):
        r = pl.ds(pl.multiple_of(g * 8, 8), 8)
        part[xp, r, :] = part[xp, r, :] + rx_a[r, :]
        return c

    lax.fori_loop(0, d8 // 8, add_a, 0)
    to_x = remote(part.at[xp, rows_d], rx_x.at[rows_d], sx.at[1], rxs.at[1], {"chan": xp})
    to_x.start()
    partial(sib)
    to_sib_b = remote(part.at[sib, rows_d], rx_b.at[rows_d], sx.at[2], rxs.at[2], {"chan": sib})
    to_sib_b.start()
    partial(ch)

    for k in range(1, n_ch):
        to = lax.rem(ch + k, n_ch)
        remote(gsend.at[to], grecv.at[ch], sg.at[k], rg.at[k], {"chan": to}).wait()
    share_wait(w2r, ch, n_ch, ch_peer, sw, rw)
    share_wait(gsl, ch, n_ch, ch_peer, sb, rb)
    g = gsend[ch].astype(F32)
    for k in range(1, n_ch):
        g = g + grecv[lax.rem(ch + k, n_ch)].astype(F32)
    gcur[...] = g
    px = iota((TAP, n_px), 1)
    py, pxx = px >> 5, px & (SIDE - 1)
    for ky in range(3):
        for kx in range(3):
            shift = (ky - 1) * SIDE + (kx - 1)
            t = ky * 3 + kx
            v = gcur[...]
            if shift != 0:
                v = pltpu.roll(v, shift % n_px, 1)
            ok = None
            for off, pos in ((ky - 1, py), (kx - 1, pxx)):
                if off == 1:
                    test = pos >= 1
                elif off == -1:
                    test = pos <= SIDE - 2
                else:
                    continue
                ok = test if ok is None else ok & test
            if ok is not None:
                v = jnp.where(ok, v, 0.0)
            g9[t * TAP : (t + 1) * TAP, :] = v.astype(BF16)
    acc = jnp.zeros((dpad, w2b.shape[1]), F32)
    for j in range(n_ch):
        rows = iota((dpad, TAP), 0)
        cols = iota((dpad, TAP), 1)
        place = jnp.where((rows == cols + j * grow) & (cols < grow), 1.0, 0.0).astype(BF16)
        acc = acc + jnp.dot(place, w2r[j], preferred_element_type=F32)
    w2b[...] = acc.astype(BF16)
    g9[pl.ds(9 * TAP, TAPS - 9 * TAP), :] = jnp.zeros((TAPS - 9 * TAP, n_px), BF16)
    back[...] = jnp.dot(w2b[...], g9[...], preferred_element_type=F32)
    rows = iota((dpad, LANES), 0)
    cols = iota((dpad, LANES), 1)
    gain2c = jnp.zeros((dpad, 1), F32)
    bias2c = jnp.zeros((dpad, 1), F32)
    for j in range(n_ch):
        place = (rows == cols + j * grow) & (cols < grow)
        gain2c = gain2c + jnp.sum(jnp.where(place, gsl[j, 0:1, :], 0.0), axis=1, keepdims=True)
        bias2c = bias2c + jnp.sum(jnp.where(place, gsl[j, 1:2, :], 0.0), axis=1, keepdims=True)
    col_c[0] = jnp.broadcast_to(gain2c, (dpad, LANES))
    col_c[1] = jnp.broadcast_to(bias2c, (dpad, LANES))

    to_x.wait()
    to_sib_b.wait()
    sum_a[...] = jnp.zeros(sum_a.shape, F32)
    sum_b[...] = jnp.zeros(sum_b.shape, F32)

    def gather(g, c):
        r = pl.ds(pl.multiple_of(g * 8, 8), 8)
        s_acc = jnp.zeros((8, LANES), F32)
        q_acc = jnp.zeros((8, LANES), F32)
        for t in range(tiles):
            sl = slice(t * LANES, (t + 1) * LANES)
            v = (part[ch, r, sl] + rx_b[r, sl]) + rx_x[r, sl]
            hid[r, sl] = v
            s_acc = s_acc + v
            q_acc = q_acc + v * v
        sum_a[r, :] = s_acc
        sum_b[r, :] = q_acc
        return c

    lax.fori_loop(0, d8 // 8, gather, 0)
    hid[pl.ds(d8, dpad - d8), :] = jnp.zeros((dpad - d8, n_px), F32)
    gp2[...] = jnp.zeros(gp2.shape, F32)

    def pack(slots):
        s, q = as_rows(sum_a[0:d8, :], d_sizes), as_rows(sum_b[0:d8, :], d_sizes)
        slots[me, 0:1, :] = s[0]
        slots[me, 1:2, :] = s[1]
        slots[me, 2:3, :] = q[0]
        slots[me, 3:4, :] = q[1]

    def columns_d(row0, row1):
        tail = jnp.zeros((dpad - d8, LANES), F32)
        return jnp.concatenate(
            [as_column(row0, LANES), as_column(row1, d8 - LANES), tail], axis=0
        )

    pack(ar2)
    share_start(ar2, me, n_dev, dev_peer, s2, r2)

    def slopes(j):
        def body(g, c):
            r = pl.ds(pl.multiple_of(g * 16, 16), 16)
            a, b = col_a[r, :], col_b[r, :]
            k = 0.5 * col_k[r, :]
            for t in range(tiles):
                sl = slice(t * LANES, (t + 1) * LANES)
                v = xb[j, r, sl].astype(F32) * a + b
                th = jnp.tanh(v)
                slope[j, r, sl] = ((1.0 + th) * (1.0 + v * (1.0 - th))) * (mask[j, :, sl] * k)
            return c

        lax.fori_loop(0, cp // 16, body, 0)

    for j in range(n_img):
        slopes(j)

    share_wait(ar2, me, n_dev, dev_peer, s2, r2)
    tot2 = total(ar2)
    mean2 = [tot2[i : i + 1] / count for i in range(2)]
    rstd2 = [lax.rsqrt(tot2[2 + i : 3 + i] / count - mean2[i] * mean2[i] + EPS) for i in range(2)]
    mean2c = columns_d(*mean2)
    rstd2c = columns_d(*rstd2)
    scale2c = rstd2c * col_c[0]
    col_c[2] = mean2c
    col_c[3] = rstd2c
    col_c[4] = scale2c
    col_c[5] = 0.5 * scale2c
    col_c[6] = 0.5 * (col_c[1] - mean2c * scale2c)

    def second(g, c):
        r = pl.ds(pl.multiple_of(g * 16, 16), 16)
        a, b, m = col_c[5, r, :], col_c[6, r, :], col_c[2, r, :]
        s_acc = jnp.zeros((16, LANES), F32)
        q_acc = jnp.zeros((16, LANES), F32)
        for t in range(tiles):
            sl = slice(t * LANES, (t + 1) * LANES)
            h = hid[r, sl]
            mk = mask[ch, :, sl]
            v = h * a + b
            th = jnp.tanh(v)
            act2[r, sl] = ((v * th + v) * mk).astype(BF16)
            gp = (0.5 * mk) * ((1.0 + th) * (1.0 + v * (1.0 - th))) * back[r, sl]
            gp2[r, sl] = gp
            s_acc = s_acc + gp
            q_acc = q_acc + gp * (h - m)
        sum_a[r, :] = s_acc
        sum_b[r, :] = q_acc
        return c

    lax.fori_loop(0, dpad // 16, second, 0)
    pack(ar3)
    share_start(ar3, me, n_dev, dev_peer, s3, r3)

    w2acc[...] = lax.dot_general(
        act2[...], g9[...], (((1,), (1,)), ((), ())), preferred_element_type=F32
    )
    cw[...] = jnp.zeros(cw.shape, F32)
    for j in range(n_ch):
        for q in range(20):
            lt, rt = q // 5, q % 5
            cw[j, q // 3, (q % 3) * 8 : (q % 3) * 8 + 8, :] = w2acc[
                j * grow + rt * 8 : j * grow + rt * 8 + 8, lt * LANES : (lt + 1) * LANES
            ]
    for k in range(1, n_ch):
        to = lax.rem(ch + k, n_ch)
        remote(cw.at[to], cwr.at[ch], sc.at[k], rc.at[k], {"chan": to}).start()
    zbuf[...] = lax.dot_general(
        w2b[...], act2[...], (((0,), (0,)), ((), ())), preferred_element_type=F32
    )
    new = jnp.zeros((TAP, n_px), F32)
    for ky in range(3):
        for kx in range(3):
            shift = (ky - 1) * SIDE + (kx - 1)
            t = ky * 3 + kx
            v = zbuf[t * TAP : (t + 1) * TAP, :]
            if shift != 0:
                v = pltpu.roll(v, (-shift) % n_px, 1)
            ok = None
            for off, pos in ((ky - 1, py), (kx - 1, pxx)):
                if off == -1:
                    test = pos >= 1
                elif off == 1:
                    test = pos <= SIDE - 2
                else:
                    continue
                ok = test if ok is None else ok & test
            if ok is not None:
                v = jnp.where(ok, v, 0.0)
            new = new + v
    new = new * jnp.concatenate([mask[ch]] * (TAP // 16), axis=0)
    gall[ch] = new[0 : gall.shape[1]]

    share_wait(ar3, me, n_dev, dev_peer, s3, r3)
    tot3 = total(ar3)
    gain_sum2 = [tot3[2 + i : 3 + i] * rstd2[i] for i in range(2)]
    bias_sum2 = [tot3[i : i + 1] for i in range(2)]
    gain_sum2c = columns_d(*gain_sum2)
    bias_sum2c = columns_d(*bias_sum2)
    col_c[5] = col_c[4] * bias_sum2c / count
    col_c[6] = col_c[4] * col_c[3] * gain_sum2c / count

    def third(g, c):
        r = pl.ds(pl.multiple_of(g * 16, 16), 16)
        c1, c2, c3, m = col_c[4, r, :], col_c[5, r, :], col_c[6, r, :], col_c[2, r, :]
        for t in range(tiles):
            sl = slice(t * LANES, (t + 1) * LANES)
            gha[ch, r, sl] = (
                c1 * gp2[r, sl] - mask[ch, :, sl] * (c2 + c3 * (hid[r, sl] - m))
            ).astype(BF16)
        return c

    lax.fori_loop(0, dpad // 16, third, 0)

    def spread(buf, send, recv):
        to_sib = remote(buf.at[ch], buf.at[ch], send.at[0], recv.at[0], {"chan": sib})
        to_xp = remote(buf.at[ch], buf.at[ch], send.at[1], recv.at[1], {"chan": xp})
        on = remote(buf.at[xp], buf.at[xp], send.at[2], recv.at[2], {"chan": sib})
        return to_sib, to_xp, on

    grad_sib, grad_xp, grad_on = spread(gha, sh, rh)
    grad_xp.start()
    grad_sib.start()
    new_sib, new_xp, new_on = spread(gall, so, ro)
    new_xp.start()
    new_sib.start()
    d_rows, d_cols = iota((dpad, LANES), 0), iota((dpad, LANES), 1)
    here_d = (d_rows == d_cols + ch * grow) & (d_cols < grow)
    out_g2[...] = jnp.sum(jnp.where(here_d, gain_sum2c, 0.0), axis=0, keepdims=True)[:, 0:grow]
    out_b2[...] = jnp.sum(jnp.where(here_d, bias_sum2c, 0.0), axis=0, keepdims=True)[:, 0:grow]

    w1acc[...] = jnp.zeros(w1acc.shape, F32)
    sum_a[...] = jnp.zeros(sum_a.shape, F32)
    sum_b[...] = jnp.zeros(sum_b.shape, F32)

    def weight_grad(j):
        w1acc[0:dpad, 0:cp] = w1acc[0:dpad, 0:cp] + lax.dot_general(
            gha[j], act[j], (((1,), (1,)), ((), ())), preferred_element_type=F32
        )

    def input_grad(j):
        gact[...] = lax.dot_general(
            w1s[...], gha[j], (((0,), (0,)), ((), ())), preferred_element_type=F32
        )

        def body(g, c):
            r = pl.ds(pl.multiple_of(g * 16, 16), 16)
            m = col_m[r, :]
            s_acc, q_acc = sum_a[r, :], sum_b[r, :]
            for t in range(tiles):
                sl = slice(t * LANES, (t + 1) * LANES)
                gp = gact[r, sl] * slope[j, r, sl]
                gp1[j, r, sl] = gp
                s_acc = s_acc + gp
                q_acc = q_acc + gp * (xb[j, r, sl].astype(F32) - m)
            sum_a[r, :] = s_acc
            sum_b[r, :] = q_acc
            return c

        lax.fori_loop(0, cp // 16, body, 0)

    weight_grad(ch)
    input_grad(ch)
    grad_sib.wait()
    weight_grad(sib)
    input_grad(sib)
    grad_xp.wait()
    grad_on.start()
    weight_grad(xp)
    input_grad(xp)
    for k in range(1, n_ch):
        to = lax.rem(ch + k, n_ch)
        remote(cw.at[to], cwr.at[ch], sc.at[k], rc.at[k], {"chan": to}).wait()
    for q in range(OWNERS):
        v = cw[ch, q]
        for k in range(1, n_ch):
            v = v + cwr[lax.rem(ch + k, n_ch), q]
        cb[q, 40:64, :] = v
    grad_on.wait()
    weight_grad(xs)

    for q in range(OWNERS):
        r, h = q % 4, q // 4
        cb[q, 0:40, :] = w1acc[r * 40 : r * 40 + 40, h * LANES : (h + 1) * LANES]
    stride = n_dp // OWNERS
    my_part = dp // stride
    is_owner = lax.rem(dp, stride) == 0

    def part_to(k):
        q = lax.rem(my_part + k, OWNERS)
        return q, q * stride

    def push(k, c):
        q, to = part_to(k)

        @pl.when(to != dp)
        def _():
            remote(cb.at[q], rsl.at[dp], sr.at[k], rr.at[dp], {"dp": to}).start()

        return c

    lax.fori_loop(0, OWNERS, push, 0)
    input_grad(xs)
    s4_, q4_ = as_rows(sum_a[...], c_sizes), as_rows(sum_b[...], c_sizes)
    for i in range(2):
        ar4[dp, i : i + 1, :] = s4_[i]
        ar4[dp, 2 + i : 3 + i, :] = q4_[i]
    share_start(ar4, dp, n_dp, dp_peer, s4, r4)

    def push_wait(k, c):
        q, to = part_to(k)

        @pl.when(to != dp)
        def _():
            remote(cb.at[q], rsl.at[dp], sr.at[k], rr.at[dp], {"dp": to}).wait_send()

        return c

    def pull(k, c):
        src = lax.rem(dp + k, n_dp)
        remote(cb.at[0], rsl.at[src], sr.at[0], rr.at[src], {"dp": src}).wait_recv()
        return c

    @pl.when(is_owner)
    def _():
        lax.fori_loop(1, n_dp, pull, 0)
        v = cb[my_part]
        for k in range(1, n_dp):
            v = v + rsl[lax.rem(dp + k, n_dp)]
        fin[my_part] = v

        def give(k, c):
            remote(fin.at[my_part], fin.at[my_part], sa.at[k], ra.at[my_part], dp_peer(k)).start()
            return c

        lax.fori_loop(1, n_dp, give, 0)

    lax.fori_loop(0, OWNERS, push_wait, 0)

    new_xp.wait()
    new_on.start()
    new_sib.wait()
    new_on.wait()
    for b in range(n_img):
        for t in range(tiles):
            for h in range(gall.shape[1] // 8):
                graw[pl.ds(h * 8 * rpc + t * n_img + b, 8, stride=rpc), :] = gall[
                    b, h * 8 : h * 8 + 8, t * LANES : (t + 1) * LANES
                ]
    for s in range(per_device):
        chosen = slot_of == ch * per_device + s

        def place_new(i, c):
            src = pl.ds(pl.multiple_of(i * rpc, rpc), rpc)
            dst = pl.ds(pl.multiple_of((s * grow + i) * rpc, rpc), rpc)
            out_x[dst, :] = jnp.where(chosen, graw[src, :], out_x[dst, :])
            return c

        lax.fori_loop(0, grow, place_new, 0)

    share_wait(ar4, dp, n_dp, dp_peer, s4, r4)
    tot4 = total(ar4)
    for i in range(2):
        bias_sum = tot4[i : i + 1]
        gain_sum = tot4[2 + i : 3 + i] * rstd1[i]
        size = c_sizes[i]
        r = pl.ds(i * LANES, size)
        k1 = -scale1[i] * rstd1[i] * gain_sum / count
        k0 = -scale1[i] * bias_sum / count - k1 * mean1[i]
        col_a[r, :] = as_column(scale1[i], size)
        col_b[r, :] = as_column(k0, size)
        col_m[r, :] = as_column(k1, size)
        width = min(LANES, n_c - i * LANES)
        out_g1[0:1, i * LANES : i * LANES + width] = gain_sum[:, 0:width]
        out_b1[0:1, i * LANES : i * LANES + width] = bias_sum[:, 0:width]

    def last(g, c):
        base = g * 16 * rpc
        r = pl.ds(pl.multiple_of(g * 16, 16), 16)
        a, k0, k1, keep = col_a[r, :], col_b[r, :], col_m[r, :], col_k[r, :]
        for b in range(n_img):
            for t in range(tiles):
                sl = slice(t * LANES, (t + 1) * LANES)
                v = a * gp1[b, r, sl] + mask[b, :, sl] * (k0 + k1 * xb[b, r, sl].astype(F32))
                for h in range(2):
                    at = pl.ds(base + h * 8 * rpc + t * n_img + b, 8, stride=rpc)
                    out_g[at, :] = out_g[at, :] * keep[h * 8 : h * 8 + 8] + v[h * 8 : h * 8 + 8]
        return c

    lax.fori_loop(0, cp // 16, last, 0)

    @pl.when(is_owner)
    def _():
        def gave(k, c):
            remote(fin.at[my_part], fin.at[my_part], sa.at[k], ra.at[my_part], dp_peer(k)).wait_send()
            return c

        lax.fori_loop(1, n_dp, gave, 0)

    def take(q, c):
        @pl.when(q * stride != dp)
        def _():
            remote(fin.at[q], fin.at[q], sa.at[0], ra.at[q], {"dp": q * stride}).wait_recv()

        return c

    lax.fori_loop(0, OWNERS, take, 0)
    for q in range(OWNERS):
        r, h = q % 4, q // 4
        height = min(40, n_d - r * 40)
        width = min(LANES, n_c - h * LANES)
        out_w1[r * 40 : r * 40 + height, h * LANES : h * LANES + width] = fin[q, 0:height, 0:width]
    for q in range(20):
        lt, rt = q // 5, q % 5
        w2acc[rt * 8 : rt * 8 + 8, lt * LANES : (lt + 1) * LANES] = fin[
            q // 3, 40 + (q % 3) * 8 : 48 + (q % 3) * 8, :
        ]
    v = w2acc[0:40, :]
    for t in range(9):
        u = v if t == 0 else pltpu.roll(v, TAPS - t * TAP, 1)
        out_w2[t] = u[0:grow, 0:grow]


def finish(n_rows, *refs):
    n = (len(refs) - 1) // 2
    sem = refs[-1]
    copies = []
    for i in range(n):
        src, dst = refs[i], refs[n + i]
        if i < 2:
            src = src.at[pl.ds(0, n_rows)]
        copies.append(pltpu.make_async_copy(src, dst, sem.at[i]))
    for copy in copies:
        copy.start()
    for copy in copies:
        copy.wait()


def flat(values):
    n, c, p = values.shape
    return (
        values.transpose(1, 0, 2).reshape(c, n, p // LANES, LANES).transpose(0, 2, 1, 3).reshape(-1, LANES)
    )


def unflat(rows, n, c, p):
    return rows.reshape(c, p // LANES, n, LANES).transpose(0, 2, 1, 3).reshape(c, n, p).transpose(1, 0, 2)


def on_device(
    n_dp, n_ch, features, gain1, bias1, weight1, gain2, bias2, weight2, cotangent, image_side, block_slot
):
    n_img, n_c, n_px = features.shape
    n_d = weight1.shape[1]
    grow = weight2.shape[3]
    cp = pad_to(n_c, 16)
    dpad = pad_to(n_d, 16)
    d8 = pad_to(n_d, 8)
    rpc = n_px // LANES * n_img
    n_rows, n_pad = n_c * rpc, cp * rpc
    n_dev = n_dp * n_ch
    cfg = (n_dp, n_ch, n_img, n_c, n_px, n_d, grow)
    args = (
        flat(features),
        flat(cotangent),
        weight1.T,
        gain1.reshape(1, -1),
        bias1.reshape(1, -1),
        gain2.reshape(1, -1),
        bias2.reshape(1, -1),
        weight2.reshape(9, grow, grow),
        image_side,
        block_slot,
    )
    args = [pltpu.with_memory_space_constraint(v, pltpu.HBM) for v in args]
    sd = jax.ShapeDtypeStruct
    in_vmem = pl.BlockSpec(memory_space=pltpu.VMEM)
    in_hbm = pl.BlockSpec(memory_space=pltpu.HBM)
    dma = pltpu.SemaphoreType.DMA
    v = pltpu.VMEM
    scratch = [
        v((n_rows, LANES), BF16), v((n_rows, LANES), BF16), v((n_d, n_c), BF16),
        v((1, n_c), F32), v((1, n_c), F32), v((1, grow), F32), v((1, grow), F32),
        v((9, grow, grow), BF16), pltpu.SMEM(image_side.shape, jnp.int32), pltpu.SMEM(block_slot.shape, jnp.int32),
        v((n_img, 16, n_px), F32),
        v((n_img, cp, n_px), BF16), v((n_img, cp, n_px), BF16),
        v((n_img, cp, n_px), F32), v((n_img, cp, n_px), F32), v((cp, n_px), F32),
        v((cp, LANES), F32), v((cp, LANES), F32), v((cp, LANES), F32), v((cp, LANES), F32),
        v((7, dpad, LANES), F32), v((cp, LANES), F32), v((cp, LANES), F32), v((8, LANES), F32),
        v((dpad, cp), BF16), v((n_img, dpad, n_px), F32),
        v((dpad, n_px), F32), v((dpad, n_px), F32), v((dpad, n_px), F32), v((dpad, n_px), F32),
        v((TAP * rpc, LANES), F32), v((n_ch, TAP, n_px), BF16), v((n_ch, TAP, n_px), BF16),
        v((TAPS, n_px), BF16), v((TAP, TAPS), BF16), v((n_ch, TAP, TAPS), BF16), v((dpad, TAPS), BF16),
        v((n_ch, 2, LANES), F32),
        v((dpad, n_px), BF16), v((dpad, n_px), F32), v((dpad, n_px), F32), v((TAPS, n_px), F32),
        v((n_ch, 40, n_px), F32), v((TAP, n_px), F32), v((n_ch, dpad, n_px), BF16),
        v((OWNERS, 64, LANES), F32), v((n_ch, OWNERS, 24, LANES), F32), v((n_ch, OWNERS, 24, LANES), F32),
        v((n_dp, 64, LANES), F32), v((OWNERS, 64, LANES), F32), v((160, 256), F32), v((dpad, TAPS), F32),
        v((n_dp, 4, LANES), F32), v((n_dev, 4, LANES), F32), v((n_dev, 4, LANES), F32), v((n_dp, 4, LANES), F32),
        dma((10,)),
        dma((n_dp,)), dma((n_dp,)), dma((n_dev,)), dma((n_dev,)), dma((n_dev,)), dma((n_dev,)), dma((n_dp,)), dma((n_dp,)),
        dma((3,)), dma((3,)), dma((n_ch,)), dma((n_ch,)), dma((n_ch,)), dma((n_ch,)), dma((n_ch,)), dma((n_ch,)),
        dma((3,)), dma((3,)), dma((3,)), dma((3,)), dma((n_ch,)), dma((n_ch,)),
        dma((OWNERS,)), dma((n_dp,)), dma((n_dp,)), dma((OWNERS,)),
    ]
    out_shape = (
        sd((n_pad, LANES), F32), sd((n_pad, LANES), F32), sd((n_d, n_c), F32),
        sd((1, n_c), F32), sd((1, n_c), F32), sd((9, grow, grow), F32), sd((1, grow), F32), sd((1, grow), F32),
    )
    outs = pl.pallas_call(
        functools.partial(layer, cfg),
        out_shape=out_shape,
        in_specs=[in_hbm] * len(args),
        out_specs=(in_vmem,) * len(out_shape),
        scratch_shapes=scratch,
        compiler_params=pltpu.CompilerParams(
            collective_id=0, has_side_effects=True, vmem_limit_bytes=40 << 20
        ),
    )(*args)
    final = (sd((n_rows, LANES), F32),) * 2 + out_shape[2:]
    o = pl.pallas_call(
        functools.partial(finish, n_rows),
        out_shape=final,
        in_specs=[in_vmem] * len(final),
        out_specs=(in_hbm,) * len(final),
        scratch_shapes=[dma((len(final),))],
        compiler_params=pltpu.CompilerParams(vmem_limit_bytes=8 << 20),
    )(*outs)
    return (
        unflat(o[0], n_img, n_c, n_px),
        unflat(o[1], n_img, n_c, n_px),
        o[2].T,
        o[3].reshape(-1),
        o[4].reshape(-1),
        o[5].reshape(3, 3, grow, grow),
        o[6].reshape(-1),
        o[7].reshape(-1),
    )


def solution(mesh):
    in_specs = (
        P("dp", "chan", None),
        P("chan"),
        P("chan"),
        P("chan", None),
        P("chan"),
        P("chan"),
        P(None, None, "chan", None),
        P("dp", "chan", None),
        P("dp"),
        P(),
    )
    out_specs = (
        P("dp", "chan", None),
        P("dp", "chan", None),
        P("chan", None),
        P("chan"),
        P("chan"),
        P(None, None, "chan", None),
        P("chan"),
        P("chan"),
    )
    body = functools.partial(on_device, mesh.shape["dp"], mesh.shape["chan"])
    return jax.shard_map(body, mesh=mesh, in_specs=in_specs, out_specs=out_specs, check_vma=False)
```

time: 339 us -> 70.8 us (0.21); the launches traced: 334 us -> 70.4 us
  waiting for transfers between devices: 120 us -> 0 us
  blocking collectives: 99.9 us -> 0 us
  Pallas kernels: 0 us -> 69.7 us
  local copies, waits for them, and re-layouts: 47.3 us -> 0 us
  matrix products: 25.3 us -> 0 us
  other arithmetic: 23.6 us -> 0 us
  between operations: 17.2 us -> 0.64 us
    psum x4 -> x0, blocking collectives: 99.9 us -> none  [the longest x1 37.7 us: on_device(): lax.psum((weight_part, totals(grad_pre_one), totals(grad_pre_one * norm_o...]
    psum x3 -> x0, waiting for transfers between devices: 74.8 us -> none  [the longest x1 41.1 us: on_device(): lax.psum((weight_part, totals(grad_pre_one), totals(grad_pre_one * norm_o...]
    pallas_call x0 -> x2, Pallas kernels: none -> 69.7 us  [the longest x1 67.2 us: on_device(): pl.pallas_call(functools.partial(layer, cfg), out_shape=out_shape, in_spe...]
    unnamed x6 -> x0, waiting for transfers between devices: 45.2 us -> none
    dot_general x12 -> x0, matrix products: 20 us -> none  [the longest x9 11.4 us: kernel_grad(): jnp.einsum('bcij,bdij->cd', window_in, grad_squares, preferred_element_ty...]
    unnamed x48 -> x0, local copies, waits for them, and re-layouts: 18 us -> none
    reshape x10 -> x0, local copies, waits for them, and re-layouts: 17 us -> none  [the longest x4 10.8 us: conv_three(): return result.reshape(images, kernel.shape[3], SIDE * SIDE)]
    add x1 -> x0, other arithmetic: 6.54 us -> none  [on_device(): grad_features = cotangent.astype(jnp.float32) * keep + grad_inputs]
  transfers between devices with their start and end apart: 5 -> 0, of which waited for: 3 -> 0; matrix products, arithmetic and copies ran while one was open for 17% -> 0% of each run, Pallas kernels for 0% -> 0%
where the time goes in v1:
time: 70.8 us; the launch traced here: 70.4 us
  Pallas kernels  69.7 us (98%)
    pallas_call x1, Pallas kernels, on_device(): pl.pallas_call(functools.partial(layer, cfg), out_shape=out_shape, in_spe...  67.2 us
    pallas_call x1, Pallas kernels, on_device(): pl.pallas_call(functools.partial(finish, n_rows), out_shape=final, in_spe...  2.57 us

profile of v1, /device:TPU:0, one launch (start us, length us, event | category | flops | bytes accessed | tf_op | source)
XLA Modules:
  0.0 70.4 jit_solution(2728601010611411360)
XLA Ops:
  0.6 67.2 %shard_map.161 = (f32[5632,128]{1,0:T(8,128)S(1)}, f32[5632,128]{1,0:T(8,128)S(1)}, f32[132,165]{1,0:T(8,128)S(1)}, f32[1,165]{1,0:T(1,128)S(1)}, f32[1,165]{1,0...) custom-call(bf16[5280,128]{1,0:T(8,128)(2,1)} %bitcast.40, ...), custom_call_target="tpu_custom_call" | custom-call | tf_op jit(solution)/shard_map/pallas_call | solution.py:813
  67.8 2.6 %shard_map.162 = (f32[5280,128]{1,0:T(8,128)}, f32[5280,128]{1,0:T(8,128)}, f32[132,165]{1,0:T(8,128)}, f32[1,165]{1,0:T(1,128)}, f32[1,165]{1,0:T(1,128)}, /*in...) custom-call(f32[5632,128]{1,0:T(8,128)S(1)} %get-tuple-element.24.refs_0_, ...), custom_call_target="tpu_custom_call" | custom-call | tf_op jit(solution)/shard_map/pallas_call | solution.py:824

commit v2 on v1

--- a/solution.py
+++ b/solution.py
@@ -12,6 +12,7 @@
 LANES = 128
 TAP = 48
 TAPS = 512
+PIECES = 4
 OWNERS = 8
 
 MESH = pl.DeviceIdType.MESH
@@ -52,14 +53,14 @@
     feat_h, cot_h, w1_h, gain1_h, bias1_h, gain2_h, bias2_h, w2_h, side_h, slot_h,
     out_x, out_g, out_w1, out_g1, out_b1, out_w2, out_g2, out_b2,
     feat, cot, w1v, gain1v, bias1v, gain2v, bias2v, w2v, side, slot,
-    mask, xb, act, slope, gp1, gact,
+    mask, mask_raw, xb, act, slope, gp1, gact,
     col_a, col_b, col_m, col_k, col_c, sum_a, sum_b, rowbuf,
     w1s, part, rx_a, rx_b, rx_x, hid,
-    graw, gsend, grecv, g9, w2blk, w2r, w2b, gsl,
-    act2, gp2, back, zbuf, gall, gcur, gha,
-    cb, cw, cwr, rsl, fin, w1acc, w2acc,
+    graw, gsend, gsx, gpair, grx, gcur, g9, w2blk, w2r, w2b, gsl,
+    act2, gp2, back, zbuf, gall, gha,
+    cw, cwr, cwx, cb, rsl, fin, w1acc, w2acc,
     ar1, ar2, ar3, ar4,
-    load_sem, s1, r1, s2, r2, s3, r3, s4, r4, sx, rxs, sg, rg, sw, rw, sb, rb, sh, rh, so, ro, sc, rc, sr, rr, sa, ra,
+    load_sem, s1, r1, s2, r2, s3, r3, s4, r4, sx, rxs, sp, rp, sq, rq, sg, rg, sw, rw, sb, rb, sh, rh, so, ro, sc, rc, sr, rr, sa, ra,
 ):
     n_dp, n_ch, n_img, n_c, n_px, n_d, grow = cfg
     n_dev = n_dp * n_ch
@@ -201,27 +202,27 @@
     loads[6].wait()
     gsl[ch, 0:1, 0:grow] = gain2v[...]
     gsl[ch, 1:2, 0:grow] = bias2v[...]
+    w2r[ch] = w2blk[...]
+
+    pl.semaphore_wait(barrier, n_dev - 1)
+    share_start(ar1, dp, n_dp, dp_peer, s1, r1)
+    share_start(gsl, ch, n_ch, ch_peer, sb, rb)
+    share_start(w2r, ch, n_ch, ch_peer, sw, rw)
+
     loads[1].wait()
-
-    def widen_cot(i, c):
-        r = pl.ds(pl.multiple_of(i * step_rows, step_rows), step_rows)
-        out_g[r, :] = cot[r, :].astype(F32)
-        return c
-
-    lax.fori_loop(0, n_rows // step_rows, widen_cot, 0)
     graw[...] = jnp.zeros(graw.shape, F32)
-
     picks = [jnp.where(slot_of == ch * per_device + i, 1.0, 0.0) for i in range(per_device)]
 
     def pick(i, c):
         v = jnp.zeros((rpc, LANES), F32)
         for k in range(per_device):
-            v = v + out_g[pl.ds(pl.multiple_of((k * grow + i) * rpc, rpc), rpc), :] * picks[k]
+            v = v + cot[pl.ds(pl.multiple_of((k * grow + i) * rpc, rpc), rpc), :].astype(F32) * picks[k]
         graw[pl.ds(pl.multiple_of(i * rpc, rpc), rpc), :] = v
         return c
 
     lax.fori_loop(0, grow, pick, 0)
-    for b in range(n_img):
+
+    def by_image(b):
         for t in range(tiles):
             for h in range(TAP // 16):
                 v = jnp.concatenate(
@@ -234,14 +235,26 @@
                 v = v * mask[b, :, t * LANES : (t + 1) * LANES]
                 gsend[b, h * 16 : h * 16 + 16, t * LANES : (t + 1) * LANES] = v.astype(BF16)
 
-    pl.semaphore_wait(barrier, n_dev - 1)
-    share_start(ar1, dp, n_dp, dp_peer, s1, r1)
-    w2r[ch] = w2blk[...]
-    share_start(gsl, ch, n_ch, ch_peer, sb, rb)
-    for k in range(1, n_ch):
-        to = lax.rem(ch + k, n_ch)
-        remote(gsend.at[to], grecv.at[ch], sg.at[k], rg.at[k], {"chan": to}).start()
-    share_start(w2r, ch, n_ch, ch_peer, sw, rw)
+    by_image(sib)
+    by_image(xs)
+    g_sib = [
+        remote(gsend.at[sib], gsx.at[0], sg.at[0], rg.at[0], {"chan": sib}),
+        remote(gsend.at[xs], gsx.at[1], sg.at[1], rg.at[1], {"chan": sib}),
+    ]
+    for copy in g_sib:
+        copy.start()
+    by_image(ch)
+    by_image(xp)
+    for copy in g_sib:
+        copy.wait()
+    gpair[0] = (gsend[ch].astype(F32) + gsx[0].astype(F32)).astype(BF16)
+    gpair[1] = (gsend[xp].astype(F32) + gsx[1].astype(F32)).astype(BF16)
+    g_x = [
+        remote(gpair.at[0], grx.at[1], sg.at[2], rg.at[3], {"chan": xp}),
+        remote(gpair.at[1], grx.at[0], sg.at[3], rg.at[2], {"chan": xp}),
+    ]
+    for copy in g_x:
+        copy.start()
 
     loads[2].wait()
     w1s[...] = jnp.zeros(w1s.shape, BF16)
@@ -279,69 +292,76 @@
         rstd1.append(rstd)
         scale1.append(scale)
 
-    def partial(j):
+    def partial(j, first, n):
         def body(g, c):
             r = pl.ds(pl.multiple_of(g * 16, 16), 16)
             a, b = col_a[r, :], col_b[r, :]
-            for t in range(tiles):
+            for t in range(first, first + n):
                 sl = slice(t * LANES, (t + 1) * LANES)
                 v = xb[j, r, sl].astype(F32) * a + b
                 act[j, r, sl] = ((v * jnp.tanh(v) + v) * mask[j, :, sl]).astype(BF16)
             return c
 
         lax.fori_loop(0, cp // 16, body, 0)
-        part[j] = jnp.dot(w1s[...], act[j], preferred_element_type=F32)
+        sl = slice(first * LANES, (first + n) * LANES)
+        part[j, :, sl] = jnp.dot(w1s[...], act[j, :, sl], preferred_element_type=F32)
 
     rows_d = pl.ds(0, d8)
-    partial(xs)
-    to_sib_a = remote(part.at[xs, rows_d], rx_a.at[rows_d], sx.at[0], rxs.at[0], {"chan": sib})
-    to_sib_a.start()
-    partial(xp)
-    to_sib_a.wait()
-
-    def add_a(g, c):
-        r = pl.ds(pl.multiple_of(g * 8, 8), 8)
-        part[xp, r, :] = part[xp, r, :] + rx_a[r, :]
-        return c
-
-    lax.fori_loop(0, d8 // 8, add_a, 0)
-    to_x = remote(part.at[xp, rows_d], rx_x.at[rows_d], sx.at[1], rxs.at[1], {"chan": xp})
-    to_x.start()
-    partial(sib)
-    to_sib_b = remote(part.at[sib, rows_d], rx_b.at[rows_d], sx.at[2], rxs.at[2], {"chan": sib})
+    span = tiles // PIECES
+
+    def lanes_of(p):
+        return pl.ds(p * span * LANES, span * LANES)
+
+    to_x = []
+    for p in range(PIECES):
+        at = lanes_of(p)
+        partial(xs, p * span, span)
+        over = remote(part.at[xs, rows_d, at], rx_a.at[rows_d, at], sp.at[p], rp.at[p], {"chan": sib})
+        over.start()
+        partial(xp, p * span, span)
+        over.wait()
+
+        def add_a(g, c):
+            r = pl.ds(pl.multiple_of(g * 8, 8), 8)
+            part[xp, r, at] = part[xp, r, at] + rx_a[r, at]
+            return c
+
+        lax.fori_loop(0, d8 // 8, add_a, 0)
+        to_x.append(remote(part.at[xp, rows_d, at], rx_x.at[rows_d, at], sq.at[p], rq.at[p], {"chan": xp}))
+        to_x[p].start()
+    partial(sib, 0, tiles)
+    to_sib_b = remote(part.at[sib, rows_d], rx_b.at[rows_d], sx.at[0], rxs.at[0], {"chan": sib})
     to_sib_b.start()
-    partial(ch)
-
-    for k in range(1, n_ch):
-        to = lax.rem(ch + k, n_ch)
-        remote(gsend.at[to], grecv.at[ch], sg.at[k], rg.at[k], {"chan": to}).wait()
+    partial(ch, 0, tiles)
+
+    for copy in g_x:
+        copy.wait()
     share_wait(w2r, ch, n_ch, ch_peer, sw, rw)
     share_wait(gsl, ch, n_ch, ch_peer, sb, rb)
-    g = gsend[ch].astype(F32)
-    for k in range(1, n_ch):
-        g = g + grecv[lax.rem(ch + k, n_ch)].astype(F32)
-    gcur[...] = g
     px = iota((TAP, n_px), 1)
     py, pxx = px >> 5, px & (SIDE - 1)
-    for ky in range(3):
-        for kx in range(3):
-            shift = (ky - 1) * SIDE + (kx - 1)
-            t = ky * 3 + kx
-            v = gcur[...]
-            if shift != 0:
-                v = pltpu.roll(v, shift % n_px, 1)
-            ok = None
-            for off, pos in ((ky - 1, py), (kx - 1, pxx)):
-                if off == 1:
-                    test = pos >= 1
-                elif off == -1:
-                    test = pos <= SIDE - 2
-                else:
-                    continue
-                ok = test if ok is None else ok & test
-            if ok is not None:
-                v = jnp.where(ok, v, 0.0)
-            g9[t * TAP : (t + 1) * TAP, :] = v.astype(BF16)
+    for i in range(2):
+        gcur[...] = gpair[i].astype(F32) + grx[i].astype(F32)
+        for ky in range(3):
+            for kx in range(3):
+                shift = (ky - 1) * SIDE + (kx - 1)
+                t = ky * 3 + kx
+                v = gcur[...]
+                if shift != 0:
+                    v = pltpu.roll(v, shift % n_px, 1)
+                ok = None
+                for off, pos in ((ky - 1, py), (kx - 1, pxx)):
+                    if off == 1:
+                        test = pos >= 1
+                    elif off == -1:
+                        test = pos <= SIDE - 2
+                    else:
+                        continue
+                    ok = test if ok is None else ok & test
+                if ok is not None:
+                    v = jnp.where(ok, v, 0.0)
+                g9[i, t * TAP : (t + 1) * TAP, :] = v.astype(BF16)
+        g9[i, pl.ds(9 * TAP, TAPS - 9 * TAP), :] = jnp.zeros((TAPS - 9 * TAP, n_px), BF16)
     acc = jnp.zeros((dpad, w2b.shape[1]), F32)
     for j in range(n_ch):
         rows = iota((dpad, TAP), 0)
@@ -349,8 +369,8 @@
         place = jnp.where((rows == cols + j * grow) & (cols < grow), 1.0, 0.0).astype(BF16)
         acc = acc + jnp.dot(place, w2r[j], preferred_element_type=F32)
     w2b[...] = acc.astype(BF16)
-    g9[pl.ds(9 * TAP, TAPS - 9 * TAP), :] = jnp.zeros((TAPS - 9 * TAP, n_px), BF16)
-    back[...] = jnp.dot(w2b[...], g9[...], preferred_element_type=F32)
+    for i in range(2):
+        back[i] = jnp.dot(w2b[...], g9[i], preferred_element_type=F32)
     rows = iota((dpad, LANES), 0)
     cols = iota((dpad, LANES), 1)
     gain2c = jnp.zeros((dpad, 1), F32)
@@ -362,45 +382,6 @@
     col_c[0] = jnp.broadcast_to(gain2c, (dpad, LANES))
     col_c[1] = jnp.broadcast_to(bias2c, (dpad, LANES))
 
-    to_x.wait()
-    to_sib_b.wait()
-    sum_a[...] = jnp.zeros(sum_a.shape, F32)
-    sum_b[...] = jnp.zeros(sum_b.shape, F32)
-
-    def gather(g, c):
-        r = pl.ds(pl.multiple_of(g * 8, 8), 8)
-        s_acc = jnp.zeros((8, LANES), F32)
-        q_acc = jnp.zeros((8, LANES), F32)
-        for t in range(tiles):
-            sl = slice(t * LANES, (t + 1) * LANES)
-            v = (part[ch, r, sl] + rx_b[r, sl]) + rx_x[r, sl]
-            hid[r, sl] = v
-            s_acc = s_acc + v
-            q_acc = q_acc + v * v
-        sum_a[r, :] = s_acc
-        sum_b[r, :] = q_acc
-        return c
-
-    lax.fori_loop(0, d8 // 8, gather, 0)
-    hid[pl.ds(d8, dpad - d8), :] = jnp.zeros((dpad - d8, n_px), F32)
-    gp2[...] = jnp.zeros(gp2.shape, F32)
-
-    def pack(slots):
-        s, q = as_rows(sum_a[0:d8, :], d_sizes), as_rows(sum_b[0:d8, :], d_sizes)
-        slots[me, 0:1, :] = s[0]
-        slots[me, 1:2, :] = s[1]
-        slots[me, 2:3, :] = q[0]
-        slots[me, 3:4, :] = q[1]
-
-    def columns_d(row0, row1):
-        tail = jnp.zeros((dpad - d8, LANES), F32)
-        return jnp.concatenate(
-            [as_column(row0, LANES), as_column(row1, d8 - LANES), tail], axis=0
-        )
-
-    pack(ar2)
-    share_start(ar2, me, n_dev, dev_peer, s2, r2)
-
     def slopes(j):
         def body(g, c):
             r = pl.ds(pl.multiple_of(g * 16, 16), 16)
@@ -417,6 +398,61 @@
 
     for j in range(n_img):
         slopes(j)
+
+    def widen_cot(i, c):
+        r = pl.ds(pl.multiple_of(i * step_rows, step_rows), step_rows)
+        out_g[r, :] = cot[r, :].astype(F32)
+        return c
+
+    lax.fori_loop(0, n_rows // step_rows, widen_cot, 0)
+
+    to_sib_b.wait()
+    sum_a[...] = jnp.zeros(sum_a.shape, F32)
+    sum_b[...] = jnp.zeros(sum_b.shape, F32)
+    hid[:, d8:dpad, :] = jnp.zeros((2, dpad - d8, n_px), F32)
+    gp2[...] = jnp.zeros(gp2.shape, F32)
+
+    def across(p):
+        at = lanes_of(p)
+        return remote(hid.at[0, rows_d, at], hid.at[1, rows_d, at], sh.at[p], rh.at[p], {"chan": xp})
+
+    for p in range(PIECES):
+        to_x[p].wait()
+
+        def gather(g, c):
+            r = pl.ds(pl.multiple_of(g * 8, 8), 8)
+            s_acc, q_acc = sum_a[r, :], sum_b[r, :]
+            for t in range(p * span, (p + 1) * span):
+                sl = slice(t * LANES, (t + 1) * LANES)
+                v = (part[ch, r, sl] + rx_b[r, sl]) + rx_x[r, sl]
+                hid[0, r, sl] = v
+                s_acc = s_acc + v
+                q_acc = q_acc + v * v
+            sum_a[r, :] = s_acc
+            sum_b[r, :] = q_acc
+            return c
+
+        lax.fori_loop(0, d8 // 8, gather, 0)
+        if p == 0:
+            across(p).start()
+
+    def pack(slots):
+        s, q = as_rows(sum_a[0:d8, :], d_sizes), as_rows(sum_b[0:d8, :], d_sizes)
+        slots[me, 0:1, :] = s[0]
+        slots[me, 1:2, :] = s[1]
+        slots[me, 2:3, :] = q[0]
+        slots[me, 3:4, :] = q[1]
+
+    def columns_d(row0, row1):
+        tail = jnp.zeros((dpad - d8, LANES), F32)
+        return jnp.concatenate(
+            [as_column(row0, LANES), as_column(row1, d8 - LANES), tail], axis=0
+        )
+
+    pack(ar2)
+    share_start(ar2, me, n_dev, dev_peer, s2, r2)
+    for p in range(1, PIECES - 1):
+        across(p).start()
 
     share_wait(ar2, me, n_dev, dev_peer, s2, r2)
     tot2 = total(ar2)
@@ -438,13 +474,13 @@
         q_acc = jnp.zeros((16, LANES), F32)
         for t in range(tiles):
             sl = slice(t * LANES, (t + 1) * LANES)
-            h = hid[r, sl]
+            h = hid[0, r, sl]
             mk = mask[ch, :, sl]
             v = h * a + b
             th = jnp.tanh(v)
             act2[r, sl] = ((v * th + v) * mk).astype(BF16)
-            gp = (0.5 * mk) * ((1.0 + th) * (1.0 + v * (1.0 - th))) * back[r, sl]
-            gp2[r, sl] = gp
+            gp = (0.5 * mk) * ((1.0 + th) * (1.0 + v * (1.0 - th))) * back[0, r, sl]
+            gp2[0, r, sl] = gp
             s_acc = s_acc + gp
             q_acc = q_acc + gp * (h - m)
         sum_a[r, :] = s_acc
@@ -454,9 +490,10 @@
     lax.fori_loop(0, dpad // 16, second, 0)
     pack(ar3)
     share_start(ar3, me, n_dev, dev_peer, s3, r3)
+    across(PIECES - 1).start()
 
     w2acc[...] = lax.dot_general(
-        act2[...], g9[...], (((1,), (1,)), ((), ())), preferred_element_type=F32
+        act2[...], g9[0], (((1,), (1,)), ((), ())), preferred_element_type=F32
     )
     cw[...] = jnp.zeros(cw.shape, F32)
     for j in range(n_ch):
@@ -465,9 +502,38 @@
             cw[j, q // 3, (q % 3) * 8 : (q % 3) * 8 + 8, :] = w2acc[
                 j * grow + rt * 8 : j * grow + rt * 8 + 8, lt * LANES : (lt + 1) * LANES
             ]
-    for k in range(1, n_ch):
-        to = lax.rem(ch + k, n_ch)
-        remote(cw.at[to], cwr.at[ch], sc.at[k], rc.at[k], {"chan": to}).start()
+    w_sib = [
+        remote(cw.at[xs], cwr.at[1], sc.at[0], rc.at[0], {"chan": sib}),
+        remote(cw.at[sib], cwr.at[0], sc.at[1], rc.at[1], {"chan": sib}),
+    ]
+    for copy in w_sib:
+        copy.start()
+
+    def second_other(p):
+        def body(g, c):
+            r = pl.ds(pl.multiple_of(g * 16, 16), 16)
+            a, b = col_c[5, r, :], col_c[6, r, :]
+            for t in range(p * span, (p + 1) * span):
+                sl = slice(t * LANES, (t + 1) * LANES)
+                v = hid[1, r, sl] * a + b
+                th = jnp.tanh(v)
+                gp2[1, r, sl] = (
+                    (0.5 * mask[xp, :, sl]) * ((1.0 + th) * (1.0 + v * (1.0 - th))) * back[1, r, sl]
+                )
+            return c
+
+        lax.fori_loop(0, dpad // 16, body, 0)
+
+    for p in range(PIECES - 1):
+        across(p).wait()
+        second_other(p)
+    for copy in w_sib:
+        copy.wait()
+    cw[xp] = cw[xp] + cwr[1]
+    cw[ch] = cw[ch] + cwr[0]
+    w_x = remote(cw.at[xp], cwx, sc.at[2], rc.at[2], {"chan": xp})
+    w_x.start()
+
     zbuf[...] = lax.dot_general(
         w2b[...], act2[...], (((0,), (0,)), ((), ())), preferred_element_type=F32
     )
@@ -493,7 +559,14 @@
             new = new + v
     new = new * jnp.concatenate([mask[ch]] * (TAP // 16), axis=0)
     gall[ch] = new[0 : gall.shape[1]]
-
+    new_sib = remote(gall.at[ch], gall.at[ch], so.at[0], ro.at[0], {"chan": sib})
+    new_xp = remote(gall.at[ch], gall.at[ch], so.at[1], ro.at[1], {"chan": xp})
+    new_on = remote(gall.at[xp], gall.at[xp], so.at[2], ro.at[2], {"chan": sib})
+    new_xp.start()
+    new_sib.start()
+
+    across(PIECES - 1).wait()
+    second_other(PIECES - 1)
     share_wait(ar3, me, n_dev, dev_peer, s3, r3)
     tot3 = total(ar3)
     gain_sum2 = [tot3[2 + i : 3 + i] * rstd2[i] for i in range(2)]
@@ -503,30 +576,25 @@
     col_c[5] = col_c[4] * bias_sum2c / count
     col_c[6] = col_c[4] * col_c[3] * gain_sum2c / count
 
-    def third(g, c):
-        r = pl.ds(pl.multiple_of(g * 16, 16), 16)
-        c1, c2, c3, m = col_c[4, r, :], col_c[5, r, :], col_c[6, r, :], col_c[2, r, :]
-        for t in range(tiles):
-            sl = slice(t * LANES, (t + 1) * LANES)
-            gha[ch, r, sl] = (
-                c1 * gp2[r, sl] - mask[ch, :, sl] * (c2 + c3 * (hid[r, sl] - m))
-            ).astype(BF16)
-        return c
-
-    lax.fori_loop(0, dpad // 16, third, 0)
-
-    def spread(buf, send, recv):
-        to_sib = remote(buf.at[ch], buf.at[ch], send.at[0], recv.at[0], {"chan": sib})
-        to_xp = remote(buf.at[ch], buf.at[ch], send.at[1], recv.at[1], {"chan": xp})
-        on = remote(buf.at[xp], buf.at[xp], send.at[2], recv.at[2], {"chan": sib})
-        return to_sib, to_xp, on
-
-    grad_sib, grad_xp, grad_on = spread(gha, sh, rh)
-    grad_xp.start()
+    def third(i, j):
+        def body(g, c):
+            r = pl.ds(pl.multiple_of(g * 16, 16), 16)
+            c1, c2, c3, m = col_c[4, r, :], col_c[5, r, :], col_c[6, r, :], col_c[2, r, :]
+            for t in range(tiles):
+                sl = slice(t * LANES, (t + 1) * LANES)
+                gha[j, r, sl] = (
+                    c1 * gp2[i, r, sl] - mask[j, :, sl] * (c2 + c3 * (hid[i, r, sl] - m))
+                ).astype(BF16)
+            return c
+
+        lax.fori_loop(0, dpad // 16, body, 0)
+
+    third(0, ch)
+    grad_sib = remote(gha.at[ch], gha.at[ch], sx.at[1], rxs.at[1], {"chan": sib})
     grad_sib.start()
-    new_sib, new_xp, new_on = spread(gall, so, ro)
-    new_xp.start()
-    new_sib.start()
+    third(1, xp)
+    grad_xs = remote(gha.at[xp], gha.at[xp], sx.at[2], rxs.at[2], {"chan": sib})
+    grad_xs.start()
     d_rows, d_cols = iota((dpad, LANES), 0), iota((dpad, LANES), 1)
     here_d = (d_rows == d_cols + ch * grow) & (d_cols < grow)
     out_g2[...] = jnp.sum(jnp.where(here_d, gain_sum2c, 0.0), axis=0, keepdims=True)[:, 0:grow]
@@ -563,23 +631,13 @@
         lax.fori_loop(0, cp // 16, body, 0)
 
     weight_grad(ch)
-    input_grad(ch)
+    weight_grad(xp)
+    w_x.wait()
+    for q in range(OWNERS):
+        cb[q, 40:64, :] = cw[ch, q] + cwx[q]
     grad_sib.wait()
     weight_grad(sib)
-    input_grad(sib)
-    grad_xp.wait()
-    grad_on.start()
-    weight_grad(xp)
-    input_grad(xp)
-    for k in range(1, n_ch):
-        to = lax.rem(ch + k, n_ch)
-        remote(cw.at[to], cwr.at[ch], sc.at[k], rc.at[k], {"chan": to}).wait()
-    for q in range(OWNERS):
-        v = cw[ch, q]
-        for k in range(1, n_ch):
-            v = v + cwr[lax.rem(ch + k, n_ch), q]
-        cb[q, 40:64, :] = v
-    grad_on.wait()
+    grad_xs.wait()
     weight_grad(xs)
 
     for q in range(OWNERS):
@@ -603,12 +661,34 @@
         return c
 
     lax.fori_loop(0, OWNERS, push, 0)
-    input_grad(xs)
+    for j in range(n_img):
+        input_grad(j)
     s4_, q4_ = as_rows(sum_a[...], c_sizes), as_rows(sum_b[...], c_sizes)
     for i in range(2):
         ar4[dp, i : i + 1, :] = s4_[i]
         ar4[dp, 2 + i : 3 + i, :] = q4_[i]
     share_start(ar4, dp, n_dp, dp_peer, s4, r4)
+
+    for i in range(2):
+        col_a[pl.ds(i * LANES, c_sizes[i]), :] = as_column(scale1[i], c_sizes[i])
+        for b in range(n_img):
+            for t in range(tiles // 2):
+                u = i * (tiles // 2) + t
+                mask_raw[u * n_img + b : u * n_img + b + 1, :] = mask[b, 0:1, u * LANES : (u + 1) * LANES]
+
+    def direct(g, c):
+        base = g * 16 * rpc
+        r = pl.ds(pl.multiple_of(g * 16, 16), 16)
+        a, keep = col_a[r, :], col_k[r, :]
+        for b in range(n_img):
+            for t in range(tiles):
+                v = a * gp1[b, r, t * LANES : (t + 1) * LANES]
+                for h in range(2):
+                    at = pl.ds(base + h * 8 * rpc + t * n_img + b, 8, stride=rpc)
+                    out_g[at, :] = out_g[at, :] * keep[h * 8 : h * 8 + 8] + v[h * 8 : h * 8 + 8]
+        return c
+
+    lax.fori_loop(0, cp // 16, direct, 0)
 
     def push_wait(k, c):
         q, to = part_to(k)
@@ -670,27 +750,23 @@
         r = pl.ds(i * LANES, size)
         k1 = -scale1[i] * rstd1[i] * gain_sum / count
         k0 = -scale1[i] * bias_sum / count - k1 * mean1[i]
-        col_a[r, :] = as_column(scale1[i], size)
         col_b[r, :] = as_column(k0, size)
         col_m[r, :] = as_column(k1, size)
         width = min(LANES, n_c - i * LANES)
         out_g1[0:1, i * LANES : i * LANES + width] = gain_sum[:, 0:width]
         out_b1[0:1, i * LANES : i * LANES + width] = bias_sum[:, 0:width]
-
-    def last(g, c):
-        base = g * 16 * rpc
-        r = pl.ds(pl.multiple_of(g * 16, 16), 16)
-        a, k0, k1, keep = col_a[r, :], col_b[r, :], col_m[r, :], col_k[r, :]
-        for b in range(n_img):
-            for t in range(tiles):
-                sl = slice(t * LANES, (t + 1) * LANES)
-                v = a * gp1[b, r, sl] + mask[b, :, sl] * (k0 + k1 * xb[b, r, sl].astype(F32))
-                for h in range(2):
-                    at = pl.ds(base + h * 8 * rpc + t * n_img + b, 8, stride=rpc)
-                    out_g[at, :] = out_g[at, :] * keep[h * 8 : h * 8 + 8] + v[h * 8 : h * 8 + 8]
-        return c
-
-    lax.fori_loop(0, cp // 16, last, 0)
+    mask_of = mask_raw[...]
+
+    def last(i, c):
+        for k in range(5):
+            row = i * 5 + k
+            at = pl.ds(pl.multiple_of(row * rpc, rpc), rpc)
+            k0 = jnp.broadcast_to(col_b[pl.ds(row, 1), :], (rpc, LANES))
+            k1 = jnp.broadcast_to(col_m[pl.ds(row, 1), :], (rpc, LANES))
+            out_g[at, :] = out_g[at, :] + mask_of * (k0 + k1 * out_x[at, :])
+        return c
+
+    lax.fori_loop(0, n_c // 5, last, 0)
 
     @pl.when(is_owner)
     def _():
@@ -785,25 +861,28 @@
         v((n_rows, LANES), BF16), v((n_rows, LANES), BF16), v((n_d, n_c), BF16),
         v((1, n_c), F32), v((1, n_c), F32), v((1, grow), F32), v((1, grow), F32),
         v((9, grow, grow), BF16), pltpu.SMEM(image_side.shape, jnp.int32), pltpu.SMEM(block_slot.shape, jnp.int32),
-        v((n_img, 16, n_px), F32),
+        v((n_img, 16, n_px), F32), v((rpc, LANES), F32),
         v((n_img, cp, n_px), BF16), v((n_img, cp, n_px), BF16),
         v((n_img, cp, n_px), F32), v((n_img, cp, n_px), F32), v((cp, n_px), F32),
         v((cp, LANES), F32), v((cp, LANES), F32), v((cp, LANES), F32), v((cp, LANES), F32),
         v((7, dpad, LANES), F32), v((cp, LANES), F32), v((cp, LANES), F32), v((8, LANES), F32),
         v((dpad, cp), BF16), v((n_img, dpad, n_px), F32),
-        v((dpad, n_px), F32), v((dpad, n_px), F32), v((dpad, n_px), F32), v((dpad, n_px), F32),
-        v((TAP * rpc, LANES), F32), v((n_ch, TAP, n_px), BF16), v((n_ch, TAP, n_px), BF16),
-        v((TAPS, n_px), BF16), v((TAP, TAPS), BF16), v((n_ch, TAP, TAPS), BF16), v((dpad, TAPS), BF16),
+        v((dpad, n_px), F32), v((dpad, n_px), F32), v((dpad, n_px), F32), v((2, dpad, n_px), F32),
+        v((TAP * rpc, LANES), F32), v((n_ch, TAP, n_px), BF16),
+        v((2, TAP, n_px), BF16), v((2, TAP, n_px), BF16), v((2, TAP, n_px), BF16), v((TAP, n_px), F32),
+        v((2, TAPS, n_px), BF16), v((TAP, TAPS), BF16), v((n_ch, TAP, TAPS), BF16), v((dpad, TAPS), BF16),
         v((n_ch, 2, LANES), F32),
-        v((dpad, n_px), BF16), v((dpad, n_px), F32), v((dpad, n_px), F32), v((TAPS, n_px), F32),
-        v((n_ch, 40, n_px), F32), v((TAP, n_px), F32), v((n_ch, dpad, n_px), BF16),
-        v((OWNERS, 64, LANES), F32), v((n_ch, OWNERS, 24, LANES), F32), v((n_ch, OWNERS, 24, LANES), F32),
+        v((dpad, n_px), BF16), v((2, dpad, n_px), F32), v((2, dpad, n_px), F32), v((TAPS, n_px), F32),
+        v((n_ch, 40, n_px), F32), v((n_ch, dpad, n_px), BF16),
+        v((n_ch, OWNERS, 24, LANES), F32), v((2, OWNERS, 24, LANES), F32), v((OWNERS, 24, LANES), F32),
+        v((OWNERS, 64, LANES), F32),
         v((n_dp, 64, LANES), F32), v((OWNERS, 64, LANES), F32), v((160, 256), F32), v((dpad, TAPS), F32),
         v((n_dp, 4, LANES), F32), v((n_dev, 4, LANES), F32), v((n_dev, 4, LANES), F32), v((n_dp, 4, LANES), F32),
         dma((10,)),
         dma((n_dp,)), dma((n_dp,)), dma((n_dev,)), dma((n_dev,)), dma((n_dev,)), dma((n_dev,)), dma((n_dp,)), dma((n_dp,)),
-        dma((3,)), dma((3,)), dma((n_ch,)), dma((n_ch,)), dma((n_ch,)), dma((n_ch,)), dma((n_ch,)), dma((n_ch,)),
-        dma((3,)), dma((3,)), dma((3,)), dma((3,)), dma((n_ch,)), dma((n_ch,)),
+        dma((3,)), dma((3,)), dma((PIECES,)), dma((PIECES,)), dma((PIECES,)), dma((PIECES,)),
+        dma((4,)), dma((4,)), dma((n_ch,)), dma((n_ch,)), dma((n_ch,)), dma((n_ch,)),
+        dma((PIECES,)), dma((PIECES,)), dma((3,)), dma((3,)), dma((3,)), dma((3,)),
         dma((OWNERS,)), dma((n_dp,)), dma((n_dp,)), dma((OWNERS,)),
     ]
     out_shape = (

time: 70.8 us -> 63.6 us (0.90)
  Pallas kernels: 69.7 us -> 62.8 us
    pallas_call x1, Pallas kernels: 67.2 us -> 60.2 us  [on_device(): pl.pallas_call(functools.partial(layer, cfg), out_shape=out_shape, in_spe...]
where the time goes in v2:
time: 63.6 us; the launch traced here: 63.5 us
  Pallas kernels  62.8 us (99%)
  between operations  0.64 us (1%)
    pallas_call x1, Pallas kernels, on_device(): pl.pallas_call(functools.partial(layer, cfg), out_shape=out_shape, in_spe...  60.2 us
    pallas_call x1, Pallas kernels, on_device(): pl.pallas_call(functools.partial(finish, n_rows), out_shape=final, in_spe...  2.57 us

profile of v2, /device:TPU:0, one launch (start us, length us, event | category | flops | bytes accessed | tf_op | source)
XLA Modules:
  0.0 63.5 jit_solution(3736324017956222985)
XLA Ops:
  0.6 60.2 %shard_map.161 = (f32[5632,128]{1,0:T(8,128)S(1)}, f32[5632,128]{1,0:T(8,128)S(1)}, f32[132,165]{1,0:T(8,128)S(1)}, f32[1,165]{1,0:T(1,128)S(1)}, f32[1,165]{1,0...) custom-call(bf16[5280,128]{1,0:T(8,128)(2,1)} %bitcast.40, ...), custom_call_target="tpu_custom_call" | custom-call | tf_op jit(solution)/shard_map/pallas_call | solution.py:892
  60.9 2.6 %shard_map.162 = (f32[5280,128]{1,0:T(8,128)}, f32[5280,128]{1,0:T(8,128)}, f32[132,165]{1,0:T(8,128)}, f32[1,165]{1,0:T(1,128)}, f32[1,165]{1,0:T(1,128)}, /*in...) custom-call(f32[5632,128]{1,0:T(8,128)S(1)} %get-tuple-element.24.refs_0_, ...), custom_call_target="tpu_custom_call" | custom-call | tf_op jit(solution)/shard_map/pallas_call | solution.py:903

commit v3 on v2

--- a/solution.py
+++ b/solution.py
@@ -53,12 +53,12 @@
     feat_h, cot_h, w1_h, gain1_h, bias1_h, gain2_h, bias2_h, w2_h, side_h, slot_h,
     out_x, out_g, out_w1, out_g1, out_b1, out_w2, out_g2, out_b2,
     feat, cot, w1v, gain1v, bias1v, gain2v, bias2v, w2v, side, slot,
-    mask, mask_raw, xb, act, slope, gp1, gact,
+    mask, mask_raw, base, xb, act, slope, gp1, gact,
     col_a, col_b, col_m, col_k, col_c, sum_a, sum_b, rowbuf,
     w1s, part, rx_a, rx_b, rx_x, hid,
     graw, gsend, gsx, gpair, grx, gcur, g9, w2blk, w2r, w2b, gsl,
     act2, gp2, back, zbuf, gall, gha,
-    cw, cwr, cwx, cb, rsl, fin, w1acc, w2acc,
+    cw, cwr, cwx, cb, coded, rsl, fin, w1acc, w2acc,
     ar1, ar2, ar3, ar4,
     load_sem, s1, r1, s2, r2, s3, r3, s4, r4, sx, rxs, sp, rp, sq, rq, sg, rg, sw, rw, sb, rb, sh, rh, so, ro, sc, rc, sr, rr, sa, ra,
 ):
@@ -204,11 +204,6 @@
     gsl[ch, 1:2, 0:grow] = bias2v[...]
     w2r[ch] = w2blk[...]
 
-    pl.semaphore_wait(barrier, n_dev - 1)
-    share_start(ar1, dp, n_dp, dp_peer, s1, r1)
-    share_start(gsl, ch, n_ch, ch_peer, sb, rb)
-    share_start(w2r, ch, n_ch, ch_peer, sw, rw)
-
     loads[1].wait()
     graw[...] = jnp.zeros(graw.shape, F32)
     picks = [jnp.where(slot_of == ch * per_device + i, 1.0, 0.0) for i in range(per_device)]
@@ -237,14 +232,30 @@
 
     by_image(sib)
     by_image(xs)
+    loads[2].wait()
+    w1s[...] = jnp.zeros(w1s.shape, BF16)
+    w1s[0:n_d, 0:n_c] = w1v[...]
+    rowbuf[...] = jnp.zeros(rowbuf.shape, F32)
+    loads[3].wait()
+    loads[4].wait()
+    rowbuf[0:1, :] = gain1v[0:1, 0:LANES]
+    rowbuf[1:2, 0 : n_c - LANES] = gain1v[0:1, LANES:n_c]
+    rowbuf[2:3, :] = bias1v[0:1, 0:LANES]
+    rowbuf[3:4, 0 : n_c - LANES] = bias1v[0:1, LANES:n_c]
+
+    pl.semaphore_wait(barrier, n_dev - 1)
+    share_start(ar1, dp, n_dp, dp_peer, s1, r1)
+    share_start(gsl, ch, n_ch, ch_peer, sb, rb)
+    share_start(w2r, ch, n_ch, ch_peer, sw, rw)
+
+    by_image(ch)
+    by_image(xp)
     g_sib = [
         remote(gsend.at[sib], gsx.at[0], sg.at[0], rg.at[0], {"chan": sib}),
         remote(gsend.at[xs], gsx.at[1], sg.at[1], rg.at[1], {"chan": sib}),
     ]
     for copy in g_sib:
         copy.start()
-    by_image(ch)
-    by_image(xp)
     for copy in g_sib:
         copy.wait()
     gpair[0] = (gsend[ch].astype(F32) + gsx[0].astype(F32)).astype(BF16)
@@ -255,17 +266,6 @@
     ]
     for copy in g_x:
         copy.start()
-
-    loads[2].wait()
-    w1s[...] = jnp.zeros(w1s.shape, BF16)
-    w1s[0:n_d, 0:n_c] = w1v[...]
-    rowbuf[...] = jnp.zeros(rowbuf.shape, F32)
-    loads[3].wait()
-    loads[4].wait()
-    rowbuf[0:1, :] = gain1v[0:1, 0:LANES]
-    rowbuf[1:2, 0 : n_c - LANES] = gain1v[0:1, LANES:n_c]
-    rowbuf[2:3, :] = bias1v[0:1, 0:LANES]
-    rowbuf[3:4, 0 : n_c - LANES] = bias1v[0:1, LANES:n_c]
 
     share_wait(ar1, dp, n_dp, dp_peer, s1, r1)
     tot1 = total(ar1)
@@ -401,7 +401,8 @@
 
     def widen_cot(i, c):
         r = pl.ds(pl.multiple_of(i * step_rows, step_rows), step_rows)
-        out_g[r, :] = cot[r, :].astype(F32)
+        k = [jnp.broadcast_to(col_k[pl.ds(i * 3 + n, 1), :], (rpc, LANES)) for n in range(3)]
+        base[r, :] = cot[r, :].astype(F32) * jnp.concatenate(k, axis=0)
         return c
 
     lax.fori_loop(0, n_rows // step_rows, widen_cot, 0)
@@ -495,13 +496,12 @@
     w2acc[...] = lax.dot_general(
         act2[...], g9[0], (((1,), (1,)), ((), ())), preferred_element_type=F32
     )
-    cw[...] = jnp.zeros(cw.shape, F32)
     for j in range(n_ch):
-        for q in range(20):
-            lt, rt = q // 5, q % 5
-            cw[j, q // 3, (q % 3) * 8 : (q % 3) * 8 + 8, :] = w2acc[
-                j * grow + rt * 8 : j * grow + rt * 8 + 8, lt * LANES : (lt + 1) * LANES
-            ]
+        for lt in range(4):
+            sl = slice(lt * LANES, (lt + 1) * LANES)
+            cw[j, lt * 32 : lt * 32 + 32, :] = w2acc[j * grow : j * grow + 32, sl]
+            cw[j, 128 + lt : 129 + lt, :] = w2acc[j * grow + 32 : j * grow + 33, sl]
+        cw[j, 132:136, :] = jnp.zeros((4, LANES), F32)
     w_sib = [
         remote(cw.at[xs], cwr.at[1], sc.at[0], rc.at[0], {"chan": sib}),
         remote(cw.at[sib], cwr.at[0], sc.at[1], rc.at[1], {"chan": sib}),
@@ -524,15 +524,17 @@
 
         lax.fori_loop(0, dpad // 16, body, 0)
 
-    for p in range(PIECES - 1):
-        across(p).wait()
-        second_other(p)
+    across(0).wait()
+    second_other(0)
     for copy in w_sib:
         copy.wait()
     cw[xp] = cw[xp] + cwr[1]
     cw[ch] = cw[ch] + cwr[0]
     w_x = remote(cw.at[xp], cwx, sc.at[2], rc.at[2], {"chan": xp})
     w_x.start()
+    for p in range(1, PIECES - 1):
+        across(p).wait()
+        second_other(p)
 
     zbuf[...] = lax.dot_general(
         w2b[...], act2[...], (((0,), (0,)), ((), ())), preferred_element_type=F32
@@ -565,21 +567,19 @@
     new_xp.start()
     new_sib.start()
 
-    across(PIECES - 1).wait()
-    second_other(PIECES - 1)
     share_wait(ar3, me, n_dev, dev_peer, s3, r3)
     tot3 = total(ar3)
     gain_sum2 = [tot3[2 + i : 3 + i] * rstd2[i] for i in range(2)]
     bias_sum2 = [tot3[i : i + 1] for i in range(2)]
     gain_sum2c = columns_d(*gain_sum2)
     bias_sum2c = columns_d(*bias_sum2)
-    col_c[5] = col_c[4] * bias_sum2c / count
-    col_c[6] = col_c[4] * col_c[3] * gain_sum2c / count
+    col_c[7] = col_c[4] * bias_sum2c / count
+    col_c[8] = col_c[4] * col_c[3] * gain_sum2c / count
 
     def third(i, j):
         def body(g, c):
             r = pl.ds(pl.multiple_of(g * 16, 16), 16)
-            c1, c2, c3, m = col_c[4, r, :], col_c[5, r, :], col_c[6, r, :], col_c[2, r, :]
+            c1, c2, c3, m = col_c[4, r, :], col_c[7, r, :], col_c[8, r, :], col_c[2, r, :]
             for t in range(tiles):
                 sl = slice(t * LANES, (t + 1) * LANES)
                 gha[j, r, sl] = (
@@ -592,6 +592,8 @@
     third(0, ch)
     grad_sib = remote(gha.at[ch], gha.at[ch], sx.at[1], rxs.at[1], {"chan": sib})
     grad_sib.start()
+    across(PIECES - 1).wait()
+    second_other(PIECES - 1)
     third(1, xp)
     grad_xs = remote(gha.at[xp], gha.at[xp], sx.at[2], rxs.at[2], {"chan": sib})
     grad_xs.start()
@@ -633,16 +635,39 @@
     weight_grad(ch)
     weight_grad(xp)
     w_x.wait()
-    for q in range(OWNERS):
-        cb[q, 40:64, :] = cw[ch, q] + cwx[q]
     grad_sib.wait()
     weight_grad(sib)
+    input_grad(ch)
     grad_xs.wait()
     weight_grad(xs)
 
+    for r in range(17):
+        cb[r // 5, r % 5 * 8 : r % 5 * 8 + 8, :] = w1acc[r * 8 : r * 8 + 8, 0:LANES]
+    for k in range(6):
+        v = w1acc[k * 8 : k * 8 + 8, LANES : 2 * LANES]
+        for i in range(1, 3):
+            v = v + pltpu.roll(w1acc[i * 48 + k * 8 : i * 48 + k * 8 + 8, LANES : 2 * LANES], 40 * i, 1)
+        r = 17 + k
+        cb[r // 5, r % 5 * 8 : r % 5 * 8 + 8, :] = v
+    for k in range(17):
+        r = 23 + k
+        cb[r // 5, r % 5 * 8 : r % 5 * 8 + 8, :] = cw[ch, k * 8 : k * 8 + 8, :] + cwx[k * 8 : k * 8 + 8, :]
+
+    def encode(v):
+        top = jnp.maximum(jnp.max(jnp.abs(v), axis=0, keepdims=True), 1e-30)
+        power = jnp.floor(jnp.log2(top) + 1.0001)
+        q = jnp.clip(jnp.round(v * jnp.exp2(15.0 - power)), -32767.0, 32767.0).astype(jnp.int32)
+        low = jnp.concatenate([q[24:40], jnp.broadcast_to(power.astype(jnp.int32), (8, LANES))], axis=0)
+        return (q[0:24] << 16) | (low & 0xFFFF)
+
+    def decode(w):
+        high, low = w >> 16, (w << 16) >> 16
+        scale = jnp.exp2(low[16:24].astype(F32) - 15.0)
+        q = jnp.concatenate([high, low[0:16]], axis=0).astype(F32)
+        return q * jnp.concatenate([scale] * 5, axis=0)
+
     for q in range(OWNERS):
-        r, h = q % 4, q // 4
-        cb[q, 0:40, :] = w1acc[r * 40 : r * 40 + 40, h * LANES : (h + 1) * LANES]
+        coded[q] = encode(cb[q])
     stride = n_dp // OWNERS
     my_part = dp // stride
     is_owner = lax.rem(dp, stride) == 0
@@ -656,12 +681,12 @@
 
         @pl.when(to != dp)
         def _():
-            remote(cb.at[q], rsl.at[dp], sr.at[k], rr.at[dp], {"dp": to}).start()
+            remote(coded.at[q], rsl.at[dp], sr.at[k], rr.at[dp], {"dp": to}).start()
 
         return c
 
     lax.fori_loop(0, OWNERS, push, 0)
-    for j in range(n_img):
+    for j in (xp, sib, xs):
         input_grad(j)
     s4_, q4_ = as_rows(sum_a[...], c_sizes), as_rows(sum_b[...], c_sizes)
     for i in range(2):
@@ -669,56 +694,55 @@
         ar4[dp, 2 + i : 3 + i, :] = q4_[i]
     share_start(ar4, dp, n_dp, dp_peer, s4, r4)
 
+    def scatter(g, c):
+        first = g * 16 * rpc
+        r = pl.ds(pl.multiple_of(g * 16, 16), 16)
+        for b in range(n_img):
+            for t in range(tiles):
+                v = gp1[b, r, t * LANES : (t + 1) * LANES]
+                for h in range(2):
+                    at = pl.ds(first + h * 8 * rpc + t * n_img + b, 8, stride=rpc)
+                    out_g[at, :] = v[h * 8 : h * 8 + 8]
+        return c
+
+    lax.fori_loop(0, cp // 16, scatter, 0)
+
+    def push_wait(k, c):
+        q, to = part_to(k)
+
+        @pl.when(to != dp)
+        def _():
+            remote(coded.at[q], rsl.at[dp], sr.at[k], rr.at[dp], {"dp": to}).wait_send()
+
+        return c
+
+    def pull(k, c):
+        src = lax.rem(dp + k, n_dp)
+        remote(coded.at[0], rsl.at[src], sr.at[0], rr.at[src], {"dp": src}).wait_recv()
+        return c
+
+    @pl.when(is_owner)
+    def _():
+        lax.fori_loop(1, n_dp, pull, 0)
+        v = cb[my_part]
+        for k in range(1, n_dp):
+            v = v + decode(rsl[lax.rem(dp + k, n_dp)])
+        fin[my_part] = encode(v)
+
+        def give(k, c):
+            remote(fin.at[my_part], fin.at[my_part], sa.at[k], ra.at[my_part], dp_peer(k)).start()
+            return c
+
+        lax.fori_loop(1, n_dp, give, 0)
+
+    lax.fori_loop(0, OWNERS, push_wait, 0)
+
     for i in range(2):
         col_a[pl.ds(i * LANES, c_sizes[i]), :] = as_column(scale1[i], c_sizes[i])
         for b in range(n_img):
             for t in range(tiles // 2):
                 u = i * (tiles // 2) + t
                 mask_raw[u * n_img + b : u * n_img + b + 1, :] = mask[b, 0:1, u * LANES : (u + 1) * LANES]
-
-    def direct(g, c):
-        base = g * 16 * rpc
-        r = pl.ds(pl.multiple_of(g * 16, 16), 16)
-        a, keep = col_a[r, :], col_k[r, :]
-        for b in range(n_img):
-            for t in range(tiles):
-                v = a * gp1[b, r, t * LANES : (t + 1) * LANES]
-                for h in range(2):
-                    at = pl.ds(base + h * 8 * rpc + t * n_img + b, 8, stride=rpc)
-                    out_g[at, :] = out_g[at, :] * keep[h * 8 : h * 8 + 8] + v[h * 8 : h * 8 + 8]
-        return c
-
-    lax.fori_loop(0, cp // 16, direct, 0)
-
-    def push_wait(k, c):
-        q, to = part_to(k)
-
-        @pl.when(to != dp)
-        def _():
-            remote(cb.at[q], rsl.at[dp], sr.at[k], rr.at[dp], {"dp": to}).wait_send()
-
-        return c
-
-    def pull(k, c):
-        src = lax.rem(dp + k, n_dp)
-        remote(cb.at[0], rsl.at[src], sr.at[0], rr.at[src], {"dp": src}).wait_recv()
-        return c
-
-    @pl.when(is_owner)
-    def _():
-        lax.fori_loop(1, n_dp, pull, 0)
-        v = cb[my_part]
-        for k in range(1, n_dp):
-            v = v + rsl[lax.rem(dp + k, n_dp)]
-        fin[my_part] = v
-
-        def give(k, c):
-            remote(fin.at[my_part], fin.at[my_part], sa.at[k], ra.at[my_part], dp_peer(k)).start()
-            return c
-
-        lax.fori_loop(1, n_dp, give, 0)
-
-    lax.fori_loop(0, OWNERS, push_wait, 0)
 
     new_xp.wait()
     new_on.start()
@@ -763,7 +787,8 @@
             at = pl.ds(pl.multiple_of(row * rpc, rpc), rpc)
             k0 = jnp.broadcast_to(col_b[pl.ds(row, 1), :], (rpc, LANES))
             k1 = jnp.broadcast_to(col_m[pl.ds(row, 1), :], (rpc, LANES))
-            out_g[at, :] = out_g[at, :] + mask_of * (k0 + k1 * out_x[at, :])
+            a = jnp.broadcast_to(col_a[pl.ds(row, 1), :], (rpc, LANES))
+            out_g[at, :] = base[at, :] + a * out_g[at, :] + mask_of * (k0 + k1 * out_x[at, :])
         return c
 
     lax.fori_loop(0, n_c // 5, last, 0)
@@ -785,15 +810,27 @@
 
     lax.fori_loop(0, OWNERS, take, 0)
     for q in range(OWNERS):
-        r, h = q % 4, q // 4
-        height = min(40, n_d - r * 40)
-        width = min(LANES, n_c - h * LANES)
-        out_w1[r * 40 : r * 40 + height, h * LANES : h * LANES + width] = fin[q, 0:height, 0:width]
-    for q in range(20):
-        lt, rt = q // 5, q % 5
-        w2acc[rt * 8 : rt * 8 + 8, lt * LANES : (lt + 1) * LANES] = fin[
-            q // 3, 40 + (q % 3) * 8 : 48 + (q % 3) * 8, :
-        ]
+        cb[q] = decode(fin[q])
+    for r in range(17):
+        height = min(8, n_d - r * 8)
+        out_w1[r * 8 : r * 8 + height, 0:LANES] = cb[r // 5, r % 5 * 8 : r % 5 * 8 + height, :]
+    for k in range(6):
+        r = 17 + k
+        v = cb[r // 5, r % 5 * 8 : r % 5 * 8 + 8, :]
+        for i in range(3):
+            row = i * 48 + k * 8
+            height = min(8, n_d - row)
+            if height > 0:
+                u = v if i == 0 else pltpu.roll(v, LANES - 40 * i, 1)
+                out_w1[row : row + height, LANES:n_c] = u[0:height, 0 : n_c - LANES]
+    for k in range(17):
+        r = 23 + k
+        v = cb[r // 5, r % 5 * 8 : r % 5 * 8 + 8, :]
+        if k < 16:
+            w2acc[k % 4 * 8 : k % 4 * 8 + 8, k // 4 * LANES : (k // 4 + 1) * LANES] = v
+        else:
+            for lt in range(4):
+                w2acc[32:33, lt * LANES : (lt + 1) * LANES] = v[lt : lt + 1]
     v = w2acc[0:40, :]
     for t in range(9):
         u = v if t == 0 else pltpu.roll(v, TAPS - t * TAP, 1)
@@ -861,11 +898,11 @@
         v((n_rows, LANES), BF16), v((n_rows, LANES), BF16), v((n_d, n_c), BF16),
         v((1, n_c), F32), v((1, n_c), F32), v((1, grow), F32), v((1, grow), F32),
         v((9, grow, grow), BF16), pltpu.SMEM(image_side.shape, jnp.int32), pltpu.SMEM(block_slot.shape, jnp.int32),
-        v((n_img, 16, n_px), F32), v((rpc, LANES), F32),
+        v((n_img, 16, n_px), F32), v((rpc, LANES), F32), v((n_rows, LANES), F32),
         v((n_img, cp, n_px), BF16), v((n_img, cp, n_px), BF16),
         v((n_img, cp, n_px), F32), v((n_img, cp, n_px), F32), v((cp, n_px), F32),
         v((cp, LANES), F32), v((cp, LANES), F32), v((cp, LANES), F32), v((cp, LANES), F32),
-        v((7, dpad, LANES), F32), v((cp, LANES), F32), v((cp, LANES), F32), v((8, LANES), F32),
+        v((9, dpad, LANES), F32), v((cp, LANES), F32), v((cp, LANES), F32), v((8, LANES), F32),
         v((dpad, cp), BF16), v((n_img, dpad, n_px), F32),
         v((dpad, n_px), F32), v((dpad, n_px), F32), v((dpad, n_px), F32), v((2, dpad, n_px), F32),
         v((TAP * rpc, LANES), F32), v((n_ch, TAP, n_px), BF16),
@@ -874,9 +911,9 @@
         v((n_ch, 2, LANES), F32),
         v((dpad, n_px), BF16), v((2, dpad, n_px), F32), v((2, dpad, n_px), F32), v((TAPS, n_px), F32),
         v((n_ch, 40, n_px), F32), v((n_ch, dpad, n_px), BF16),
-        v((n_ch, OWNERS, 24, LANES), F32), v((2, OWNERS, 24, LANES), F32), v((OWNERS, 24, LANES), F32),
-        v((OWNERS, 64, LANES), F32),
-        v((n_dp, 64, LANES), F32), v((OWNERS, 64, LANES), F32), v((160, 256), F32), v((dpad, TAPS), F32),
+        v((n_ch, 136, LANES), F32), v((2, 136, LANES), F32), v((136, LANES), F32),
+        v((OWNERS, 40, LANES), F32), v((OWNERS, 24, LANES), jnp.int32),
+        v((n_dp, 24, LANES), jnp.int32), v((OWNERS, 24, LANES), jnp.int32), v((dpad, 256), F32), v((dpad, TAPS), F32),
         v((n_dp, 4, LANES), F32), v((n_dev, 4, LANES), F32), v((n_dev, 4, LANES), F32), v((n_dp, 4, LANES), F32),
         dma((10,)),
         dma((n_dp,)), dma((n_dp,)), dma((n_dev,)), dma((n_dev,)), dma((n_dev,)), dma((n_dev,)), dma((n_dp,)), dma((n_dp,)),

time: 63.6 us -> 59.8 us (0.940)
  Pallas kernels: 62.8 us -> 59 us
    pallas_call x1, Pallas kernels: 60.2 us -> 56.4 us  [on_device(): pl.pallas_call(functools.partial(layer, cfg), out_shape=out_shape, in_spe...]
where the time goes in v3:
time: 59.8 us; the launch traced here: 59.6 us
  Pallas kernels  59 us (99%)
  between operations  0.64 us (1%)
    pallas_call x1, Pallas kernels, on_device(): pl.pallas_call(functools.partial(layer, cfg), out_shape=out_shape, in_spe...  56.4 us
    pallas_call x1, Pallas kernels, on_device(): pl.pallas_call(functools.partial(finish, n_rows), out_shape=final, in_spe...  2.57 us

profile of v3, /device:TPU:0, one launch (start us, length us, event | category | flops | bytes accessed | tf_op | source)
XLA Modules:
  0.0 59.6 jit_solution(16256594624067177551)
XLA Ops:
  0.6 56.4 %shard_map.161 = (f32[5632,128]{1,0:T(8,128)S(1)}, f32[5632,128]{1,0:T(8,128)S(1)}, f32[132,165]{1,0:T(8,128)S(1)}, f32[1,165]{1,0:T(1,128)S(1)}, f32[1,165]{1,0...) custom-call(bf16[5280,128]{1,0:T(8,128)(2,1)} %bitcast.40, ...), custom_call_target="tpu_custom_call" | custom-call | tf_op jit(solution)/shard_map/pallas_call | solution.py:929
  57.0 2.6 %shard_map.162 = (f32[5280,128]{1,0:T(8,128)}, f32[5280,128]{1,0:T(8,128)}, f32[132,165]{1,0:T(8,128)}, f32[1,165]{1,0:T(1,128)}, f32[1,165]{1,0:T(1,128)}, /*in...) custom-call(f32[5632,128]{1,0:T(8,128)S(1)} %get-tuple-element.24.refs_0_, ...), custom_call_target="tpu_custom_call" | custom-call | tf_op jit(solution)/shard_map/pallas_call | solution.py:940

commit v4 on v3

--- a/solution.py
+++ b/solution.py
@@ -13,6 +13,7 @@
 TAP = 48
 TAPS = 512
 PIECES = 4
+LEVELS = 1048000.0
 OWNERS = 8
 
 MESH = pl.DeviceIdType.MESH
@@ -55,7 +56,8 @@
     feat, cot, w1v, gain1v, bias1v, gain2v, bias2v, w2v, side, slot,
     mask, mask_raw, base, xb, act, slope, gp1, gact,
     col_a, col_b, col_m, col_k, col_c, sum_a, sum_b, rowbuf,
-    w1s, part, rx_a, rx_b, rx_x, hid,
+    w1s, part, rx_a, rx_b, hid, row_top, row_scale, tops_h,
+    px_out, px_in, tx_out, tx_in, ph_out, ph_in, th_out, th_in,
     graw, gsend, gsx, gpair, grx, gcur, g9, w2blk, w2r, w2b, gsl,
     act2, gp2, back, zbuf, gall, gha,
     cw, cwr, cwx, cb, coded, rsl, fin, w1acc, w2acc,
@@ -312,6 +314,60 @@
     def lanes_of(p):
         return pl.ds(p * span * LANES, span * LANES)
 
+    def tiles_of(p):
+        return [slice(t * LANES, (t + 1) * LANES) for t in range(p * span, (p + 1) * span)]
+
+    blocks, rest = d8 // 24, d8 // 24 * 24
+
+    def code(read, p, words, tops):
+        top = jnp.maximum(jnp.max(row_top[...], axis=1, keepdims=True), 1e-30)
+        tops[p, 0:1, :] = as_row(top[0:LANES])
+        tops[p, 1:2, :] = as_row(top[LANES:d8])
+        row_scale[...] = jnp.broadcast_to(LEVELS / top, (d8, LANES))
+
+        def quantized(first, n, sl):
+            r = pl.ds(pl.multiple_of(first, 8), n)
+            return jnp.round(read(r, sl) * row_scale[r, :]).astype(jnp.int32)
+
+        def block(i, c):
+            for sl in tiles_of(p):
+                q0, q1, q2 = (quantized(i * 24 + k * 8, 8, sl) for k in range(3))
+                words[pl.ds(pl.multiple_of(i * 16, 8), 8), sl] = (q0 << 11) | ((q2 >> 10) & 0x7FF)
+                words[pl.ds(pl.multiple_of(i * 16 + 8, 8), 8), sl] = (q1 << 11) | (q2 & 0x3FF)
+            return c
+
+        lax.fori_loop(0, blocks, block, 0)
+        for sl in tiles_of(p):
+            words[blocks * 16 : blocks * 16 + d8 - rest, sl] = quantized(rest, d8 - rest, sl)
+
+    def unscale(tops, p):
+        top = jnp.concatenate([as_column(tops[p, 0:1, :], LANES), as_column(tops[p, 1:2, :], d8 - LANES)], axis=0)
+        row_scale[...] = top * (1.0 / LEVELS)
+
+    def uncode(write, p, words):
+        def put(first, n, sl, q):
+            r = pl.ds(pl.multiple_of(first, 8), n)
+            write(r, sl, q.astype(F32) * row_scale[r, :])
+
+        def block(i, c):
+            for sl in tiles_of(p):
+                w0 = words[pl.ds(pl.multiple_of(i * 16, 8), 8), sl]
+                w1 = words[pl.ds(pl.multiple_of(i * 16 + 8, 8), 8), sl]
+                put(i * 24, 8, sl, w0 >> 11)
+                put(i * 24 + 8, 8, sl, w1 >> 11)
+                put(i * 24 + 16, 8, sl, (((w0 << 21) >> 21) << 10) | (w1 & 0x3FF))
+            return c
+
+        lax.fori_loop(0, blocks, block, 0)
+        for sl in tiles_of(p):
+            put(rest, d8 - rest, sl, words[blocks * 16 : blocks * 16 + d8 - rest, sl])
+
+    def top_of(values):
+        value = jnp.abs(values[0])
+        for other in values[1:]:
+            value = jnp.maximum(value, jnp.abs(other))
+        return value
+
     to_x = []
     for p in range(PIECES):
         at = lanes_of(p)
@@ -323,12 +379,21 @@
 
         def add_a(g, c):
             r = pl.ds(pl.multiple_of(g * 8, 8), 8)
-            part[xp, r, at] = part[xp, r, at] + rx_a[r, at]
+            values = [part[xp, r, sl] + rx_a[r, sl] for sl in tiles_of(p)]
+            for sl, v in zip(tiles_of(p), values):
+                part[xp, r, sl] = v
+            row_top[r, :] = top_of(values)
             return c
 
         lax.fori_loop(0, d8 // 8, add_a, 0)
-        to_x.append(remote(part.at[xp, rows_d, at], rx_x.at[rows_d, at], sq.at[p], rq.at[p], {"chan": xp}))
-        to_x[p].start()
+        code(lambda r, sl: part[xp, r, sl], p, px_out, tx_out)
+        copies = [
+            remote(tx_out.at[p], tx_in.at[p], sq.at[0, p], rq.at[0, p], {"chan": xp}),
+            remote(px_out.at[:, at], px_in.at[:, at], sq.at[1, p], rq.at[1, p], {"chan": xp}),
+        ]
+        for copy in copies:
+            copy.start()
+        to_x.append(copies)
     partial(sib, 0, tiles)
     to_sib_b = remote(part.at[sib, rows_d], rx_b.at[rows_d], sx.at[0], rxs.at[0], {"chan": sib})
     to_sib_b.start()
@@ -415,27 +480,42 @@
 
     def across(p):
         at = lanes_of(p)
-        return remote(hid.at[0, rows_d, at], hid.at[1, rows_d, at], sh.at[p], rh.at[p], {"chan": xp})
+        return [
+            remote(th_out.at[p], th_in.at[p], sh.at[0, p], rh.at[0, p], {"chan": xp}),
+            remote(ph_out.at[:, at], ph_in.at[:, at], sh.at[1, p], rh.at[1, p], {"chan": xp}),
+        ]
+
+    def start_across(p):
+        for copy in across(p):
+            copy.start()
 
     for p in range(PIECES):
-        to_x[p].wait()
-
-        def gather(g, c):
+        for copy in to_x[p]:
+            copy.wait()
+        unscale(tx_in, p)
+
+        def gather(r, sl, v):
+            hid[0, r, sl] = (part[ch, r, sl] + rx_b[r, sl]) + v
+
+        uncode(gather, p, px_in)
+
+        def sums(g, c):
             r = pl.ds(pl.multiple_of(g * 8, 8), 8)
             s_acc, q_acc = sum_a[r, :], sum_b[r, :]
-            for t in range(p * span, (p + 1) * span):
-                sl = slice(t * LANES, (t + 1) * LANES)
-                v = (part[ch, r, sl] + rx_b[r, sl]) + rx_x[r, sl]
-                hid[0, r, sl] = v
+            values = [hid[0, r, sl] for sl in tiles_of(p)]
+            for v in values:
                 s_acc = s_acc + v
                 q_acc = q_acc + v * v
             sum_a[r, :] = s_acc
             sum_b[r, :] = q_acc
-            return c
-
-        lax.fori_loop(0, d8 // 8, gather, 0)
+            tops_h[p, r, :] = top_of(values)
+            return c
+
+        lax.fori_loop(0, d8 // 8, sums, 0)
         if p == 0:
-            across(p).start()
+            row_top[...] = tops_h[p]
+            code(lambda r, sl: hid[0, r, sl], p, ph_out, th_out)
+            start_across(p)
 
     def pack(slots):
         s, q = as_rows(sum_a[0:d8, :], d_sizes), as_rows(sum_b[0:d8, :], d_sizes)
@@ -452,8 +532,11 @@
 
     pack(ar2)
     share_start(ar2, me, n_dev, dev_peer, s2, r2)
-    for p in range(1, PIECES - 1):
-        across(p).start()
+    for p in range(1, PIECES):
+        row_top[...] = tops_h[p]
+        code(lambda r, sl: hid[0, r, sl], p, ph_out, th_out)
+        if p < PIECES - 1:
+            start_across(p)
 
     share_wait(ar2, me, n_dev, dev_peer, s2, r2)
     tot2 = total(ar2)
@@ -491,7 +574,7 @@
     lax.fori_loop(0, dpad // 16, second, 0)
     pack(ar3)
     share_start(ar3, me, n_dev, dev_peer, s3, r3)
-    across(PIECES - 1).start()
+    start_across(PIECES - 1)
 
     w2acc[...] = lax.dot_general(
         act2[...], g9[0], (((1,), (1,)), ((), ())), preferred_element_type=F32
@@ -510,6 +593,15 @@
         copy.start()
 
     def second_other(p):
+        for copy in across(p):
+            copy.wait()
+        unscale(th_in, p)
+
+        def keep_hidden(r, sl, v):
+            hid[1, r, sl] = v
+
+        uncode(keep_hidden, p, ph_in)
+
         def body(g, c):
             r = pl.ds(pl.multiple_of(g * 16, 16), 16)
             a, b = col_c[5, r, :], col_c[6, r, :]
@@ -524,7 +616,6 @@
 
         lax.fori_loop(0, dpad // 16, body, 0)
 
-    across(0).wait()
     second_other(0)
     for copy in w_sib:
         copy.wait()
@@ -533,7 +624,6 @@
     w_x = remote(cw.at[xp], cwx, sc.at[2], rc.at[2], {"chan": xp})
     w_x.start()
     for p in range(1, PIECES - 1):
-        across(p).wait()
         second_other(p)
 
     zbuf[...] = lax.dot_general(
@@ -592,7 +682,6 @@
     third(0, ch)
     grad_sib = remote(gha.at[ch], gha.at[ch], sx.at[1], rxs.at[1], {"chan": sib})
     grad_sib.start()
-    across(PIECES - 1).wait()
     second_other(PIECES - 1)
     third(1, xp)
     grad_xs = remote(gha.at[xp], gha.at[xp], sx.at[2], rxs.at[2], {"chan": sib})
@@ -875,6 +964,7 @@
     rpc = n_px // LANES * n_img
     n_rows, n_pad = n_c * rpc, cp * rpc
     n_dev = n_dp * n_ch
+    words = d8 // 24 * 16 + d8 % 24
     cfg = (n_dp, n_ch, n_img, n_c, n_px, n_d, grow)
     args = (
         flat(features),
@@ -904,7 +994,10 @@
         v((cp, LANES), F32), v((cp, LANES), F32), v((cp, LANES), F32), v((cp, LANES), F32),
         v((9, dpad, LANES), F32), v((cp, LANES), F32), v((cp, LANES), F32), v((8, LANES), F32),
         v((dpad, cp), BF16), v((n_img, dpad, n_px), F32),
-        v((dpad, n_px), F32), v((dpad, n_px), F32), v((dpad, n_px), F32), v((2, dpad, n_px), F32),
+        v((dpad, n_px), F32), v((dpad, n_px), F32), v((2, dpad, n_px), F32),
+        v((d8, LANES), F32), v((d8, LANES), F32), v((PIECES, d8, LANES), F32),
+        v((words, n_px), jnp.int32), v((words, n_px), jnp.int32), v((PIECES, 2, LANES), F32), v((PIECES, 2, LANES), F32),
+        v((words, n_px), jnp.int32), v((words, n_px), jnp.int32), v((PIECES, 2, LANES), F32), v((PIECES, 2, LANES), F32),
         v((TAP * rpc, LANES), F32), v((n_ch, TAP, n_px), BF16),
         v((2, TAP, n_px), BF16), v((2, TAP, n_px), BF16), v((2, TAP, n_px), BF16), v((TAP, n_px), F32),
         v((2, TAPS, n_px), BF16), v((TAP, TAPS), BF16), v((n_ch, TAP, TAPS), BF16), v((dpad, TAPS), BF16),
@@ -917,9 +1010,9 @@
         v((n_dp, 4, LANES), F32), v((n_dev, 4, LANES), F32), v((n_dev, 4, LANES), F32), v((n_dp, 4, LANES), F32),
         dma((10,)),
         dma((n_dp,)), dma((n_dp,)), dma((n_dev,)), dma((n_dev,)), dma((n_dev,)), dma((n_dev,)), dma((n_dp,)), dma((n_dp,)),
-        dma((3,)), dma((3,)), dma((PIECES,)), dma((PIECES,)), dma((PIECES,)), dma((PIECES,)),
+        dma((3,)), dma((3,)), dma((PIECES,)), dma((PIECES,)), dma((2, PIECES)), dma((2, PIECES)),
         dma((4,)), dma((4,)), dma((n_ch,)), dma((n_ch,)), dma((n_ch,)), dma((n_ch,)),
-        dma((PIECES,)), dma((PIECES,)), dma((3,)), dma((3,)), dma((3,)), dma((3,)),
+        dma((2, PIECES)), dma((2, PIECES)), dma((3,)), dma((3,)), dma((3,)), dma((3,)),
         dma((OWNERS,)), dma((n_dp,)), dma((n_dp,)), dma((OWNERS,)),
     ]
     out_shape = (

time: 59.8 us -> 54.7 us (0.915)
  Pallas kernels: 59 us -> 53.9 us
    pallas_call x1, Pallas kernels: 56.4 us -> 51.3 us  [on_device(): pl.pallas_call(functools.partial(layer, cfg), out_shape=out_shape, in_spe...]
where the time goes in v4:
time: 54.7 us; the launch traced here: 54.5 us
  Pallas kernels  53.9 us (99%)
  between operations  0.64 us (1%)
    pallas_call x1, Pallas kernels, on_device(): pl.pallas_call(functools.partial(layer, cfg), out_shape=out_shape, in_spe...  51.3 us
    pallas_call x1, Pallas kernels, on_device(): pl.pallas_call(functools.partial(finish, n_rows), out_shape=final, in_spe...  2.57 us

profile of v4, /device:TPU:0, one launch (start us, length us, event | category | flops | bytes accessed | tf_op | source)
XLA Modules:
  0.0 54.5 jit_solution(9979013296281010874)
XLA Ops:
  0.6 51.3 %shard_map.161 = (f32[5632,128]{1,0:T(8,128)S(1)}, f32[5632,128]{1,0:T(8,128)S(1)}, f32[132,165]{1,0:T(8,128)S(1)}, f32[1,165]{1,0:T(1,128)S(1)}, f32[1,165]{1,0...) custom-call(bf16[5280,128]{1,0:T(8,128)(2,1)} %bitcast.40, ...), custom_call_target="tpu_custom_call" | custom-call | tf_op jit(solution)/shard_map/pallas_call | solution.py:1022
  52.0 2.6 %shard_map.162 = (f32[5280,128]{1,0:T(8,128)}, f32[5280,128]{1,0:T(8,128)}, f32[132,165]{1,0:T(8,128)}, f32[1,165]{1,0:T(1,128)}, f32[1,165]{1,0:T(1,128)}, /*in...) custom-call(f32[5632,128]{1,0:T(8,128)S(1)} %get-tuple-element.24.refs_0_, ...), custom_call_target="tpu_custom_call" | custom-call | tf_op jit(solution)/shard_map/pallas_call | solution.py:1033

commit v5 on v4

--- a/solution.py
+++ b/solution.py
@@ -12,7 +12,9 @@
 LANES = 128
 TAP = 48
 TAPS = 512
-PIECES = 4
+SPANS = (1, 2, 3, 2)
+PIECES = len(SPANS)
+AHEAD = 2
 LEVELS = 1048000.0
 OWNERS = 8
 
@@ -52,17 +54,17 @@
 def layer(
     cfg,
     feat_h, cot_h, w1_h, gain1_h, bias1_h, gain2_h, bias2_h, w2_h, side_h, slot_h,
-    out_x, out_g, out_w1, out_g1, out_b1, out_w2, out_g2, out_b2,
+    out_x, out_g, out_w1, out_g1, out_b1, out_w2, out_g2, out_b2, out_new, out_slot,
     feat, cot, w1v, gain1v, bias1v, gain2v, bias2v, w2v, side, slot,
     mask, mask_raw, base, xb, act, slope, gp1, gact,
-    col_a, col_b, col_m, col_k, col_c, sum_a, sum_b, rowbuf,
+    col_a, col_b, col_m, col_k, col_c, sum_a, sum_b, sums_s, sums_q, rowbuf,
     w1s, part, rx_a, rx_b, hid, row_top, row_scale, tops_h,
     px_out, px_in, tx_out, tx_in, ph_out, ph_in, th_out, th_in,
     graw, gsend, gsx, gpair, grx, gcur, g9, w2blk, w2r, w2b, gsl,
     act2, gp2, back, zbuf, gall, gha,
     cw, cwr, cwx, cb, coded, rsl, fin, w1acc, w2acc,
     ar1, ar2, ar3, ar4,
-    load_sem, s1, r1, s2, r2, s3, r3, s4, r4, sx, rxs, sp, rp, sq, rq, sg, rg, sw, rw, sb, rb, sh, rh, so, ro, sc, rc, sr, rr, sa, ra,
+    load_sem, s1, r1, s2, r2, s3, r3, s4, r4, sx, rxs, sp, rp, sq, rq, sg, rg, sw, rw, sb, rb, sh, rh, st, rt, so, ro, sc, rc, sr, rr, sa, ra,
 ):
     n_dp, n_ch, n_img, n_c, n_px, n_d, grow = cfg
     n_dev = n_dp * n_ch
@@ -83,14 +85,26 @@
     xs = (1 - cx) * half + (1 - cc)
 
     def dev_peer(k):
-        q = lax.rem(me + k, n_dev)
+        q = me ^ k
         return {"dp": q // n_ch, "chan": lax.rem(q, n_ch)}
 
     def dp_peer(k):
-        return {"dp": lax.rem(dp + k, n_dp)}
+        return {"dp": dp ^ k}
 
     def ch_peer(k):
-        return {"chan": lax.rem(ch + k, n_ch)}
+        return {"chan": ch ^ k}
+
+    def far_first(count, step):
+        if count <= 32:
+            for k in range(count - 1, 0, -1):
+                step(k)
+        else:
+
+            def body(i, c):
+                step(count - 1 - i)
+                return c
+
+            lax.fori_loop(0, count - 1, body, 0)
 
     loads = [
         pltpu.make_async_copy(h, v, load_sem.at[i])
@@ -105,11 +119,10 @@
         copy.start()
     barrier = pltpu.get_barrier_semaphore()
 
-    def greet(k, c):
+    def greet(k):
         pl.semaphore_signal(barrier, inc=1, device_id=dev_peer(k), device_id_type=MESH)
-        return c
-
-    lax.fori_loop(1, n_dev, greet, 0)
+
+    far_first(n_dev, greet)
 
     def remote(src, dst, send, recv, device):
         return pltpu.make_async_remote_copy(
@@ -117,18 +130,16 @@
         )
 
     def share_start(slots, mine, count, peer, send, recv):
-        def step(k, c):
+        def step(k):
             remote(slots.at[mine], slots.at[mine], send.at[k], recv.at[k], peer(k)).start()
-            return c
-
-        lax.fori_loop(1, count, step, 0)
+
+        far_first(count, step)
 
     def share_wait(slots, mine, count, peer, send, recv):
-        def step(k, c):
+        def step(k):
             remote(slots.at[mine], slots.at[mine], send.at[k], recv.at[k], peer(k)).wait()
-            return c
-
-        lax.fori_loop(1, count, step, 0)
+
+        far_first(count, step)
 
     def total(slots):
         if slots.shape[0] <= 32:
@@ -140,56 +151,107 @@
 
     for copy in loads[8:]:
         copy.wait()
-    lane16 = iota((16, n_px), 1)
-    row_of, col_of = lane16 >> 5, lane16 & (SIDE - 1)
+    row_r, lane_r = iota((rpc, LANES), 0), iota((rpc, LANES), 1)
+    tile_of, image_of = row_r // n_img, row_r % n_img
     count_here = jnp.int32(0)
+    side_of = jnp.zeros((rpc, LANES), jnp.int32)
     for b in range(n_img):
-        s = side[b]
-        count_here = count_here + s * s
-        mask[b] = jnp.where((row_of < s) & (col_of < s), 1.0, 0.0)
-    new_slot = slot[slot.shape[0] - 1]
-    per_device = n_c // grow
-    slot_of = iota((rpc, LANES), 0) * 0 + new_slot
-
+        count_here = count_here + side[b] * side[b]
+        side_of = jnp.where(image_of == b, side[b], side_of)
+    pixel_of = tile_of * LANES + lane_r
+    mask_raw[...] = jnp.where((pixel_of // SIDE < side_of) & (pixel_of % SIDE < side_of), 1.0, 0.0)
+    mask_of = mask_raw[...]
     n_rows = feat.shape[0]
-    out_x[pl.ds(n_rows, out_x.shape[0] - n_rows), :] = jnp.zeros((out_x.shape[0] - n_rows, LANES), F32)
-    out_g[pl.ds(n_rows, out_g.shape[0] - n_rows), :] = jnp.zeros((out_g.shape[0] - n_rows, LANES), F32)
-    step_rows = 3 * rpc
     loads[0].wait()
 
-    def widen(i, c):
-        r = pl.ds(pl.multiple_of(i * step_rows, step_rows), step_rows)
-        out_x[r, :] = feat[r, :].astype(F32)
-        return c
-
-    lax.fori_loop(0, n_rows // step_rows, widen, 0)
-
-    def relayout(g, c):
-        base = g * 16 * rpc
-        r = pl.ds(pl.multiple_of(g * 16, 16), 16)
-        s_acc = jnp.zeros((16, LANES), F32)
-        q_acc = jnp.zeros((16, LANES), F32)
-        for b in range(n_img):
-            for t in range(tiles):
-                k = t * n_img + b
-                v = jnp.concatenate(
-                    [out_x[pl.ds(base + h * 8 * rpc + k, 8, stride=rpc), :] for h in range(2)], axis=0
-                )
-                w = v * mask[b, :, t * LANES : (t + 1) * LANES]
-                s_acc = s_acc + w
-                q_acc = q_acc + w * v
-                xb[b, r, t * LANES : (t + 1) * LANES] = v.astype(BF16)
-        sum_a[r, :] = s_acc
-        sum_b[r, :] = q_acc
-        return c
-
-    lax.fori_loop(0, cp // 16, relayout, 0)
+    def halves(v):
+        while v.shape[0] > 8:
+            n = v.shape[0] // 2
+            v = v[0:n] + v[n:]
+        return v
+
+    def first_sums(i, c):
+        for k in range(5):
+            row = i * 5 + k
+            v = feat[pl.ds(pl.multiple_of(row * rpc, rpc), rpc), :].astype(F32)
+            w = v * mask_of
+            at = pl.ds(pl.multiple_of(row * 8, 8), 8)
+            sums_s[at, :] = halves(w)
+            sums_q[at, :] = halves(w * v)
+        return c
+
+    lax.fori_loop(0, n_c // 5, first_sums, 0)
+    sums_s[n_c * 8 : cp * 8, :] = jnp.zeros(((cp - n_c) * 8, LANES), F32)
+    sums_q[n_c * 8 : cp * 8, :] = jnp.zeros(((cp - n_c) * 8, LANES), F32)
+
+    def first_fold(g, c):
+        for src, dst in ((sums_s, sum_a), (sums_q, sum_b)):
+            v = src[pl.ds(g * 64, 8, stride=8), :]
+            for k in range(1, 8):
+                v = v + src[pl.ds(g * 64 + k, 8, stride=8), :]
+            dst[pl.ds(pl.multiple_of(g * 8, 8), 8), :] = v
+        return c
+
+    lax.fori_loop(0, cp // 8, first_fold, 0)
     lane1 = iota((1, LANES), 1)
     s0, sq0 = as_rows(sum_a[...], c_sizes), as_rows(sum_b[...], c_sizes)
     ar1[dp, 0:1, :] = s0[0]
     ar1[dp, 1:2, :] = jnp.where(lane1 == LANES - 1, count_here.astype(F32), s0[1])
     ar1[dp, 2:3, :] = sq0[0]
     ar1[dp, 3:4, :] = sq0[1]
+
+    pl.semaphore_wait(barrier, n_dev - 1)
+    share_start(ar1, dp, n_dp, dp_peer, s1, r1)
+
+    new_slot = slot[slot.shape[0] - 1]
+    per_device = n_c // grow
+    slot_of = iota((rpc, LANES), 0) * 0 + new_slot
+    loads[1].wait()
+    graw[grow * rpc : TAP * rpc, :] = jnp.zeros(((TAP - grow) * rpc, LANES), F32)
+    picks = [jnp.where(slot_of == ch * per_device + i, mask_of, 0.0) for i in range(per_device)]
+
+    def pick(i, c):
+        v = jnp.zeros((rpc, LANES), F32)
+        for k in range(per_device):
+            v = v + cot[pl.ds(pl.multiple_of((k * grow + i) * rpc, rpc), rpc), :].astype(F32) * picks[k]
+        graw[pl.ds(pl.multiple_of(i * rpc, rpc), rpc), :] = v
+        return c
+
+    lax.fori_loop(0, grow, pick, 0)
+
+    def by_image(b):
+        for t in range(tiles):
+            for h in range(TAP // 16):
+                v = jnp.concatenate(
+                    [
+                        graw[pl.ds((h * 16 + i * 8) * rpc + t * n_img + b, 8, stride=rpc), :]
+                        for i in range(2)
+                    ],
+                    axis=0,
+                )
+                gsend[b, h * 16 : h * 16 + 16, t * LANES : (t + 1) * LANES] = v.astype(BF16)
+
+    by_image(sib)
+    by_image(xs)
+    g_sib = [
+        remote(gsend.at[sib], gsx.at[0], sg.at[0], rg.at[0], {"chan": sib}),
+        remote(gsend.at[xs], gsx.at[1], sg.at[1], rg.at[1], {"chan": sib}),
+    ]
+    for copy in g_sib:
+        copy.start()
+    by_image(ch)
+    by_image(xp)
+
+    for copy in g_sib:
+        copy.wait()
+    gpair[0] = (gsend[ch].astype(F32) + gsx[0].astype(F32)).astype(BF16)
+    gpair[1] = (gsend[xp].astype(F32) + gsx[1].astype(F32)).astype(BF16)
+    g_x = [
+        remote(gpair.at[0], grx.at[1], sg.at[2], rg.at[3], {"chan": xp}),
+        remote(gpair.at[1], grx.at[0], sg.at[3], rg.at[2], {"chan": xp}),
+    ]
+    for copy in g_x:
+        copy.start()
 
     loads[7].wait()
     w2blk[...] = jnp.zeros(w2blk.shape, BF16)
@@ -206,34 +268,42 @@
     gsl[ch, 1:2, 0:grow] = bias2v[...]
     w2r[ch] = w2blk[...]
 
-    loads[1].wait()
-    graw[...] = jnp.zeros(graw.shape, F32)
-    picks = [jnp.where(slot_of == ch * per_device + i, 1.0, 0.0) for i in range(per_device)]
-
-    def pick(i, c):
-        v = jnp.zeros((rpc, LANES), F32)
-        for k in range(per_device):
-            v = v + cot[pl.ds(pl.multiple_of((k * grow + i) * rpc, rpc), rpc), :].astype(F32) * picks[k]
-        graw[pl.ds(pl.multiple_of(i * rpc, rpc), rpc), :] = v
-        return c
-
-    lax.fori_loop(0, grow, pick, 0)
-
-    def by_image(b):
-        for t in range(tiles):
-            for h in range(TAP // 16):
+    w_near = remote(w2r.at[ch], w2r.at[ch], sw.at[0], rw.at[0], {"chan": sib})
+    w_far = remote(w2r.at[ch], w2r.at[ch], sw.at[1], rw.at[1], {"chan": xp})
+    w_on = remote(w2r.at[xp], w2r.at[xp], sw.at[2], rw.at[2], {"chan": sib})
+    w_far.start()
+    w_near.start()
+    share_start(gsl, ch, n_ch, ch_peer, sb, rb)
+
+    lane16 = iota((16, n_px), 1)
+    row_of, col_of = lane16 >> 5, lane16 & (SIDE - 1)
+    for b in range(n_img):
+        mask[b] = jnp.where((row_of < side[b]) & (col_of < side[b]), 1.0, 0.0)
+
+    out_x[pl.ds(n_rows, out_x.shape[0] - n_rows), :] = jnp.zeros((out_x.shape[0] - n_rows, LANES), F32)
+    out_g[pl.ds(n_rows, out_g.shape[0] - n_rows), :] = jnp.zeros((out_g.shape[0] - n_rows, LANES), F32)
+    step_rows = 3 * rpc
+
+    def widen(i, c):
+        r = pl.ds(pl.multiple_of(i * step_rows, step_rows), step_rows)
+        out_x[r, :] = feat[r, :].astype(F32)
+        return c
+
+    lax.fori_loop(0, n_rows // step_rows, widen, 0)
+
+    def relayout(g, c):
+        base_row = g * 16 * rpc
+        r = pl.ds(pl.multiple_of(g * 16, 16), 16)
+        for b in range(n_img):
+            for t in range(tiles):
+                k = t * n_img + b
                 v = jnp.concatenate(
-                    [
-                        graw[pl.ds((h * 16 + i * 8) * rpc + t * n_img + b, 8, stride=rpc), :]
-                        for i in range(2)
-                    ],
-                    axis=0,
+                    [out_x[pl.ds(base_row + h * 8 * rpc + k, 8, stride=rpc), :] for h in range(2)], axis=0
                 )
-                v = v * mask[b, :, t * LANES : (t + 1) * LANES]
-                gsend[b, h * 16 : h * 16 + 16, t * LANES : (t + 1) * LANES] = v.astype(BF16)
-
-    by_image(sib)
-    by_image(xs)
+                xb[b, r, t * LANES : (t + 1) * LANES] = v.astype(BF16)
+        return c
+
+    lax.fori_loop(0, cp // 16, relayout, 0)
     loads[2].wait()
     w1s[...] = jnp.zeros(w1s.shape, BF16)
     w1s[0:n_d, 0:n_c] = w1v[...]
@@ -245,34 +315,11 @@
     rowbuf[2:3, :] = bias1v[0:1, 0:LANES]
     rowbuf[3:4, 0 : n_c - LANES] = bias1v[0:1, LANES:n_c]
 
-    pl.semaphore_wait(barrier, n_dev - 1)
-    share_start(ar1, dp, n_dp, dp_peer, s1, r1)
-    share_start(gsl, ch, n_ch, ch_peer, sb, rb)
-    share_start(w2r, ch, n_ch, ch_peer, sw, rw)
-
-    by_image(ch)
-    by_image(xp)
-    g_sib = [
-        remote(gsend.at[sib], gsx.at[0], sg.at[0], rg.at[0], {"chan": sib}),
-        remote(gsend.at[xs], gsx.at[1], sg.at[1], rg.at[1], {"chan": sib}),
-    ]
-    for copy in g_sib:
-        copy.start()
-    for copy in g_sib:
-        copy.wait()
-    gpair[0] = (gsend[ch].astype(F32) + gsx[0].astype(F32)).astype(BF16)
-    gpair[1] = (gsend[xp].astype(F32) + gsx[1].astype(F32)).astype(BF16)
-    g_x = [
-        remote(gpair.at[0], grx.at[1], sg.at[2], rg.at[3], {"chan": xp}),
-        remote(gpair.at[1], grx.at[0], sg.at[3], rg.at[2], {"chan": xp}),
-    ]
-    for copy in g_x:
-        copy.start()
 
     share_wait(ar1, dp, n_dp, dp_peer, s1, r1)
     tot1 = total(ar1)
     count = tot1[1:2, LANES - 1 : LANES]
-    mean1, rstd1, scale1 = [], [], []
+    mean1, rstd1, scale1, keep1 = [], [], [], []
     for i in range(2):
         mean = tot1[i : i + 1] / count
         rstd = lax.rsqrt(tot1[2 + i : 3 + i] / count - mean * mean + EPS)
@@ -288,9 +335,8 @@
         r = pl.ds(i * LANES, size)
         col_a[r, :] = as_column(0.5 * scale * keep, size)
         col_b[r, :] = as_column(0.5 * shift * keep, size)
-        col_m[r, :] = as_column(mean, size)
-        col_k[r, :] = as_column(keep, size)
         mean1.append(mean)
+        keep1.append(keep)
         rstd1.append(rstd)
         scale1.append(scale)
 
@@ -309,13 +355,14 @@
         part[j, :, sl] = jnp.dot(w1s[...], act[j, :, sl], preferred_element_type=F32)
 
     rows_d = pl.ds(0, d8)
-    span = tiles // PIECES
+    unit = tiles // sum(SPANS)
+    edges = [sum(SPANS[:p]) * unit for p in range(PIECES + 1)]
 
     def lanes_of(p):
-        return pl.ds(p * span * LANES, span * LANES)
+        return pl.ds(edges[p] * LANES, (edges[p + 1] - edges[p]) * LANES)
 
     def tiles_of(p):
-        return [slice(t * LANES, (t + 1) * LANES) for t in range(p * span, (p + 1) * span)]
+        return [slice(t * LANES, (t + 1) * LANES) for t in range(edges[p], edges[p + 1])]
 
     blocks, rest = d8 // 24, d8 // 24 * 24
 
@@ -368,14 +415,22 @@
             value = jnp.maximum(value, jnp.abs(other))
         return value
 
+    def piece_of(j, p):
+        partial(j, edges[p], edges[p + 1] - edges[p])
+
+    def over(p):
+        at = lanes_of(p)
+        return remote(part.at[xs, rows_d, at], rx_a.at[rows_d, at], sp.at[p], rp.at[p], {"chan": sib})
+
     to_x = []
+    piece_of(xs, 0)
+    over(0).start()
+    piece_of(xp, 0)
     for p in range(PIECES):
-        at = lanes_of(p)
-        partial(xs, p * span, span)
-        over = remote(part.at[xs, rows_d, at], rx_a.at[rows_d, at], sp.at[p], rp.at[p], {"chan": sib})
-        over.start()
-        partial(xp, p * span, span)
-        over.wait()
+        if p + 1 < PIECES:
+            piece_of(xs, p + 1)
+            over(p + 1).start()
+        over(p).wait()
 
         def add_a(g, c):
             r = pl.ds(pl.multiple_of(g * 8, 8), 8)
@@ -387,6 +442,7 @@
 
         lax.fori_loop(0, d8 // 8, add_a, 0)
         code(lambda r, sl: part[xp, r, sl], p, px_out, tx_out)
+        at = lanes_of(p)
         copies = [
             remote(tx_out.at[p], tx_in.at[p], sq.at[0, p], rq.at[0, p], {"chan": xp}),
             remote(px_out.at[:, at], px_in.at[:, at], sq.at[1, p], rq.at[1, p], {"chan": xp}),
@@ -394,6 +450,14 @@
         for copy in copies:
             copy.start()
         to_x.append(copies)
+        if p + 1 < PIECES:
+            piece_of(xp, p + 1)
+    for i in range(2):
+        r = pl.ds(i * LANES, c_sizes[i])
+        col_m[r, :] = as_column(mean1[i], c_sizes[i])
+        col_k[r, :] = as_column(keep1[i], c_sizes[i])
+    w_far.wait()
+    w_on.start()
     partial(sib, 0, tiles)
     to_sib_b = remote(part.at[sib, rows_d], rx_b.at[rows_d], sx.at[0], rxs.at[0], {"chan": sib})
     to_sib_b.start()
@@ -401,7 +465,8 @@
 
     for copy in g_x:
         copy.wait()
-    share_wait(w2r, ch, n_ch, ch_peer, sw, rw)
+    w_near.wait()
+    w_on.wait()
     share_wait(gsl, ch, n_ch, ch_peer, sb, rb)
     px = iota((TAP, n_px), 1)
     py, pxx = px >> 5, px & (SIDE - 1)
@@ -447,6 +512,71 @@
     col_c[0] = jnp.broadcast_to(gain2c, (dpad, LANES))
     col_c[1] = jnp.broadcast_to(bias2c, (dpad, LANES))
 
+    to_sib_b.wait()
+    sum_a[...] = jnp.zeros(sum_a.shape, F32)
+    sum_b[...] = jnp.zeros(sum_b.shape, F32)
+    hid[:, d8:dpad, :] = jnp.zeros((2, dpad - d8, n_px), F32)
+    gp2[...] = jnp.zeros(gp2.shape, F32)
+
+    def across(p):
+        at = lanes_of(p)
+        return [
+            remote(th_out.at[p], th_in.at[p], sh.at[0, p], rh.at[0, p], {"chan": xp}),
+            remote(ph_out.at[:, at], ph_in.at[:, at], sh.at[1, p], rh.at[1, p], {"chan": xp}),
+        ]
+
+    def start_across(p):
+        for copy in across(p):
+            copy.start()
+
+    for p in range(PIECES):
+        for copy in to_x[p]:
+            copy.wait()
+        unscale(tx_in, p)
+
+        def gather(r, sl, v):
+            hid[0, r, sl] = (part[ch, r, sl] + rx_b[r, sl]) + v
+
+        uncode(gather, p, px_in)
+
+        def sums(g, c):
+            r = pl.ds(pl.multiple_of(g * 8, 8), 8)
+            s_acc, q_acc = sum_a[r, :], sum_b[r, :]
+            values = [hid[0, r, sl] for sl in tiles_of(p)]
+            for v in values:
+                s_acc = s_acc + v
+                q_acc = q_acc + v * v
+            sum_a[r, :] = s_acc
+            sum_b[r, :] = q_acc
+            tops_h[p, r, :] = top_of(values)
+            return c
+
+        lax.fori_loop(0, d8 // 8, sums, 0)
+        if p < AHEAD:
+            row_top[...] = tops_h[p]
+            code(lambda r, sl: hid[0, r, sl], p, ph_out, th_out)
+            start_across(p)
+
+    def pack(slots):
+        s, q = as_rows(sum_a[0:d8, :], d_sizes), as_rows(sum_b[0:d8, :], d_sizes)
+        slots[me, 0:1, :] = s[0]
+        slots[me, 1:2, :] = s[1]
+        slots[me, 2:3, :] = q[0]
+        slots[me, 3:4, :] = q[1]
+
+    def columns_d(row0, row1):
+        tail = jnp.zeros((dpad - d8, LANES), F32)
+        return jnp.concatenate(
+            [as_column(row0, LANES), as_column(row1, d8 - LANES), tail], axis=0
+        )
+
+    pack(ar2)
+    share_start(ar2, me, n_dev, dev_peer, s2, r2)
+    for p in range(AHEAD, PIECES):
+        row_top[...] = tops_h[p]
+        code(lambda r, sl: hid[0, r, sl], p, ph_out, th_out)
+        start_across(p)
+
     def slopes(j):
         def body(g, c):
             r = pl.ds(pl.multiple_of(g * 16, 16), 16)
@@ -471,72 +601,6 @@
         return c
 
     lax.fori_loop(0, n_rows // step_rows, widen_cot, 0)
-
-    to_sib_b.wait()
-    sum_a[...] = jnp.zeros(sum_a.shape, F32)
-    sum_b[...] = jnp.zeros(sum_b.shape, F32)
-    hid[:, d8:dpad, :] = jnp.zeros((2, dpad - d8, n_px), F32)
-    gp2[...] = jnp.zeros(gp2.shape, F32)
-
-    def across(p):
-        at = lanes_of(p)
-        return [
-            remote(th_out.at[p], th_in.at[p], sh.at[0, p], rh.at[0, p], {"chan": xp}),
-            remote(ph_out.at[:, at], ph_in.at[:, at], sh.at[1, p], rh.at[1, p], {"chan": xp}),
-        ]
-
-    def start_across(p):
-        for copy in across(p):
-            copy.start()
-
-    for p in range(PIECES):
-        for copy in to_x[p]:
-            copy.wait()
-        unscale(tx_in, p)
-
-        def gather(r, sl, v):
-            hid[0, r, sl] = (part[ch, r, sl] + rx_b[r, sl]) + v
-
-        uncode(gather, p, px_in)
-
-        def sums(g, c):
-            r = pl.ds(pl.multiple_of(g * 8, 8), 8)
-            s_acc, q_acc = sum_a[r, :], sum_b[r, :]
-            values = [hid[0, r, sl] for sl in tiles_of(p)]
-            for v in values:
-                s_acc = s_acc + v
-                q_acc = q_acc + v * v
-            sum_a[r, :] = s_acc
-            sum_b[r, :] = q_acc
-            tops_h[p, r, :] = top_of(values)
-            return c
-
-        lax.fori_loop(0, d8 // 8, sums, 0)
-        if p == 0:
-            row_top[...] = tops_h[p]
-            code(lambda r, sl: hid[0, r, sl], p, ph_out, th_out)
-            start_across(p)
-
-    def pack(slots):
-        s, q = as_rows(sum_a[0:d8, :], d_sizes), as_rows(sum_b[0:d8, :], d_sizes)
-        slots[me, 0:1, :] = s[0]
-        slots[me, 1:2, :] = s[1]
-        slots[me, 2:3, :] = q[0]
-        slots[me, 3:4, :] = q[1]
-
-    def columns_d(row0, row1):
-        tail = jnp.zeros((dpad - d8, LANES), F32)
-        return jnp.concatenate(
-            [as_column(row0, LANES), as_column(row1, d8 - LANES), tail], axis=0
-        )
-
-    pack(ar2)
-    share_start(ar2, me, n_dev, dev_peer, s2, r2)
-    for p in range(1, PIECES):
-        row_top[...] = tops_h[p]
-        code(lambda r, sl: hid[0, r, sl], p, ph_out, th_out)
-        if p < PIECES - 1:
-            start_across(p)
 
     share_wait(ar2, me, n_dev, dev_peer, s2, r2)
     tot2 = total(ar2)
@@ -574,7 +638,6 @@
     lax.fori_loop(0, dpad // 16, second, 0)
     pack(ar3)
     share_start(ar3, me, n_dev, dev_peer, s3, r3)
-    start_across(PIECES - 1)
 
     w2acc[...] = lax.dot_general(
         act2[...], g9[0], (((1,), (1,)), ((), ())), preferred_element_type=F32
@@ -605,8 +668,7 @@
         def body(g, c):
             r = pl.ds(pl.multiple_of(g * 16, 16), 16)
             a, b = col_c[5, r, :], col_c[6, r, :]
-            for t in range(p * span, (p + 1) * span):
-                sl = slice(t * LANES, (t + 1) * LANES)
+            for sl in tiles_of(p):
                 v = hid[1, r, sl] * a + b
                 th = jnp.tanh(v)
                 gp2[1, r, sl] = (
@@ -615,16 +677,6 @@
             return c
 
         lax.fori_loop(0, dpad // 16, body, 0)
-
-    second_other(0)
-    for copy in w_sib:
-        copy.wait()
-    cw[xp] = cw[xp] + cwr[1]
-    cw[ch] = cw[ch] + cwr[0]
-    w_x = remote(cw.at[xp], cwx, sc.at[2], rc.at[2], {"chan": xp})
-    w_x.start()
-    for p in range(1, PIECES - 1):
-        second_other(p)
 
     zbuf[...] = lax.dot_general(
         w2b[...], act2[...], (((0,), (0,)), ((), ())), preferred_element_type=F32
@@ -651,11 +703,19 @@
             new = new + v
     new = new * jnp.concatenate([mask[ch]] * (TAP // 16), axis=0)
     gall[ch] = new[0 : gall.shape[1]]
+    for copy in w_sib:
+        copy.wait()
+    cw[xp] = cw[xp] + cwr[1]
+    cw[ch] = cw[ch] + cwr[0]
+    w_x = remote(cw.at[xp], cwx, sc.at[2], rc.at[2], {"chan": xp})
+    w_x.start()
     new_sib = remote(gall.at[ch], gall.at[ch], so.at[0], ro.at[0], {"chan": sib})
     new_xp = remote(gall.at[ch], gall.at[ch], so.at[1], ro.at[1], {"chan": xp})
     new_on = remote(gall.at[xp], gall.at[xp], so.at[2], ro.at[2], {"chan": sib})
     new_xp.start()
     new_sib.start()
+    for p in range(PIECES):
+        second_other(p)
 
     share_wait(ar3, me, n_dev, dev_peer, s3, r3)
     tot3 = total(ar3)
@@ -666,12 +726,11 @@
     col_c[7] = col_c[4] * bias_sum2c / count
     col_c[8] = col_c[4] * col_c[3] * gain_sum2c / count
 
-    def third(i, j):
+    def third(i, j, k):
         def body(g, c):
             r = pl.ds(pl.multiple_of(g * 16, 16), 16)
             c1, c2, c3, m = col_c[4, r, :], col_c[7, r, :], col_c[8, r, :], col_c[2, r, :]
-            for t in range(tiles):
-                sl = slice(t * LANES, (t + 1) * LANES)
+            for sl in [slice(t * LANES, (t + 1) * LANES) for t in range(k * tiles // 2, (k + 1) * tiles // 2)]:
                 gha[j, r, sl] = (
                     c1 * gp2[i, r, sl] - mask[j, :, sl] * (c2 + c3 * (hid[i, r, sl] - m))
                 ).astype(BF16)
@@ -679,13 +738,14 @@
 
         lax.fori_loop(0, dpad // 16, body, 0)
 
-    third(0, ch)
-    grad_sib = remote(gha.at[ch], gha.at[ch], sx.at[1], rxs.at[1], {"chan": sib})
-    grad_sib.start()
-    second_other(PIECES - 1)
-    third(1, xp)
-    grad_xs = remote(gha.at[xp], gha.at[xp], sx.at[2], rxs.at[2], {"chan": sib})
-    grad_xs.start()
+    grads = []
+    for i, j in ((0, ch), (1, xp)):
+        for k in range(2):
+            third(i, j, k)
+            at = pl.ds(k * (n_px // 2), n_px // 2)
+            copy = remote(gha.at[j, :, at], gha.at[j, :, at], st.at[i, k], rt.at[i, k], {"chan": sib})
+            copy.start()
+            grads.append(copy)
     d_rows, d_cols = iota((dpad, LANES), 0), iota((dpad, LANES), 1)
     here_d = (d_rows == d_cols + ch * grow) & (d_cols < grow)
     out_g2[...] = jnp.sum(jnp.where(here_d, gain_sum2c, 0.0), axis=0, keepdims=True)[:, 0:grow]
@@ -695,9 +755,10 @@
     sum_a[...] = jnp.zeros(sum_a.shape, F32)
     sum_b[...] = jnp.zeros(sum_b.shape, F32)
 
-    def weight_grad(j):
+    def weight_grad(j, k=None):
+        at = slice(0, n_px) if k is None else slice(k * (n_px // 2), (k + 1) * (n_px // 2))
         w1acc[0:dpad, 0:cp] = w1acc[0:dpad, 0:cp] + lax.dot_general(
-            gha[j], act[j], (((1,), (1,)), ((), ())), preferred_element_type=F32
+            gha[j, :, at], act[j, :, at], (((1,), (1,)), ((), ())), preferred_element_type=F32
         )
 
     def input_grad(j):
@@ -724,11 +785,11 @@
     weight_grad(ch)
     weight_grad(xp)
     w_x.wait()
-    grad_sib.wait()
-    weight_grad(sib)
     input_grad(ch)
-    grad_xs.wait()
-    weight_grad(xs)
+    for i, j in ((0, sib), (1, xs)):
+        for k in range(2):
+            grads[2 * i + k].wait()
+            weight_grad(j, k)
 
     for r in range(17):
         cb[r // 5, r % 5 * 8 : r % 5 * 8 + 8, :] = w1acc[r * 8 : r * 8 + 8, 0:LANES]
@@ -762,7 +823,7 @@
     is_owner = lax.rem(dp, stride) == 0
 
     def part_to(k):
-        q = lax.rem(my_part + k, OWNERS)
+        q = my_part ^ (OWNERS - 1 - k)
         return q, q * stride
 
     def push(k, c):
@@ -782,6 +843,8 @@
         ar4[dp, i : i + 1, :] = s4_[i]
         ar4[dp, 2 + i : 3 + i, :] = q4_[i]
     share_start(ar4, dp, n_dp, dp_peer, s4, r4)
+    new_xp.wait()
+    new_on.start()
 
     def scatter(g, c):
         first = g * 16 * rpc
@@ -794,7 +857,7 @@
                     out_g[at, :] = v[h * 8 : h * 8 + 8]
         return c
 
-    lax.fori_loop(0, cp // 16, scatter, 0)
+    lax.fori_loop(0, 5, scatter, 0)
 
     def push_wait(k, c):
         q, to = part_to(k)
@@ -818,41 +881,26 @@
             v = v + decode(rsl[lax.rem(dp + k, n_dp)])
         fin[my_part] = encode(v)
 
-        def give(k, c):
+        def give(k):
             remote(fin.at[my_part], fin.at[my_part], sa.at[k], ra.at[my_part], dp_peer(k)).start()
-            return c
-
-        lax.fori_loop(1, n_dp, give, 0)
+
+        far_first(n_dp, give)
 
     lax.fori_loop(0, OWNERS, push_wait, 0)
+    lax.fori_loop(5, cp // 16, scatter, 0)
 
     for i in range(2):
         col_a[pl.ds(i * LANES, c_sizes[i]), :] = as_column(scale1[i], c_sizes[i])
-        for b in range(n_img):
-            for t in range(tiles // 2):
-                u = i * (tiles // 2) + t
-                mask_raw[u * n_img + b : u * n_img + b + 1, :] = mask[b, 0:1, u * LANES : (u + 1) * LANES]
-
-    new_xp.wait()
-    new_on.start()
+
     new_sib.wait()
     new_on.wait()
     for b in range(n_img):
         for t in range(tiles):
             for h in range(gall.shape[1] // 8):
-                graw[pl.ds(h * 8 * rpc + t * n_img + b, 8, stride=rpc), :] = gall[
+                out_new[pl.ds(h * 8 * rpc + t * n_img + b, 8, stride=rpc), :] = gall[
                     b, h * 8 : h * 8 + 8, t * LANES : (t + 1) * LANES
                 ]
-    for s in range(per_device):
-        chosen = slot_of == ch * per_device + s
-
-        def place_new(i, c):
-            src = pl.ds(pl.multiple_of(i * rpc, rpc), rpc)
-            dst = pl.ds(pl.multiple_of((s * grow + i) * rpc, rpc), rpc)
-            out_x[dst, :] = jnp.where(chosen, graw[src, :], out_x[dst, :])
-            return c
-
-        lax.fori_loop(0, grow, place_new, 0)
+    out_slot[...] = (slot_of - ch * per_device)[0:8].astype(F32)
 
     share_wait(ar4, dp, n_dp, dp_peer, s4, r4)
     tot4 = total(ar4)
@@ -926,17 +974,23 @@
         out_w2[t] = u[0:grow, 0:grow]
 
 
-def finish(n_rows, *refs):
-    n = (len(refs) - 1) // 2
-    sem = refs[-1]
-    copies = []
-    for i in range(n):
-        src, dst = refs[i], refs[n + i]
-        if i < 2:
-            src = src.at[pl.ds(0, n_rows)]
-        copies.append(pltpu.make_async_copy(src, dst, sem.at[i]))
+def finish(n_rows, grow_rows, *refs):
+    n = (len(refs) - 3) // 2
+    new, slot = refs[n : n + 2]
+    outs, sem = refs[n + 2 : -1], refs[-1]
+    segments = n_rows // grow_rows
+    copies = [pltpu.make_async_copy(refs[1].at[pl.ds(0, n_rows)], outs[1], sem.at[1])]
+    copies += [pltpu.make_async_copy(refs[i], outs[i], sem.at[i]) for i in range(2, n)]
     for copy in copies:
         copy.start()
+    here = jnp.max(slot[...])
+    for k in range(segments):
+        at = pl.ds(k * grow_rows, grow_rows)
+        kept = pltpu.make_async_copy(refs[0].at[at], outs[0].at[at], sem.at[n + k])
+        grown = pltpu.make_async_copy(new.at[pl.ds(0, grow_rows)], outs[0].at[at], sem.at[n + k])
+        pl.when(here == k)(grown.start)
+        pl.when(here != k)(kept.start)
+        copies.append(kept)
     for copy in copies:
         copy.wait()
 
@@ -992,7 +1046,8 @@
         v((n_img, cp, n_px), BF16), v((n_img, cp, n_px), BF16),
         v((n_img, cp, n_px), F32), v((n_img, cp, n_px), F32), v((cp, n_px), F32),
         v((cp, LANES), F32), v((cp, LANES), F32), v((cp, LANES), F32), v((cp, LANES), F32),
-        v((9, dpad, LANES), F32), v((cp, LANES), F32), v((cp, LANES), F32), v((8, LANES), F32),
+        v((9, dpad, LANES), F32), v((cp, LANES), F32), v((cp, LANES), F32),
+        v((cp * 8, LANES), F32), v((cp * 8, LANES), F32), v((8, LANES), F32),
         v((dpad, cp), BF16), v((n_img, dpad, n_px), F32),
         v((dpad, n_px), F32), v((dpad, n_px), F32), v((2, dpad, n_px), F32),
         v((d8, LANES), F32), v((d8, LANES), F32), v((PIECES, d8, LANES), F32),
@@ -1012,12 +1067,13 @@
         dma((n_dp,)), dma((n_dp,)), dma((n_dev,)), dma((n_dev,)), dma((n_dev,)), dma((n_dev,)), dma((n_dp,)), dma((n_dp,)),
         dma((3,)), dma((3,)), dma((PIECES,)), dma((PIECES,)), dma((2, PIECES)), dma((2, PIECES)),
         dma((4,)), dma((4,)), dma((n_ch,)), dma((n_ch,)), dma((n_ch,)), dma((n_ch,)),
-        dma((2, PIECES)), dma((2, PIECES)), dma((3,)), dma((3,)), dma((3,)), dma((3,)),
+        dma((2, PIECES)), dma((2, PIECES)), dma((2, 2)), dma((2, 2)), dma((3,)), dma((3,)), dma((3,)), dma((3,)),
         dma((OWNERS,)), dma((n_dp,)), dma((n_dp,)), dma((OWNERS,)),
     ]
     out_shape = (
         sd((n_pad, LANES), F32), sd((n_pad, LANES), F32), sd((n_d, n_c), F32),
         sd((1, n_c), F32), sd((1, n_c), F32), sd((9, grow, grow), F32), sd((1, grow), F32), sd((1, grow), F32),
+        sd((40 * rpc, LANES), F32), sd((8, LANES), F32),
     )
     outs = pl.pallas_call(
         functools.partial(layer, cfg),
@@ -1029,13 +1085,13 @@
             collective_id=0, has_side_effects=True, vmem_limit_bytes=40 << 20
         ),
     )(*args)
-    final = (sd((n_rows, LANES), F32),) * 2 + out_shape[2:]
+    final = (sd((n_rows, LANES), F32),) * 2 + out_shape[2:-2]
     o = pl.pallas_call(
-        functools.partial(finish, n_rows),
+        functools.partial(finish, n_rows, grow * rpc),
         out_shape=final,
-        in_specs=[in_vmem] * len(final),
+        in_specs=[in_vmem] * len(outs),
         out_specs=(in_hbm,) * len(final),
-        scratch_shapes=[dma((len(final),))],
+        scratch_shapes=[dma((len(final) + n_c // grow,))],
         compiler_params=pltpu.CompilerParams(vmem_limit_bytes=8 << 20),
     )(*outs)
     return (

time: 54.7 us -> 52.7 us (0.963)
  Pallas kernels: 53.9 us -> 51.9 us
    pallas_call x1, Pallas kernels: 51.3 us -> 49.3 us  [on_device(): pl.pallas_call(functools.partial(layer, cfg), out_shape=out_shape, in_spe...]
where the time goes in v5:
time: 52.7 us; the launch traced here: 52.6 us
  Pallas kernels  51.9 us (98%)
  between operations  0.64 us (1%)
    pallas_call x1, Pallas kernels, on_device(): pl.pallas_call(functools.partial(layer, cfg), out_shape=out_shape, in_spe...  49.3 us
    pallas_call x1, Pallas kernels, on_device(): pl.pallas_call(functools.partial(finish, n_rows, grow * rpc), out_shape=f...  2.62 us

profile of v5, /device:TPU:0, one launch (start us, length us, event | category | flops | bytes accessed | tf_op | source)
XLA Modules:
  0.0 52.6 jit_solution(6622425782170700872)
XLA Ops:
  0.6 49.3 %shard_map.161 = (f32[5632,128]{1,0:T(8,128)S(1)}, f32[5632,128]{1,0:T(8,128)S(1)}, f32[132,165]{1,0:T(8,128)S(1)}, f32[1,165]{1,0:T(1,128)S(1)}, f32[1,165]{1,0...) custom-call(bf16[5280,128]{1,0:T(8,128)(2,1)} %bitcast.40, ...), custom_call_target="tpu_custom_call" | custom-call | tf_op jit(solution)/shard_map/pallas_call | solution.py:1078
  50.0 2.6 %shard_map.162 = (f32[5280,128]{1,0:T(8,128)}, f32[5280,128]{1,0:T(8,128)}, f32[132,165]{1,0:T(8,128)}, f32[1,165]{1,0:T(1,128)}, f32[1,165]{1,0:T(1,128)}, /*in...) custom-call(f32[5632,128]{1,0:T(8,128)S(1)} %get-tuple-element.26.refs_0_, ...), custom_call_target="tpu_custom_call" | custom-call | tf_op jit(solution)/shard_map/pallas_call | solution.py:1089

commit v6 on v5

--- a/solution.py
+++ b/solution.py
@@ -15,7 +15,7 @@
 SPANS = (1, 2, 3, 2)
 PIECES = len(SPANS)
 AHEAD = 2
-LEVELS = 1048000.0
+LEVELS = 524000.0
 OWNERS = 8
 
 MESH = pl.DeviceIdType.MESH
@@ -60,7 +60,7 @@
     col_a, col_b, col_m, col_k, col_c, sum_a, sum_b, sums_s, sums_q, rowbuf,
     w1s, part, rx_a, rx_b, hid, row_top, row_scale, tops_h,
     px_out, px_in, tx_out, tx_in, ph_out, ph_in, th_out, th_in,
-    graw, gsend, gsx, gpair, grx, gcur, g9, w2blk, w2r, w2b, gsl,
+    graw, gsend, gsx, gpair, grx, gcur, g9, w2pad, w2wide, w2r, w2b, gsl,
     act2, gp2, back, zbuf, gall, gha,
     cw, cwr, cwx, cb, coded, rsl, fin, w1acc, w2acc,
     ar1, ar2, ar3, ar4,
@@ -106,16 +106,24 @@
 
             lax.fori_loop(0, count - 1, body, 0)
 
-    loads = [
-        pltpu.make_async_copy(h, v, load_sem.at[i])
+    loads = {
+        i: pltpu.make_async_copy(h, v, load_sem.at[i])
         for i, (h, v) in enumerate(
             (
-                (feat_h, feat), (cot_h, cot), (w1_h, w1v), (gain1_h, gain1v), (bias1_h, bias1v),
+                (cot_h, cot), (w1_h, w1v), (gain1_h, gain1v), (bias1_h, bias1v),
                 (gain2_h, gain2v), (bias2_h, bias2v), (w2_h, w2v), (side_h, side), (slot_h, slot),
-            )
+            ),
+            1,
         )
+    }
+    third_rows = feat.shape[0] // 3
+    feat_parts = [
+        pltpu.make_async_copy(
+            feat_h.at[pl.ds(k * third_rows, third_rows)], feat.at[pl.ds(k * third_rows, third_rows)], load_sem.at[10 + k]
+        )
+        for k in range(3)
     ]
-    for copy in loads:
+    for copy in [loads[8], loads[9], *feat_parts, *(loads[i] for i in range(1, 8))]:
         copy.start()
     barrier = pltpu.get_barrier_semaphore()
 
@@ -149,8 +157,8 @@
             return value
         return lax.fori_loop(1, slots.shape[0], lambda i, v: v + slots[i], slots[0])
 
-    for copy in loads[8:]:
-        copy.wait()
+    loads[8].wait()
+    loads[9].wait()
     row_r, lane_r = iota((rpc, LANES), 0), iota((rpc, LANES), 1)
     tile_of, image_of = row_r // n_img, row_r % n_img
     count_here = jnp.int32(0)
@@ -162,7 +170,6 @@
     mask_raw[...] = jnp.where((pixel_of // SIDE < side_of) & (pixel_of % SIDE < side_of), 1.0, 0.0)
     mask_of = mask_raw[...]
     n_rows = feat.shape[0]
-    loads[0].wait()
 
     def halves(v):
         while v.shape[0] > 8:
@@ -180,7 +187,9 @@
             sums_q[at, :] = halves(w * v)
         return c
 
-    lax.fori_loop(0, n_c // 5, first_sums, 0)
+    for k in range(3):
+        feat_parts[k].wait()
+        lax.fori_loop(n_c // 15 * k, n_c // 15 * (k + 1), first_sums, 0)
     sums_s[n_c * 8 : cp * 8, :] = jnp.zeros(((cp - n_c) * 8, LANES), F32)
     sums_q[n_c * 8 : cp * 8, :] = jnp.zeros(((cp - n_c) * 8, LANES), F32)
 
@@ -242,6 +251,21 @@
     by_image(ch)
     by_image(xp)
 
+    lane16 = iota((16, n_px), 1)
+    row_of, col_of = lane16 >> 5, lane16 & (SIDE - 1)
+    for b in range(n_img):
+        mask[b] = jnp.where((row_of < side[b]) & (col_of < side[b]), 1.0, 0.0)
+
+    out_x[pl.ds(n_rows, out_x.shape[0] - n_rows), :] = jnp.zeros((out_x.shape[0] - n_rows, LANES), F32)
+    step_rows = 3 * rpc
+
+    def widen(i, c):
+        r = pl.ds(pl.multiple_of(i * step_rows, step_rows), step_rows)
+        out_x[r, :] = feat[r, :].astype(F32)
+        return c
+
+    lax.fori_loop(0, n_rows // step_rows, widen, 0)
+
     for copy in g_sib:
         copy.wait()
     gpair[0] = (gsend[ch].astype(F32) + gsx[0].astype(F32)).astype(BF16)
@@ -253,21 +277,37 @@
     for copy in g_x:
         copy.start()
 
+    def relayout(b):
+        def body(g, c):
+            r = pl.ds(pl.multiple_of(g * 16, 16), 16)
+            for t in range(tiles):
+                k = g * 16 * rpc + t * n_img + b
+                v = jnp.concatenate([out_x[pl.ds(k + h * 8 * rpc, 8, stride=rpc), :] for h in range(2)], axis=0)
+                xb[b, r, t * LANES : (t + 1) * LANES] = v.astype(BF16)
+            return c
+
+        lax.fori_loop(0, cp // 16, body, 0)
+
+    relayout(xs)
+    relayout(xp)
     loads[7].wait()
-    w2blk[...] = jnp.zeros(w2blk.shape, BF16)
-    acc = jnp.zeros((grow, w2blk.shape[1]), F32)
+    w2pad[...] = jnp.zeros(w2pad.shape, F32)
+    w2wide[...] = jnp.zeros(w2wide.shape, F32)
     for t in range(9):
-        place = jnp.where(
-            iota((grow, w2blk.shape[1]), 1) == iota((grow, w2blk.shape[1]), 0) + t * TAP, 1.0, 0.0
-        ).astype(BF16)
-        acc = acc + jnp.dot(w2v[t], place, preferred_element_type=F32)
-    w2blk[0:grow, :] = acc.astype(BF16)
+        w2pad[t, 0:grow, 0:grow] = w2v[t].astype(F32)
+        tile, off = t * TAP // LANES, t * TAP % LANES
+        v = pltpu.roll(w2pad[t], off, 1) if off else w2pad[t]
+        lane = iota(v.shape, 1)
+        here = slice(tile * LANES, (tile + 1) * LANES)
+        w2wide[:, here] = w2wide[:, here] + jnp.where(lane >= off, v, 0.0)
+        if off + grow > LANES:
+            there = slice((tile + 1) * LANES, (tile + 2) * LANES)
+            w2wide[:, there] = w2wide[:, there] + jnp.where(lane < off, v, 0.0)
+    w2r[ch] = w2wide[...].astype(BF16)
     loads[5].wait()
     loads[6].wait()
     gsl[ch, 0:1, 0:grow] = gain2v[...]
     gsl[ch, 1:2, 0:grow] = bias2v[...]
-    w2r[ch] = w2blk[...]
-
     w_near = remote(w2r.at[ch], w2r.at[ch], sw.at[0], rw.at[0], {"chan": sib})
     w_far = remote(w2r.at[ch], w2r.at[ch], sw.at[1], rw.at[1], {"chan": xp})
     w_on = remote(w2r.at[xp], w2r.at[xp], sw.at[2], rw.at[2], {"chan": sib})
@@ -275,35 +315,6 @@
     w_near.start()
     share_start(gsl, ch, n_ch, ch_peer, sb, rb)
 
-    lane16 = iota((16, n_px), 1)
-    row_of, col_of = lane16 >> 5, lane16 & (SIDE - 1)
-    for b in range(n_img):
-        mask[b] = jnp.where((row_of < side[b]) & (col_of < side[b]), 1.0, 0.0)
-
-    out_x[pl.ds(n_rows, out_x.shape[0] - n_rows), :] = jnp.zeros((out_x.shape[0] - n_rows, LANES), F32)
-    out_g[pl.ds(n_rows, out_g.shape[0] - n_rows), :] = jnp.zeros((out_g.shape[0] - n_rows, LANES), F32)
-    step_rows = 3 * rpc
-
-    def widen(i, c):
-        r = pl.ds(pl.multiple_of(i * step_rows, step_rows), step_rows)
-        out_x[r, :] = feat[r, :].astype(F32)
-        return c
-
-    lax.fori_loop(0, n_rows // step_rows, widen, 0)
-
-    def relayout(g, c):
-        base_row = g * 16 * rpc
-        r = pl.ds(pl.multiple_of(g * 16, 16), 16)
-        for b in range(n_img):
-            for t in range(tiles):
-                k = t * n_img + b
-                v = jnp.concatenate(
-                    [out_x[pl.ds(base_row + h * 8 * rpc + k, 8, stride=rpc), :] for h in range(2)], axis=0
-                )
-                xb[b, r, t * LANES : (t + 1) * LANES] = v.astype(BF16)
-        return c
-
-    lax.fori_loop(0, cp // 16, relayout, 0)
     loads[2].wait()
     w1s[...] = jnp.zeros(w1s.shape, BF16)
     w1s[0:n_d, 0:n_c] = w1v[...]
@@ -364,7 +375,8 @@
     def tiles_of(p):
         return [slice(t * LANES, (t + 1) * LANES) for t in range(edges[p], edges[p + 1])]
 
-    blocks, rest = d8 // 24, d8 // 24 * 24
+    blocks, rest = d8 // 64, d8 // 64 * 64
+    plain = blocks * 40
 
     def code(read, p, words, tops):
         top = jnp.maximum(jnp.max(row_top[...], axis=1, keepdims=True), 1e-30)
@@ -377,15 +389,19 @@
             return jnp.round(read(r, sl) * row_scale[r, :]).astype(jnp.int32)
 
         def block(i, c):
-            for sl in tiles_of(p):
-                q0, q1, q2 = (quantized(i * 24 + k * 8, 8, sl) for k in range(3))
-                words[pl.ds(pl.multiple_of(i * 16, 8), 8), sl] = (q0 << 11) | ((q2 >> 10) & 0x7FF)
-                words[pl.ds(pl.multiple_of(i * 16 + 8, 8), 8), sl] = (q1 << 11) | (q2 & 0x3FF)
+            for t, sl in enumerate(tiles_of(p), edges[p]):
+                high = jnp.zeros((8, LANES), jnp.int32)
+                for k in range(4):
+                    first = quantized(i * 64 + k * 8, 8, sl)
+                    second = quantized(i * 64 + 32 + k * 8, 8, sl)
+                    words[t, pl.ds(pl.multiple_of(i * 40 + k * 8, 8), 8), :] = (first << 12) | (second & 0xFFF)
+                    high = high | (((second >> 12) & 0xFF) << (8 * k))
+                words[t, pl.ds(pl.multiple_of(i * 40 + 32, 8), 8), :] = high
             return c
 
         lax.fori_loop(0, blocks, block, 0)
-        for sl in tiles_of(p):
-            words[blocks * 16 : blocks * 16 + d8 - rest, sl] = quantized(rest, d8 - rest, sl)
+        for t, sl in enumerate(tiles_of(p), edges[p]):
+            words[t, plain : plain + d8 - rest, :] = quantized(rest, d8 - rest, sl)
 
     def unscale(tops, p):
         top = jnp.concatenate([as_column(tops[p, 0:1, :], LANES), as_column(tops[p, 1:2, :], d8 - LANES)], axis=0)
@@ -397,17 +413,17 @@
             write(r, sl, q.astype(F32) * row_scale[r, :])
 
         def block(i, c):
-            for sl in tiles_of(p):
-                w0 = words[pl.ds(pl.multiple_of(i * 16, 8), 8), sl]
-                w1 = words[pl.ds(pl.multiple_of(i * 16 + 8, 8), 8), sl]
-                put(i * 24, 8, sl, w0 >> 11)
-                put(i * 24 + 8, 8, sl, w1 >> 11)
-                put(i * 24 + 16, 8, sl, (((w0 << 21) >> 21) << 10) | (w1 & 0x3FF))
+            for t, sl in enumerate(tiles_of(p), edges[p]):
+                high = words[t, pl.ds(pl.multiple_of(i * 40 + 32, 8), 8), :]
+                for k in range(4):
+                    low = words[t, pl.ds(pl.multiple_of(i * 40 + k * 8, 8), 8), :]
+                    put(i * 64 + k * 8, 8, sl, low >> 12)
+                    put(i * 64 + 32 + k * 8, 8, sl, (((high << (24 - 8 * k)) >> 24) << 12) | (low & 0xFFF))
             return c
 
         lax.fori_loop(0, blocks, block, 0)
-        for sl in tiles_of(p):
-            put(rest, d8 - rest, sl, words[blocks * 16 : blocks * 16 + d8 - rest, sl])
+        for t, sl in enumerate(tiles_of(p), edges[p]):
+            put(rest, d8 - rest, sl, words[t, plain : plain + d8 - rest, :])
 
     def top_of(values):
         value = jnp.abs(values[0])
@@ -442,10 +458,10 @@
 
         lax.fori_loop(0, d8 // 8, add_a, 0)
         code(lambda r, sl: part[xp, r, sl], p, px_out, tx_out)
-        at = lanes_of(p)
+        at = pl.ds(edges[p], edges[p + 1] - edges[p])
         copies = [
             remote(tx_out.at[p], tx_in.at[p], sq.at[0, p], rq.at[0, p], {"chan": xp}),
-            remote(px_out.at[:, at], px_in.at[:, at], sq.at[1, p], rq.at[1, p], {"chan": xp}),
+            remote(px_out.at[at], px_in.at[at], sq.at[1, p], rq.at[1, p], {"chan": xp}),
         ]
         for copy in copies:
             copy.start()
@@ -456,8 +472,8 @@
         r = pl.ds(i * LANES, c_sizes[i])
         col_m[r, :] = as_column(mean1[i], c_sizes[i])
         col_k[r, :] = as_column(keep1[i], c_sizes[i])
-    w_far.wait()
-    w_on.start()
+    relayout(sib)
+    relayout(ch)
     partial(sib, 0, tiles)
     to_sib_b = remote(part.at[sib, rows_d], rx_b.at[rows_d], sx.at[0], rxs.at[0], {"chan": sib})
     to_sib_b.start()
@@ -465,9 +481,6 @@
 
     for copy in g_x:
         copy.wait()
-    w_near.wait()
-    w_on.wait()
-    share_wait(gsl, ch, n_ch, ch_peer, sb, rb)
     px = iota((TAP, n_px), 1)
     py, pxx = px >> 5, px & (SIDE - 1)
     for i in range(2):
@@ -492,6 +505,95 @@
                     v = jnp.where(ok, v, 0.0)
                 g9[i, t * TAP : (t + 1) * TAP, :] = v.astype(BF16)
         g9[i, pl.ds(9 * TAP, TAPS - 9 * TAP), :] = jnp.zeros((TAPS - 9 * TAP, n_px), BF16)
+    def slopes(j):
+        def body(g, c):
+            r = pl.ds(pl.multiple_of(g * 16, 16), 16)
+            a, b = col_a[r, :], col_b[r, :]
+            k = 0.5 * col_k[r, :]
+            for t in range(tiles):
+                sl = slice(t * LANES, (t + 1) * LANES)
+                v = xb[j, r, sl].astype(F32) * a + b
+                th = jnp.tanh(v)
+                slope[j, r, sl] = ((1.0 + th) * (1.0 + v * (1.0 - th))) * (mask[j, :, sl] * k)
+            return c
+
+        lax.fori_loop(0, cp // 16, body, 0)
+
+    slopes(xs)
+    slopes(xp)
+
+    to_sib_b.wait()
+    sum_a[...] = jnp.zeros(sum_a.shape, F32)
+    sum_b[...] = jnp.zeros(sum_b.shape, F32)
+    hid[:, d8:dpad, :] = jnp.zeros((2, dpad - d8, n_px), F32)
+    gp2[...] = jnp.zeros(gp2.shape, F32)
+
+    def across(p):
+        at = pl.ds(edges[p], edges[p + 1] - edges[p])
+        return [
+            remote(th_out.at[p], th_in.at[p], sh.at[0, p], rh.at[0, p], {"chan": xp}),
+            remote(ph_out.at[at], ph_in.at[at], sh.at[1, p], rh.at[1, p], {"chan": xp}),
+        ]
+
+    def start_across(p):
+        for copy in across(p):
+            copy.start()
+
+    for p in range(PIECES):
+        for copy in to_x[p]:
+            copy.wait()
+        unscale(tx_in, p)
+
+        def gather(r, sl, v):
+            hid[0, r, sl] = (part[ch, r, sl] + rx_b[r, sl]) + v
+
+        uncode(gather, p, px_in)
+
+        def sums(g, c):
+            r = pl.ds(pl.multiple_of(g * 8, 8), 8)
+            s_acc, q_acc = sum_a[r, :], sum_b[r, :]
+            values = [hid[0, r, sl] for sl in tiles_of(p)]
+            for v in values:
+                s_acc = s_acc + v
+                q_acc = q_acc + v * v
+            sum_a[r, :] = s_acc
+            sum_b[r, :] = q_acc
+            tops_h[p, r, :] = top_of(values)
+            return c
+
+        lax.fori_loop(0, d8 // 8, sums, 0)
+        if p < AHEAD:
+            row_top[...] = tops_h[p]
+            code(lambda r, sl: hid[0, r, sl], p, ph_out, th_out)
+            start_across(p)
+
+    def pack(slots):
+        s, q = as_rows(sum_a[0:d8, :], d_sizes), as_rows(sum_b[0:d8, :], d_sizes)
+        slots[me, 0:1, :] = s[0]
+        slots[me, 1:2, :] = s[1]
+        slots[me, 2:3, :] = q[0]
+        slots[me, 3:4, :] = q[1]
+
+    def columns_d(row0, row1):
+        tail = jnp.zeros((dpad - d8, LANES), F32)
+        return jnp.concatenate(
+            [as_column(row0, LANES), as_column(row1, d8 - LANES), tail], axis=0
+        )
+
+    pack(ar2)
+    share_start(ar2, me, n_dev, dev_peer, s2, r2)
+    for p in range(AHEAD, PIECES):
+        row_top[...] = tops_h[p]
+        code(lambda r, sl: hid[0, r, sl], p, ph_out, th_out)
+        start_across(p)
+
+    w_far.wait()
+    w_on.start()
+    slopes(sib)
+    slopes(ch)
+    w_near.wait()
+    w_on.wait()
+    share_wait(gsl, ch, n_ch, ch_peer, sb, rb)
     acc = jnp.zeros((dpad, w2b.shape[1]), F32)
     for j in range(n_ch):
         rows = iota((dpad, TAP), 0)
@@ -511,88 +613,6 @@
         bias2c = bias2c + jnp.sum(jnp.where(place, gsl[j, 1:2, :], 0.0), axis=1, keepdims=True)
     col_c[0] = jnp.broadcast_to(gain2c, (dpad, LANES))
     col_c[1] = jnp.broadcast_to(bias2c, (dpad, LANES))
-
-    to_sib_b.wait()
-    sum_a[...] = jnp.zeros(sum_a.shape, F32)
-    sum_b[...] = jnp.zeros(sum_b.shape, F32)
-    hid[:, d8:dpad, :] = jnp.zeros((2, dpad - d8, n_px), F32)
-    gp2[...] = jnp.zeros(gp2.shape, F32)
-
-    def across(p):
-        at = lanes_of(p)
-        return [
-            remote(th_out.at[p], th_in.at[p], sh.at[0, p], rh.at[0, p], {"chan": xp}),
-            remote(ph_out.at[:, at], ph_in.at[:, at], sh.at[1, p], rh.at[1, p], {"chan": xp}),
-        ]
-
-    def start_across(p):
-        for copy in across(p):
-            copy.start()
-
-    for p in range(PIECES):
-        for copy in to_x[p]:
-            copy.wait()
-        unscale(tx_in, p)
-
-        def gather(r, sl, v):
-            hid[0, r, sl] = (part[ch, r, sl] + rx_b[r, sl]) + v
-
-        uncode(gather, p, px_in)
-
-        def sums(g, c):
-            r = pl.ds(pl.multiple_of(g * 8, 8), 8)
-            s_acc, q_acc = sum_a[r, :], sum_b[r, :]
-            values = [hid[0, r, sl] for sl in tiles_of(p)]
-            for v in values:
-                s_acc = s_acc + v
-                q_acc = q_acc + v * v
-            sum_a[r, :] = s_acc
-            sum_b[r, :] = q_acc
-            tops_h[p, r, :] = top_of(values)
-            return c
-
-        lax.fori_loop(0, d8 // 8, sums, 0)
-        if p < AHEAD:
-            row_top[...] = tops_h[p]
-            code(lambda r, sl: hid[0, r, sl], p, ph_out, th_out)
-            start_across(p)
-
-    def pack(slots):
-        s, q = as_rows(sum_a[0:d8, :], d_sizes), as_rows(sum_b[0:d8, :], d_sizes)
-        slots[me, 0:1, :] = s[0]
-        slots[me, 1:2, :] = s[1]
-        slots[me, 2:3, :] = q[0]
-        slots[me, 3:4, :] = q[1]
-
-    def columns_d(row0, row1):
-        tail = jnp.zeros((dpad - d8, LANES), F32)
-        return jnp.concatenate(
-            [as_column(row0, LANES), as_column(row1, d8 - LANES), tail], axis=0
-        )
-
-    pack(ar2)
-    share_start(ar2, me, n_dev, dev_peer, s2, r2)
-    for p in range(AHEAD, PIECES):
-        row_top[...] = tops_h[p]
-        code(lambda r, sl: hid[0, r, sl], p, ph_out, th_out)
-        start_across(p)
-
-    def slopes(j):
-        def body(g, c):
-            r = pl.ds(pl.multiple_of(g * 16, 16), 16)
-            a, b = col_a[r, :], col_b[r, :]
-            k = 0.5 * col_k[r, :]
-            for t in range(tiles):
-                sl = slice(t * LANES, (t + 1) * LANES)
-                v = xb[j, r, sl].astype(F32) * a + b
-                th = jnp.tanh(v)
-                slope[j, r, sl] = ((1.0 + th) * (1.0 + v * (1.0 - th))) * (mask[j, :, sl] * k)
-            return c
-
-        lax.fori_loop(0, cp // 16, body, 0)
-
-    for j in range(n_img):
-        slopes(j)
 
     def widen_cot(i, c):
         r = pl.ds(pl.multiple_of(i * step_rows, step_rows), step_rows)
@@ -1018,7 +1038,7 @@
     rpc = n_px // LANES * n_img
     n_rows, n_pad = n_c * rpc, cp * rpc
     n_dev = n_dp * n_ch
-    words = d8 // 24 * 16 + d8 % 24
+    words = d8 // 64 * 40 + d8 % 64
     cfg = (n_dp, n_ch, n_img, n_c, n_px, n_d, grow)
     args = (
         flat(features),
@@ -1051,11 +1071,11 @@
         v((dpad, cp), BF16), v((n_img, dpad, n_px), F32),
         v((dpad, n_px), F32), v((dpad, n_px), F32), v((2, dpad, n_px), F32),
         v((d8, LANES), F32), v((d8, LANES), F32), v((PIECES, d8, LANES), F32),
-        v((words, n_px), jnp.int32), v((words, n_px), jnp.int32), v((PIECES, 2, LANES), F32), v((PIECES, 2, LANES), F32),
-        v((words, n_px), jnp.int32), v((words, n_px), jnp.int32), v((PIECES, 2, LANES), F32), v((PIECES, 2, LANES), F32),
+        v((n_px // LANES, words, LANES), jnp.int32), v((n_px // LANES, words, LANES), jnp.int32), v((PIECES, 2, LANES), F32), v((PIECES, 2, LANES), F32),
+        v((n_px // LANES, words, LANES), jnp.int32), v((n_px // LANES, words, LANES), jnp.int32), v((PIECES, 2, LANES), F32), v((PIECES, 2, LANES), F32),
         v((TAP * rpc, LANES), F32), v((n_ch, TAP, n_px), BF16),
         v((2, TAP, n_px), BF16), v((2, TAP, n_px), BF16), v((2, TAP, n_px), BF16), v((TAP, n_px), F32),
-        v((2, TAPS, n_px), BF16), v((TAP, TAPS), BF16), v((n_ch, TAP, TAPS), BF16), v((dpad, TAPS), BF16),
+        v((2, TAPS, n_px), BF16), v((9, TAP, LANES), F32), v((TAP, TAPS), F32), v((n_ch, TAP, TAPS), BF16), v((dpad, TAPS), BF16),
         v((n_ch, 2, LANES), F32),
         v((dpad, n_px), BF16), v((2, dpad, n_px), F32), v((2, dpad, n_px), F32), v((TAPS, n_px), F32),
         v((n_ch, 40, n_px), F32), v((n_ch, dpad, n_px), BF16),
@@ -1063,7 +1083,7 @@
         v((OWNERS, 40, LANES), F32), v((OWNERS, 24, LANES), jnp.int32),
         v((n_dp, 24, LANES), jnp.int32), v((OWNERS, 24, LANES), jnp.int32), v((dpad, 256), F32), v((dpad, TAPS), F32),
         v((n_dp, 4, LANES), F32), v((n_dev, 4, LANES), F32), v((n_dev, 4, LANES), F32), v((n_dp, 4, LANES), F32),
-        dma((10,)),
+        dma((13,)),
         dma((n_dp,)), dma((n_dp,)), dma((n_dev,)), dma((n_dev,)), dma((n_dev,)), dma((n_dev,)), dma((n_dp,)), dma((n_dp,)),
         dma((3,)), dma((3,)), dma((PIECES,)), dma((PIECES,)), dma((2, PIECES)), dma((2, PIECES)),
         dma((4,)), dma((4,)), dma((n_ch,)), dma((n_ch,)), dma((n_ch,)), dma((n_ch,)),

time: 52.7 us -> 52 us (0.987)
  Pallas kernels: 51.9 us -> 51.2 us
    pallas_call x1, Pallas kernels: 49.3 us -> 48.5 us  [on_device(): pl.pallas_call(functools.partial(layer, cfg), out_shape=out_shape, in_spe...]
where the time goes in v6:
time: 52 us; the launch traced here: 51.8 us
  Pallas kernels  51.2 us (98%)
  between operations  0.64 us (1%)
    pallas_call x1, Pallas kernels, on_device(): pl.pallas_call(functools.partial(layer, cfg), out_shape=out_shape, in_spe...  48.5 us
    pallas_call x1, Pallas kernels, on_device(): pl.pallas_call(functools.partial(finish, n_rows, grow * rpc), out_shape=f...  2.62 us

profile of v6, /device:TPU:0, one launch (start us, length us, event | category | flops | bytes accessed | tf_op | source)
XLA Modules:
  0.0 51.8 jit_solution(5584326901314767316)
XLA Ops:
  0.6 48.5 %shard_map.161 = (f32[5632,128]{1,0:T(8,128)S(1)}, f32[5632,128]{1,0:T(8,128)S(1)}, f32[132,165]{1,0:T(8,128)S(1)}, f32[1,165]{1,0:T(1,128)S(1)}, f32[1,165]{1,0...) custom-call(bf16[5280,128]{1,0:T(8,128)(2,1)} %bitcast.40, ...), custom_call_target="tpu_custom_call" | custom-call | tf_op jit(solution)/shard_map/pallas_call | solution.py:1098
  49.2 2.6 %shard_map.162 = (f32[5280,128]{1,0:T(8,128)}, f32[5280,128]{1,0:T(8,128)}, f32[132,165]{1,0:T(8,128)}, f32[1,165]{1,0:T(1,128)}, f32[1,165]{1,0:T(1,128)}, /*in...) custom-call(f32[5632,128]{1,0:T(8,128)S(1)} %get-tuple-element.26.refs_0_, ...), custom_call_target="tpu_custom_call" | custom-call | tf_op jit(solution)/shard_map/pallas_call | solution.py:1109

commit v7 on v6

--- a/solution.py
+++ b/solution.py
@@ -57,7 +57,7 @@
     out_x, out_g, out_w1, out_g1, out_b1, out_w2, out_g2, out_b2, out_new, out_slot,
     feat, cot, w1v, gain1v, bias1v, gain2v, bias2v, w2v, side, slot,
     mask, mask_raw, base, xb, act, slope, gp1, gact,
-    col_a, col_b, col_m, col_k, col_c, sum_a, sum_b, sums_s, sums_q, rowbuf,
+    col_a, col_b, col_m, col_k, col_c, sum_a, sum_b, rowbuf,
     w1s, part, rx_a, rx_b, hid, row_top, row_scale, tops_h,
     px_out, px_in, tx_out, tx_in, ph_out, ph_in, th_out, th_in,
     graw, gsend, gsx, gpair, grx, gcur, g9, w2pad, w2wide, w2r, w2b, gsl,
@@ -116,13 +116,14 @@
             1,
         )
     }
-    third_rows = feat.shape[0] // 3
-    feat_parts = [
-        pltpu.make_async_copy(
-            feat_h.at[pl.ds(k * third_rows, third_rows)], feat.at[pl.ds(k * third_rows, third_rows)], load_sem.at[10 + k]
-        )
-        for k in range(3)
-    ]
+    feat_groups, feat_parts, start = [], [], 0
+    for k in range(3):
+        groups = pad_to(n_c, 8) // 8 * (k + 1) // 3 - sum(feat_groups)
+        size = min(groups * 8, n_c - start) * rpc
+        at = pl.ds(start * rpc, size)
+        feat_parts.append(pltpu.make_async_copy(feat_h.at[at], feat.at[at], load_sem.at[10 + k]))
+        feat_groups.append(groups)
+        start += groups * 8
     for copy in [loads[8], loads[9], *feat_parts, *(loads[i] for i in range(1, 8))]:
         copy.start()
     barrier = pltpu.get_barrier_semaphore()
@@ -177,31 +178,40 @@
             v = v[0:n] + v[n:]
         return v
 
-    def first_sums(i, c):
-        for k in range(5):
-            row = i * 5 + k
-            v = feat[pl.ds(pl.multiple_of(row * rpc, rpc), rpc), :].astype(F32)
+    sub = iota((8, LANES), 0)
+
+    def fold(values):
+        for d in (4, 2, 1):
+            half_n = len(values) // 2
+            values = [
+                jnp.where((sub & d) == 0, u + pltpu.roll(u, 8 - d, 0), v + pltpu.roll(v, d, 0))
+                for u, v in zip(values[:half_n], values[half_n:])
+            ]
+        return values[0]
+
+    def first_sums(g, c, n=8):
+        s, q = [], []
+        for k in range(n):
+            v = feat[pl.ds(pl.multiple_of((g * 8 + k) * rpc, rpc), rpc), :].astype(F32)
             w = v * mask_of
-            at = pl.ds(pl.multiple_of(row * 8, 8), 8)
-            sums_s[at, :] = halves(w)
-            sums_q[at, :] = halves(w * v)
+            s.append(halves(w))
+            q.append(halves(w * v))
+        none = [jnp.zeros((8, LANES), F32)] * (8 - n)
+        at = pl.ds(pl.multiple_of(g * 8, 8), 8)
+        sum_a[at, :] = fold(s + none)
+        sum_b[at, :] = fold(q + none)
         return c
 
-    for k in range(3):
+    whole, done = n_c // 8, 0
+    for k, groups in enumerate(feat_groups):
         feat_parts[k].wait()
-        lax.fori_loop(n_c // 15 * k, n_c // 15 * (k + 1), first_sums, 0)
-    sums_s[n_c * 8 : cp * 8, :] = jnp.zeros(((cp - n_c) * 8, LANES), F32)
-    sums_q[n_c * 8 : cp * 8, :] = jnp.zeros(((cp - n_c) * 8, LANES), F32)
-
-    def first_fold(g, c):
-        for src, dst in ((sums_s, sum_a), (sums_q, sum_b)):
-            v = src[pl.ds(g * 64, 8, stride=8), :]
-            for k in range(1, 8):
-                v = v + src[pl.ds(g * 64 + k, 8, stride=8), :]
-            dst[pl.ds(pl.multiple_of(g * 8, 8), 8), :] = v
-        return c
-
-    lax.fori_loop(0, cp // 8, first_fold, 0)
+        lax.fori_loop(done, min(done + groups, whole), first_sums, 0)
+        done += groups
+    if n_c % 8:
+        first_sums(whole, 0, n_c % 8)
+    spare = pl.ds(pad_to(n_c, 8), cp - pad_to(n_c, 8))
+    sum_a[spare, :] = jnp.zeros((cp - pad_to(n_c, 8), LANES), F32)
+    sum_b[spare, :] = jnp.zeros((cp - pad_to(n_c, 8), LANES), F32)
     lane1 = iota((1, LANES), 1)
     s0, sq0 = as_rows(sum_a[...], c_sizes), as_rows(sum_b[...], c_sizes)
     ar1[dp, 0:1, :] = s0[0]
@@ -209,14 +219,11 @@
     ar1[dp, 2:3, :] = sq0[0]
     ar1[dp, 3:4, :] = sq0[1]
 
-    pl.semaphore_wait(barrier, n_dev - 1)
-    share_start(ar1, dp, n_dp, dp_peer, s1, r1)
-
     new_slot = slot[slot.shape[0] - 1]
     per_device = n_c // grow
     slot_of = iota((rpc, LANES), 0) * 0 + new_slot
     loads[1].wait()
-    graw[grow * rpc : TAP * rpc, :] = jnp.zeros(((TAP - grow) * rpc, LANES), F32)
+    graw[grow * rpc : 40 * rpc, :] = jnp.zeros(((40 - grow) * rpc, LANES), F32)
     picks = [jnp.where(slot_of == ch * per_device + i, mask_of, 0.0) for i in range(per_device)]
 
     def pick(i, c):
@@ -228,29 +235,26 @@
 
     lax.fori_loop(0, grow, pick, 0)
 
-    def by_image(b):
+    pl.semaphore_wait(barrier, n_dev - 1)
+    share_start(ar1, dp, n_dp, dp_peer, s1, r1)
+
+    def by_image(q, first, second):
+        def rows_of(b, t, o):
+            return graw[pl.ds(o * rpc + t * n_img + b, 8, stride=rpc), :]
+
         for t in range(tiles):
-            for h in range(TAP // 16):
-                v = jnp.concatenate(
-                    [
-                        graw[pl.ds((h * 16 + i * 8) * rpc + t * n_img + b, 8, stride=rpc), :]
-                        for i in range(2)
-                    ],
-                    axis=0,
-                )
-                gsend[b, h * 16 : h * 16 + 16, t * LANES : (t + 1) * LANES] = v.astype(BF16)
-
-    by_image(sib)
-    by_image(xs)
-    g_sib = [
-        remote(gsend.at[sib], gsx.at[0], sg.at[0], rg.at[0], {"chan": sib}),
-        remote(gsend.at[xs], gsx.at[1], sg.at[1], rg.at[1], {"chan": sib}),
-    ]
-    for copy in g_sib:
-        copy.start()
-    by_image(ch)
-    by_image(xp)
-
+            sl = slice(t * LANES, (t + 1) * LANES)
+            for i, b in enumerate((first, second)):
+                for h in range(2):
+                    v = jnp.concatenate([rows_of(b, t, h * 16), rows_of(b, t, h * 16 + 8)], axis=0)
+                    gsend[q, i * 32 + h * 16 : i * 32 + h * 16 + 16, sl] = v.astype(BF16)
+            v = jnp.concatenate([rows_of(first, t, 32), rows_of(second, t, 32)], axis=0)
+            gsend[q, 64:80, sl] = v.astype(BF16)
+
+    by_image(0, sib, xs)
+    g_sib = remote(gsend.at[0], gsx, sg.at[0], rg.at[0], {"chan": sib})
+    g_sib.start()
+    by_image(1, ch, xp)
     lane16 = iota((16, n_px), 1)
     row_of, col_of = lane16 >> 5, lane16 & (SIDE - 1)
     for b in range(n_img):
@@ -266,30 +270,11 @@
 
     lax.fori_loop(0, n_rows // step_rows, widen, 0)
 
-    for copy in g_sib:
-        copy.wait()
-    gpair[0] = (gsend[ch].astype(F32) + gsx[0].astype(F32)).astype(BF16)
-    gpair[1] = (gsend[xp].astype(F32) + gsx[1].astype(F32)).astype(BF16)
-    g_x = [
-        remote(gpair.at[0], grx.at[1], sg.at[2], rg.at[3], {"chan": xp}),
-        remote(gpair.at[1], grx.at[0], sg.at[3], rg.at[2], {"chan": xp}),
-    ]
-    for copy in g_x:
-        copy.start()
-
-    def relayout(b):
-        def body(g, c):
-            r = pl.ds(pl.multiple_of(g * 16, 16), 16)
-            for t in range(tiles):
-                k = g * 16 * rpc + t * n_img + b
-                v = jnp.concatenate([out_x[pl.ds(k + h * 8 * rpc, 8, stride=rpc), :] for h in range(2)], axis=0)
-                xb[b, r, t * LANES : (t + 1) * LANES] = v.astype(BF16)
-            return c
-
-        lax.fori_loop(0, cp // 16, body, 0)
-
-    relayout(xs)
-    relayout(xp)
+    g_sib.wait()
+    gpair[...] = (gsend[1].astype(F32) + gsx[...].astype(F32)).astype(BF16)
+    g_x = remote(gpair, grx, sg.at[1], rg.at[1], {"chan": xp})
+    g_x.start()
+
     loads[7].wait()
     w2pad[...] = jnp.zeros(w2pad.shape, F32)
     w2wide[...] = jnp.zeros(w2wide.shape, F32)
@@ -357,7 +342,10 @@
             a, b = col_a[r, :], col_b[r, :]
             for t in range(first, first + n):
                 sl = slice(t * LANES, (t + 1) * LANES)
-                v = xb[j, r, sl].astype(F32) * a + b
+                k = g * 16 * rpc + t * n_img + j
+                v = jnp.concatenate([out_x[pl.ds(k + h * 8 * rpc, 8, stride=rpc), :] for h in range(2)], axis=0)
+                xb[j, r, sl] = v.astype(BF16)
+                v = v * a + b
                 act[j, r, sl] = ((v * jnp.tanh(v) + v) * mask[j, :, sl]).astype(BF16)
             return c
 
@@ -472,19 +460,20 @@
         r = pl.ds(i * LANES, c_sizes[i])
         col_m[r, :] = as_column(mean1[i], c_sizes[i])
         col_k[r, :] = as_column(keep1[i], c_sizes[i])
-    relayout(sib)
-    relayout(ch)
     partial(sib, 0, tiles)
     to_sib_b = remote(part.at[sib, rows_d], rx_b.at[rows_d], sx.at[0], rxs.at[0], {"chan": sib})
     to_sib_b.start()
     partial(ch, 0, tiles)
 
-    for copy in g_x:
-        copy.wait()
+    g_x.wait()
     px = iota((TAP, n_px), 1)
     py, pxx = px >> 5, px & (SIDE - 1)
+    gcur[40:TAP, :] = jnp.zeros((TAP - 40, n_px), F32)
     for i in range(2):
-        gcur[...] = gpair[i].astype(F32) + grx[i].astype(F32)
+        mine, theirs = slice(i * 32, i * 32 + 32), slice(32 - i * 32, 64 - i * 32)
+        gcur[0:32, :] = gpair[mine, :].astype(F32) + grx[theirs, :].astype(F32)
+        tails, others = gpair[64:80, :].astype(F32), grx[64:80, :].astype(F32)
+        gcur[32:40, :] = tails[i * 8 : i * 8 + 8] + others[8 - i * 8 : 16 - i * 8]
         for ky in range(3):
             for kx in range(3):
                 shift = (ky - 1) * SIDE + (kx - 1)
@@ -805,7 +794,6 @@
     weight_grad(ch)
     weight_grad(xp)
     w_x.wait()
-    input_grad(ch)
     for i, j in ((0, sib), (1, xs)):
         for k in range(2):
             grads[2 * i + k].wait()
@@ -856,7 +844,7 @@
         return c
 
     lax.fori_loop(0, OWNERS, push, 0)
-    for j in (xp, sib, xs):
+    for j in (ch, xp, sib, xs):
         input_grad(j)
     s4_, q4_ = as_rows(sum_a[...], c_sizes), as_rows(sum_b[...], c_sizes)
     for i in range(2):
@@ -1067,14 +1055,14 @@
         v((n_img, cp, n_px), F32), v((n_img, cp, n_px), F32), v((cp, n_px), F32),
         v((cp, LANES), F32), v((cp, LANES), F32), v((cp, LANES), F32), v((cp, LANES), F32),
         v((9, dpad, LANES), F32), v((cp, LANES), F32), v((cp, LANES), F32),
-        v((cp * 8, LANES), F32), v((cp * 8, LANES), F32), v((8, LANES), F32),
+        v((8, LANES), F32),
         v((dpad, cp), BF16), v((n_img, dpad, n_px), F32),
         v((dpad, n_px), F32), v((dpad, n_px), F32), v((2, dpad, n_px), F32),
         v((d8, LANES), F32), v((d8, LANES), F32), v((PIECES, d8, LANES), F32),
         v((n_px // LANES, words, LANES), jnp.int32), v((n_px // LANES, words, LANES), jnp.int32), v((PIECES, 2, LANES), F32), v((PIECES, 2, LANES), F32),
         v((n_px // LANES, words, LANES), jnp.int32), v((n_px // LANES, words, LANES), jnp.int32), v((PIECES, 2, LANES), F32), v((PIECES, 2, LANES), F32),
-        v((TAP * rpc, LANES), F32), v((n_ch, TAP, n_px), BF16),
-        v((2, TAP, n_px), BF16), v((2, TAP, n_px), BF16), v((2, TAP, n_px), BF16), v((TAP, n_px), F32),
+        v((40 * rpc, LANES), F32), v((2, 80, n_px), BF16),
+        v((80, n_px), BF16), v((80, n_px), BF16), v((80, n_px), BF16), v((TAP, n_px), F32),
         v((2, TAPS, n_px), BF16), v((9, TAP, LANES), F32), v((TAP, TAPS), F32), v((n_ch, TAP, TAPS), BF16), v((dpad, TAPS), BF16),
         v((n_ch, 2, LANES), F32),
         v((dpad, n_px), BF16), v((2, dpad, n_px), F32), v((2, dpad, n_px), F32), v((TAPS, n_px), F32),
@@ -1086,7 +1074,7 @@
         dma((13,)),
         dma((n_dp,)), dma((n_dp,)), dma((n_dev,)), dma((n_dev,)), dma((n_dev,)), dma((n_dev,)), dma((n_dp,)), dma((n_dp,)),
         dma((3,)), dma((3,)), dma((PIECES,)), dma((PIECES,)), dma((2, PIECES)), dma((2, PIECES)),
-        dma((4,)), dma((4,)), dma((n_ch,)), dma((n_ch,)), dma((n_ch,)), dma((n_ch,)),
+        dma((2,)), dma((2,)), dma((n_ch,)), dma((n_ch,)), dma((n_ch,)), dma((n_ch,)),
         dma((2, PIECES)), dma((2, PIECES)), dma((2, 2)), dma((2, 2)), dma((3,)), dma((3,)), dma((3,)), dma((3,)),
         dma((OWNERS,)), dma((n_dp,)), dma((n_dp,)), dma((OWNERS,)),
     ]

time: 52 us -> 50.4 us (0.969)
  Pallas kernels: 51.2 us -> 49.6 us
    pallas_call x1, Pallas kernels: 48.5 us -> 47 us  [on_device(): pl.pallas_call(functools.partial(layer, cfg), out_shape=out_shape, in_spe...]
where the time goes in v7:
time: 50.4 us; the launch traced here: 50.2 us
  Pallas kernels  49.6 us (98%)
  between operations  0.64 us (1%)
    pallas_call x1, Pallas kernels, on_device(): pl.pallas_call(functools.partial(layer, cfg), out_shape=out_shape, in_spe...  47 us
    pallas_call x1, Pallas kernels, on_device(): pl.pallas_call(functools.partial(finish, n_rows, grow * rpc), out_shape=f...  2.62 us

profile of v7, /device:TPU:0, one launch (start us, length us, event | category | flops | bytes accessed | tf_op | source)
XLA Modules:
  0.0 50.2 jit_solution(853087401099546973)
XLA Ops:
  0.6 47.0 %shard_map.161 = (f32[5632,128]{1,0:T(8,128)S(1)}, f32[5632,128]{1,0:T(8,128)S(1)}, f32[132,165]{1,0:T(8,128)S(1)}, f32[1,165]{1,0:T(1,128)S(1)}, f32[1,165]{1,0...) custom-call(bf16[5280,128]{1,0:T(8,128)(2,1)} %bitcast.40, ...), custom_call_target="tpu_custom_call" | custom-call | tf_op jit(solution)/shard_map/pallas_call | solution.py:1086
  47.6 2.6 %shard_map.162 = (f32[5280,128]{1,0:T(8,128)}, f32[5280,128]{1,0:T(8,128)}, f32[132,165]{1,0:T(8,128)}, f32[1,165]{1,0:T(1,128)}, f32[1,165]{1,0:T(1,128)}, /*in...) custom-call(f32[5632,128]{1,0:T(8,128)S(1)} %get-tuple-element.26.refs_0_, ...), custom_call_target="tpu_custom_call" | custom-call | tf_op jit(solution)/shard_map/pallas_call | solution.py:1097

commit v8 on v7

--- a/solution.py
+++ b/solution.py
@@ -138,6 +138,8 @@
             src_ref=src, dst_ref=dst, send_sem=send, recv_sem=recv, device_id=device, device_id_type=MESH
         )
 
+    still_sent = []
+
     def share_start(slots, mine, count, peer, send, recv):
         def step(k):
             remote(slots.at[mine], slots.at[mine], send.at[k], recv.at[k], peer(k)).start()
@@ -146,9 +148,13 @@
 
     def share_wait(slots, mine, count, peer, send, recv):
         def step(k):
-            remote(slots.at[mine], slots.at[mine], send.at[k], recv.at[k], peer(k)).wait()
+            remote(slots.at[mine], slots.at[mine], send.at[k], recv.at[k], peer(k)).wait_recv()
+
+        def sent(k):
+            remote(slots.at[mine], slots.at[mine], send.at[k], recv.at[k], peer(k)).wait_send()
 
         far_first(count, step)
+        still_sent.append(lambda: far_first(count, sent))
 
     def total(slots):
         if slots.shape[0] <= 32:
@@ -368,8 +374,6 @@
 
     def code(read, p, words, tops):
         top = jnp.maximum(jnp.max(row_top[...], axis=1, keepdims=True), 1e-30)
-        tops[p, 0:1, :] = as_row(top[0:LANES])
-        tops[p, 1:2, :] = as_row(top[LANES:d8])
         row_scale[...] = jnp.broadcast_to(LEVELS / top, (d8, LANES))
 
         def quantized(first, n, sl):
@@ -390,6 +394,8 @@
         lax.fori_loop(0, blocks, block, 0)
         for t, sl in enumerate(tiles_of(p), edges[p]):
             words[t, plain : plain + d8 - rest, :] = quantized(rest, d8 - rest, sl)
+        tops[p, 0:1, :] = as_row(top[0:LANES])
+        tops[p, 1:2, :] = as_row(top[LANES:d8])
 
     def unscale(tops, p):
         top = jnp.concatenate([as_column(tops[p, 0:1, :], LANES), as_column(tops[p, 1:2, :], d8 - LANES)], axis=0)
@@ -508,8 +514,6 @@
 
         lax.fori_loop(0, cp // 16, body, 0)
 
-    slopes(xs)
-    slopes(xp)
 
     to_sib_b.wait()
     sum_a[...] = jnp.zeros(sum_a.shape, F32)
@@ -578,8 +582,8 @@
 
     w_far.wait()
     w_on.start()
-    slopes(sib)
-    slopes(ch)
+    slopes(xs)
+    slopes(xp)
     w_near.wait()
     w_on.wait()
     share_wait(gsl, ch, n_ch, ch_peer, sb, rb)
@@ -723,9 +727,14 @@
     new_on = remote(gall.at[xp], gall.at[xp], so.at[2], ro.at[2], {"chan": sib})
     new_xp.start()
     new_sib.start()
+    slopes(sib)
+    slopes(ch)
     for p in range(PIECES):
         second_other(p)
 
+    w1acc[...] = jnp.zeros(w1acc.shape, F32)
+    sum_a[...] = jnp.zeros(sum_a.shape, F32)
+    sum_b[...] = jnp.zeros(sum_b.shape, F32)
     share_wait(ar3, me, n_dev, dev_peer, s3, r3)
     tot3 = total(ar3)
     gain_sum2 = [tot3[2 + i : 3 + i] * rstd2[i] for i in range(2)]
@@ -755,14 +764,7 @@
             copy = remote(gha.at[j, :, at], gha.at[j, :, at], st.at[i, k], rt.at[i, k], {"chan": sib})
             copy.start()
             grads.append(copy)
-    d_rows, d_cols = iota((dpad, LANES), 0), iota((dpad, LANES), 1)
-    here_d = (d_rows == d_cols + ch * grow) & (d_cols < grow)
-    out_g2[...] = jnp.sum(jnp.where(here_d, gain_sum2c, 0.0), axis=0, keepdims=True)[:, 0:grow]
-    out_b2[...] = jnp.sum(jnp.where(here_d, bias_sum2c, 0.0), axis=0, keepdims=True)[:, 0:grow]
-
-    w1acc[...] = jnp.zeros(w1acc.shape, F32)
-    sum_a[...] = jnp.zeros(sum_a.shape, F32)
-    sum_b[...] = jnp.zeros(sum_b.shape, F32)
+
 
     def weight_grad(j, k=None):
         at = slice(0, n_px) if k is None else slice(k * (n_px // 2), (k + 1) * (n_px // 2))
@@ -844,6 +846,10 @@
         return c
 
     lax.fori_loop(0, OWNERS, push, 0)
+    d_rows, d_cols = iota((dpad, LANES), 0), iota((dpad, LANES), 1)
+    here_d = (d_rows == d_cols + ch * grow) & (d_cols < grow)
+    out_g2[...] = jnp.sum(jnp.where(here_d, gain_sum2c, 0.0), axis=0, keepdims=True)[:, 0:grow]
+    out_b2[...] = jnp.sum(jnp.where(here_d, bias_sum2c, 0.0), axis=0, keepdims=True)[:, 0:grow]
     for j in (ch, xp, sib, xs):
         input_grad(j)
     s4_, q4_ = as_rows(sum_a[...], c_sizes), as_rows(sum_b[...], c_sizes)
@@ -851,8 +857,6 @@
         ar4[dp, i : i + 1, :] = s4_[i]
         ar4[dp, 2 + i : 3 + i, :] = q4_[i]
     share_start(ar4, dp, n_dp, dp_peer, s4, r4)
-    new_xp.wait()
-    new_on.start()
 
     def scatter(g, c):
         first = g * 16 * rpc
@@ -895,6 +899,8 @@
         far_first(n_dp, give)
 
     lax.fori_loop(0, OWNERS, push_wait, 0)
+    new_xp.wait()
+    new_on.start()
     lax.fori_loop(5, cp // 16, scatter, 0)
 
     for i in range(2):
@@ -937,6 +943,9 @@
         return c
 
     lax.fori_loop(0, n_c // 5, last, 0)
+
+    for wait in still_sent:
+        wait()
 
     @pl.when(is_owner)
     def _():

time: 50.4 us -> 50.3 us (level)
  no operation moved by 1% of the time
where the time goes in v8:
time: 50.3 us; the launch traced here: 50.2 us
  Pallas kernels  49.5 us (98%)
  between operations  0.64 us (1%)
    pallas_call x1, Pallas kernels, on_device(): pl.pallas_call(functools.partial(layer, cfg), out_shape=out_shape, in_spe...  46.9 us
    pallas_call x1, Pallas kernels, on_device(): pl.pallas_call(functools.partial(finish, n_rows, grow * rpc), out_shape=f...  2.62 us

profile of v8, /device:TPU:0, one launch (start us, length us, event | category | flops | bytes accessed | tf_op | source)
XLA Modules:
  0.0 50.2 jit_solution(17974984505752287385)
XLA Ops:
  0.6 46.9 %shard_map.161 = (f32[5632,128]{1,0:T(8,128)S(1)}, f32[5632,128]{1,0:T(8,128)S(1)}, f32[132,165]{1,0:T(8,128)S(1)}, f32[1,165]{1,0:T(1,128)S(1)}, f32[1,165]{1,0...) custom-call(bf16[5280,128]{1,0:T(8,128)(2,1)} %bitcast.40, ...), custom_call_target="tpu_custom_call" | custom-call | tf_op jit(solution)/shard_map/pallas_call | solution.py:1095
  47.5 2.6 %shard_map.162 = (f32[5280,128]{1,0:T(8,128)}, f32[5280,128]{1,0:T(8,128)}, f32[132,165]{1,0:T(8,128)}, f32[1,165]{1,0:T(1,128)}, f32[1,165]{1,0:T(1,128)}, /*in...) custom-call(f32[5632,128]{1,0:T(8,128)S(1)} %get-tuple-element.26.refs_0_, ...), custom_call_target="tpu_custom_call" | custom-call | tf_op jit(solution)/shard_map/pallas_call | solution.py:1106

commit v9 on v8

--- a/solution.py
+++ b/solution.py
@@ -826,8 +826,23 @@
         q = jnp.concatenate([high, low[0:16]], axis=0).astype(F32)
         return q * jnp.concatenate([scale] * 5, axis=0)
 
+    def encode_part(v):
+        top = jnp.maximum(jnp.max(jnp.abs(v), axis=0, keepdims=True), 1e-30)
+        power = jnp.floor(jnp.log2(top) + 1.0001)
+        q = jnp.clip(jnp.round(v * jnp.exp2(23.0 - power)), -8388607.0, 8388607.0).astype(jnp.int32)
+        extra = q[32:40]
+        power = jnp.broadcast_to(jnp.clip(power, -127.0, 127.0).astype(jnp.int32), (8, LANES))
+        spare = jnp.concatenate([extra, extra >> 8, extra >> 16, power], axis=0) & 0xFF
+        return (q[0:32] << 8) | spare
+
+    def decode_part(w):
+        spare = w & 0xFF
+        extra = spare[0:8] | (spare[8:16] << 8) | (((w[16:24] << 24) >> 24) << 16)
+        scale = jnp.exp2(((w[24:32] << 24) >> 24).astype(F32) - 23.0)
+        return jnp.concatenate([w >> 8, extra], axis=0).astype(F32) * jnp.concatenate([scale] * 5, axis=0)
+
     for q in range(OWNERS):
-        coded[q] = encode(cb[q])
+        coded[q] = encode_part(cb[q])
     stride = n_dp // OWNERS
     my_part = dp // stride
     is_owner = lax.rem(dp, stride) == 0
@@ -890,7 +905,7 @@
         lax.fori_loop(1, n_dp, pull, 0)
         v = cb[my_part]
         for k in range(1, n_dp):
-            v = v + decode(rsl[lax.rem(dp + k, n_dp)])
+            v = v + decode_part(rsl[lax.rem(dp + k, n_dp)])
         fin[my_part] = encode(v)
 
         def give(k):
@@ -1077,8 +1092,8 @@
         v((dpad, n_px), BF16), v((2, dpad, n_px), F32), v((2, dpad, n_px), F32), v((TAPS, n_px), F32),
         v((n_ch, 40, n_px), F32), v((n_ch, dpad, n_px), BF16),
         v((n_ch, 136, LANES), F32), v((2, 136, LANES), F32), v((136, LANES), F32),
-        v((OWNERS, 40, LANES), F32), v((OWNERS, 24, LANES), jnp.int32),
-        v((n_dp, 24, LANES), jnp.int32), v((OWNERS, 24, LANES), jnp.int32), v((dpad, 256), F32), v((dpad, TAPS), F32),
+        v((OWNERS, 40, LANES), F32), v((OWNERS, 32, LANES), jnp.int32),
+        v((n_dp, 32, LANES), jnp.int32), v((OWNERS, 24, LANES), jnp.int32), v((dpad, 256), F32), v((dpad, TAPS), F32),
         v((n_dp, 4, LANES), F32), v((n_dev, 4, LANES), F32), v((n_dev, 4, LANES), F32), v((n_dp, 4, LANES), F32),
         dma((13,)),
         dma((n_dp,)), dma((n_dp,)), dma((n_dev,)), dma((n_dev,)), dma((n_dev,)), dma((n_dev,)), dma((n_dp,)), dma((n_dp,)),

time: 50.3 us -> 51.2 us (1.018)
  Pallas kernels: 49.5 us -> 50.4 us
    pallas_call x1, Pallas kernels: 46.9 us -> 47.8 us  [on_device(): pl.pallas_call(functools.partial(layer, cfg), out_shape=out_shape, in_spe...]
where the time goes in v9:
time: 51.2 us; the launch traced here: 51.1 us
  Pallas kernels  50.4 us (98%)
  between operations  0.64 us (1%)
    pallas_call x1, Pallas kernels, on_device(): pl.pallas_call(functools.partial(layer, cfg), out_shape=out_shape, in_spe...  47.8 us
    pallas_call x1, Pallas kernels, on_device(): pl.pallas_call(functools.partial(finish, n_rows, grow * rpc), out_shape=f...  2.62 us

profile of v9, /device:TPU:0, one launch (start us, length us, event | category | flops | bytes accessed | tf_op | source)
XLA Modules:
  0.0 51.1 jit_solution(14385504046701267898)
XLA Ops:
  0.6 47.8 %shard_map.161 = (f32[5632,128]{1,0:T(8,128)S(1)}, f32[5632,128]{1,0:T(8,128)S(1)}, f32[132,165]{1,0:T(8,128)S(1)}, f32[1,165]{1,0:T(1,128)S(1)}, f32[1,165]{1,0...) custom-call(bf16[5280,128]{1,0:T(8,128)(2,1)} %bitcast.40, ...), custom_call_target="tpu_custom_call" | custom-call | tf_op jit(solution)/shard_map/pallas_call | solution.py:1110
  48.4 2.6 %shard_map.162 = (f32[5280,128]{1,0:T(8,128)}, f32[5280,128]{1,0:T(8,128)}, f32[132,165]{1,0:T(8,128)}, f32[1,165]{1,0:T(1,128)}, f32[1,165]{1,0:T(1,128)}, /*in...) custom-call(f32[5632,128]{1,0:T(8,128)S(1)} %get-tuple-element.26.refs_0_, ...), custom_call_target="tpu_custom_call" | custom-call | tf_op jit(solution)/shard_map/pallas_call | solution.py:1121

commit v10 on v9

--- a/solution.py
+++ b/solution.py
@@ -1000,10 +1000,15 @@
         else:
             for lt in range(4):
                 w2acc[32:33, lt * LANES : (lt + 1) * LANES] = v[lt : lt + 1]
-    v = w2acc[0:40, :]
+    lane40 = iota((40, LANES), 1)
     for t in range(9):
-        u = v if t == 0 else pltpu.roll(v, TAPS - t * TAP, 1)
-        out_w2[t] = u[0:grow, 0:grow]
+        tile, off = t * TAP // LANES, t * TAP % LANES
+        v = w2acc[0:40, tile * LANES : (tile + 1) * LANES]
+        if off + grow > LANES:
+            v = jnp.where(lane40 >= off, v, w2acc[0:40, (tile + 1) * LANES : (tile + 2) * LANES])
+        if off:
+            v = pltpu.roll(v, LANES - off, 1)
+        out_w2[t] = v[0:grow, 0:grow]
 
 
 def finish(n_rows, grow_rows, *refs):

time: 51.2 us -> 51.2 us (level)
  no operation moved by 1% of the time
where the time goes in v10:
time: 51.2 us; the launch traced here: 51 us
  Pallas kernels  50.4 us (98%)
  between operations  0.64 us (1%)
    pallas_call x1, Pallas kernels, on_device(): pl.pallas_call(functools.partial(layer, cfg), out_shape=out_shape, in_spe...  47.8 us
    pallas_call x1, Pallas kernels, on_device(): pl.pallas_call(functools.partial(finish, n_rows, grow * rpc), out_shape=f...  2.62 us

profile of v10, /device:TPU:0, one launch (start us, length us, event | category | flops | bytes accessed | tf_op | source)
XLA Modules:
  0.0 51.0 jit_solution(15277300555413964880)
XLA Ops:
  0.6 47.8 %shard_map.161 = (f32[5632,128]{1,0:T(8,128)S(1)}, f32[5632,128]{1,0:T(8,128)S(1)}, f32[132,165]{1,0:T(8,128)S(1)}, f32[1,165]{1,0:T(1,128)S(1)}, f32[1,165]{1,0...) custom-call(bf16[5280,128]{1,0:T(8,128)(2,1)} %bitcast.40, ...), custom_call_target="tpu_custom_call" | custom-call | tf_op jit(solution)/shard_map/pallas_call | solution.py:1115
  48.4 2.6 %shard_map.162 = (f32[5280,128]{1,0:T(8,128)}, f32[5280,128]{1,0:T(8,128)}, f32[132,165]{1,0:T(8,128)}, f32[1,165]{1,0:T(1,128)}, f32[1,165]{1,0:T(1,128)}, /*in...) custom-call(f32[5632,128]{1,0:T(8,128)S(1)} %get-tuple-element.26.refs_0_, ...), custom_call_target="tpu_custom_call" | custom-call | tf_op jit(solution)/shard_map/pallas_call | solution.py:1126
